TPU v7x, 32 devices: a whole 2x2x4 slice. The times are simulated.
32 devices in a mesh: pair: 2 (over y), grp: 4 (over z), seq: 4 (over x, core).
Axes of the slice: x: 2, y: 2, z: 4, core: 2. Of those that a mesh axis runs over, the one named last changes fastest.
Arguments:
- series: float32 [4, 8192, 64], P('grp', 'seq', 'pair'), may hold values from -8 to 8
- time_blocks: int32 [4, 4], P('grp'), may hold values from 0 to 31
- freq_blocks: int32 [4, 4], P('grp'), may hold values from 0 to 31
- positives: int32 [4], replicated, may hold values from 0 to 3, each once
- conv_weight: bfloat16 [2, 1024, 512], P('pair'), may hold values from -0.25 to 0.25
- proj_weight: bfloat16 [2, 1024, 128], P('pair'), may hold values from -0.1875 to 0.1875
Outputs:
- encoded: bfloat16 [2, 4, 4096, 1024], P('pair', 'grp', 'seq')
- loss_value: float32 [], replicated
- grad_conv: float32 [2, 1024, 512], P('pair', ('grp', 'seq'))
- grad_proj: float32 [2, 1024, 128], P('pair', 'grp')
Inputs may be any that keep to these rules, and one draw needn't show every extreme that they name: `positives`: each of 0 to 3 stands once.
All inputs are finite; a program needn't handle non-finite values.
Results may differ from a plain program's by a relative error of at most 0.0042.
Values may be sent and summed in bfloat16 or wider, within the bound.
No kernel may reach another device: no remote copies, remote signals or barrier semaphores. Data moves between devices by JAX's collectives and lax.ppermute only.
A program may use at most 128 MiB of HBM per device.

v0:
```python
import functools
import math

import jax
import jax.numpy as jnp
import ml_dtypes
import numpy as np
from jax import lax
from jax.experimental import pallas as pl
from jax.experimental.pallas import tpu as pltpu
from jax.sharding import PartitionSpec as P

TAU = 0.2
LOSS_SCALE = 256.0
LANES = 128
ROOT = math.sqrt(2.0 / math.pi)
CUBIC = 0.044715
F32 = jnp.float32
BF16 = jnp.bfloat16

VMEM = pl.BlockSpec(memory_space=pltpu.VMEM)
SMEM = pl.BlockSpec(memory_space=pltpu.SMEM)


def call(kernel, out_shape, in_specs, scratch=(), flops=0, moved=0, **kwargs):
    single = not isinstance(out_shape, (list, tuple))
    return pl.pallas_call(
        kernel,
        out_shape=out_shape,
        in_specs=in_specs,
        out_specs=VMEM if single else [VMEM] * len(out_shape),
        scratch_shapes=list(scratch),
        compiler_params=pltpu.CompilerParams(vmem_limit_bytes=56 * 1024 * 1024),
        cost_estimate=pl.CostEstimate(flops=flops, bytes_accessed=moved, transcendentals=0),
        **kwargs,
    )


def split_high_low(table):
    high = table.astype(ml_dtypes.bfloat16)
    low = (table - high.astype(np.float64)).astype(ml_dtypes.bfloat16)
    return high, low


def fourier_tables(full_len):
    first_count = 2 * LANES
    rest = full_len // first_count
    top = np.arange(first_count)
    first = (2 * np.arange(LANES)[None, :] + np.arange(2)[:, None]).reshape(-1)
    low = np.arange(rest)
    angle = (top[:, None] * first[None, :] % first_count) * (2.0 * np.pi / first_count)
    high, small = split_high_low(np.concatenate([np.cos(angle), -np.sin(angle)], axis=1))
    stage_one = np.concatenate([high, small, high], axis=0)
    turn = (low[:, None] * first[None, :] % full_len) * (2.0 * np.pi / full_len)
    angle = (low[:, None] * low[None, :] % rest) * (2.0 * np.pi / rest)
    cos, sin = np.cos(angle), np.sin(angle)
    high, small = split_high_low(np.block([[cos, sin], [-sin, cos]]))
    stage_two = np.concatenate([high, small, high], axis=1)
    return stage_one, np.cos(turn).astype(np.float32), np.sin(turn).astype(np.float32), stage_two


def arrange_kernel(groups, rest, scalars, series, *outs):
    *pieces, held = outs
    me = scalars[0]
    length, chans = series.shape
    tops = length // rest
    stacked = LANES // tops
    lows = rest // stacked
    for low in range(lows):
        rows = [series[pl.ds(part * lows + low, tops, stride=rest), :] for part in range(stacked)]
        held[pl.ds(low, chans, stride=lows), :] = jnp.concatenate(rows, axis=0).T
    size = chans // groups * lows
    for turn in range(groups):
        start = pl.multiple_of((me ^ turn) * size, 8)
        pieces[turn][...] = held[pl.ds(start, size), :]


def time_kernel(series, out):
    length, chans = series.shape
    for block in range(length // (2 * LANES)):
        for parity in range(2):
            rows = series[pl.ds(2 * LANES * block + parity, LANES, stride=2), :]
            out[chans * parity : chans * (parity + 1), LANES * block : LANES * (block + 1)] = rows.T.astype(BF16)


def high_low(values):
    high = values.astype(BF16)
    return high, (values - high.astype(F32)).astype(BF16)


def fourier_kernel(groups, full_len, scalars, time_view, stage_one, turn_cos, turn_sin, stage_two, *refs):
    pieces = refs[:groups]
    own, pay, gathered, mags, wire = refs[groups:]
    me, branch = scalars[0], scalars[1]
    rest = full_len // (2 * LANES)
    tops = 2 * LANES // groups
    stacked = LANES // tops
    lows = rest // stacked
    rows = pieces[0].shape[0]
    chans = rows // lows
    for turn in range(groups):
        gathered[turn] = pieces[turn][...]
    blocks = [gathered[source ^ me] for source in range(groups)]
    parts = [
        jnp.concatenate([block[:, part * tops : (part + 1) * tops] for block in blocks], axis=1)
        for part in range(stacked)
    ]
    steps = jnp.concatenate(parts, axis=0)
    high, low = high_low(steps)
    first = jnp.dot(jnp.concatenate([high, high, low], axis=1), stage_one[...], preferred_element_type=F32)
    first = first.reshape(stacked, chans, lows, 4 * LANES)
    cos = turn_cos[...].reshape(stacked, 1, lows, 2 * LANES)
    sin = turn_sin[...].reshape(stacked, 1, lows, 2 * LANES)
    part_re, part_im = first[..., : 2 * LANES], first[..., 2 * LANES :]
    turned_re = part_re * cos + part_im * sin
    turned_im = part_im * cos - part_re * sin
    columns = [
        jnp.concatenate(
            [turned_re[part, chan] for part in range(stacked)]
            + [turned_im[part, chan] for part in range(stacked)],
            axis=0,
        )
        for chan in range(chans)
    ]
    high, low = high_low(jnp.concatenate(columns, axis=1))
    second = jnp.dot(stage_two[...], jnp.concatenate([high, high, low], axis=0), preferred_element_type=F32)
    spec_re, spec_im = second[:rest], second[rest:]
    magnitude = jnp.sqrt(1.0 + (spec_re * spec_re + spec_im * spec_im) * (1.0 / full_len))
    for chan in range(chans):
        for parity in range(2):
            at = (parity * chans + chan) * rest
            mags[at : at + rest, :] = magnitude[:, (2 * chan + parity) * LANES : (2 * chan + parity + 1) * LANES]
    per_chunk = rest // groups
    for block in range(rest):
        chunk, inner = block // per_chunk, block % per_chunk
        wire[2 * chans * chunk : 2 * chans * (chunk + 1), LANES * inner : LANES * (inner + 1)] = mags[
            pl.ds(block, 2 * chans, stride=rest), :
        ]

    @pl.when(branch == 0)
    def _():
        own[...] = time_view[...]
        pay[...] = wire[...].astype(BF16)

    @pl.when(branch != 0)
    def _():
        own[...] = wire[...].astype(BF16)
        pay[...] = time_view[...]


def gelu_parts(values):
    square = values * values
    curve = jnp.tanh(values * (ROOT + (ROOT * CUBIC) * square))
    half = 0.5 * values
    return square, curve, half


def stack_rows(window, count):
    return jnp.concatenate([window[6 + shift : 6 + shift + count] for shift in range(4)], axis=1).astype(BF16)


def odd_rows(even, following):
    lane = lax.broadcasted_iota(jnp.int32, even.shape, 1)
    return jnp.where(lane < LANES // 2, pltpu.roll(even, LANES // 2, 1), pltpu.roll(following, LANES // 2, 1))


def slope_kernel(groups, tile, scalars, time_blocks, freq_blocks, weight, projection, *refs):
    count = 2 * groups
    slots = refs[:count]
    grads = refs[count:-7]
    payload, near, flat, tall, odd, total, pool = refs[-7:]
    me, branch = scalars[0], scalars[1]
    grp_pos = scalars[2]
    half_rows, chunk = slots[0].shape
    own_chan = half_rows // 2
    chans = own_chan // groups
    aligned = chans % 8 == 0
    halves = chunk * groups
    flat[:, :LANES] = jnp.zeros((LANES, LANES), F32)
    flat[:, LANES + halves :] = jnp.zeros((LANES, LANES), F32)
    tall[:8, :] = jnp.zeros((8, LANES), F32)
    tall[8 + halves :, :] = jnp.zeros((16, LANES), F32)
    for flip in range(2):
        for turn in range(groups):
            slot = slots[flip * groups + turn]
            side = branch ^ flip
            source = me ^ turn

            by_steps = branch == 0 if aligned else branch >= 0

            @pl.when(by_steps)
            def _(slot=slot, side=side, source=source):
                for parity in range(2):
                    row = pl.multiple_of(parity * 2 * own_chan + side * own_chan, 8)
                    lane = pl.multiple_of(LANES + source * chunk, LANES)
                    flat[pl.ds(row, own_chan), pl.ds(lane, chunk)] = slot[
                        parity * own_chan : (parity + 1) * own_chan, :
                    ].astype(F32)

            if not aligned:
                continue

            @pl.when(branch != 0)
            def _(slot=slot, side=side, source=source):
                for part in range(groups):
                    values = slot[2 * chans * part : 2 * chans * (part + 1), :].astype(F32)
                    for parity in range(2):
                        row = pl.multiple_of(parity * 2 * own_chan + side * own_chan + source * chans, chans)
                        flat[pl.ds(row, chans), LANES + part * chunk : LANES + (part + 1) * chunk] = values[
                            parity * chans : (parity + 1) * chans
                        ]

    def mask(block, _):
        keep = jnp.float32(1.0)
        for entry in range(time_blocks.shape[1]):
            listed = jnp.where(branch == 0, time_blocks[0, entry], freq_blocks[0, entry])
            keep = jnp.where(listed == block, 0.0, keep)
        at = pl.multiple_of(LANES + block * LANES, LANES)
        values = flat[:, pl.ds(at, LANES)] * keep
        flat[:, pl.ds(at, LANES)] = values
        tall[pl.ds(pl.multiple_of(8 + block * LANES, 8), LANES), :] = values.T
        return 0

    lax.fori_loop(0, halves // LANES, mask, 0)
    begin = pl.multiple_of(me * chunk, LANES)
    near[...] = tall[pl.ds(begin, chunk + 24), :]

    def shift(block, _):
        at = pl.multiple_of(block * tile, tile)
        window = tall[pl.ds(at, tile + 8), :]
        odd[pl.ds(at, tile), :] = odd_rows(window[:tile], window[1 : tile + 1])
        return 0

    lax.fori_loop(0, halves // tile, shift, 0)
    tail = tall[halves : halves + 24, :]
    odd[halves:, :] = odd_rows(tail[:16], tail[1:17])
    total[...] = jnp.zeros_like(total)
    pool[...] = jnp.zeros_like(pool)

    def step(index, _):
        at = pl.multiple_of(index * tile, tile)
        window = flat[:, pl.ds(at, tile + 2 * LANES)]
        shifted = jnp.concatenate(
            [window[:, LANES + move : LANES + move + tile] for move in range(-2, 3)], axis=0
        ).astype(BF16)
        sums = pool[...]
        for parity in range(2):
            columns = shifted[LANES // 2 * parity : LANES // 2 * parity + 4 * LANES]
            preact = jnp.dot(weight[...], columns, preferred_element_type=F32)
            square, curve, half = gelu_parts(preact)
            active = half + half * curve
            for part in range(tile // LANES):
                sums = sums + active[:, part * LANES : (part + 1) * LANES]
            slope = (0.5 + 0.5 * curve) + (half * (1.0 - curve * curve)) * (ROOT + (3.0 * ROOT * CUBIC) * square)
            source = tall if parity == 0 else odd
            rows = stack_rows(source[pl.ds(at, tile + 16), :], tile)
            total[...] += jnp.dot(slope.astype(BF16), rows, preferred_element_type=F32)
        pool[...] = sums
        return 0

    lax.fori_loop(0, halves // tile, step, 0)
    share = len(grads)
    rows = weight.shape[0] // share
    column = jnp.sum(pool[...], axis=1, keepdims=True)
    latent = jnp.sum(column * projection[...].astype(F32), axis=0, keepdims=True)
    line = jnp.broadcast_to(column, (column.shape[0], LANES)).T[0:1, :]
    payload[...] = jnp.zeros_like(payload)
    total_devices = payload.shape[0]
    for device in range(total_devices):
        target = device // groups % share
        payload[device, 0:1, :] = latent
        payload[device, 1:2, 0:rows] = line[:, target * rows : (target + 1) * rows]
    for turn in range(share):
        start = pl.multiple_of((grp_pos ^ turn) * rows, 8)
        grads[turn][...] = total[pl.ds(start, rows), :]


def encode_kernel(near, weight, out):
    tile = out.shape[0]
    at = pl.multiple_of(pl.program_id(0) * tile, tile)
    window = near[pl.ds(at, tile + 24), :]
    even = window[: tile + 16]
    shifted = odd_rows(even, window[1 : tile + 17])
    sums = None
    for rows in (even, shifted):
        preact = lax.dot_general(
            stack_rows(rows, tile), weight[...], (((1,), (1,)), ((), ())), preferred_element_type=F32
        )
        _, curve, half = gelu_parts(preact)
        active = half + half * curve
        sums = active if sums is None else sums + active
    out[...] = (sums * 0.5).astype(BF16)


def loss_kernel(groups, share, full_len, scalars, positives, arrived, projection, loss, factors, grad):
    branch, grp_pos = scalars[1], scalars[2]
    batch = positives.shape[0]
    exact = lax.Precision.HIGHEST
    latents = []
    for side in range(2):
        lines = []
        for item in range(batch):
            base = (side * share + item) * groups
            line = arrived[base, 0:1, :]
            for turn in range(1, groups):
                line = line + arrived[base + turn, 0:1, :]
            lines.append(line * (1.0 / full_len))
        latents.append(jnp.concatenate(lines, axis=0))
    scale = [lax.rsqrt(jnp.sum(latent * latent, axis=1, keepdims=True) + 1e-06) for latent in latents]
    embs = [latent * factor for latent, factor in zip(latents, scale)]
    logits = lax.dot_general(embs[0], embs[1], (((1,), (1,)), ((), ())), precision=exact, preferred_element_type=F32) / TAU
    row = lax.broadcasted_iota(jnp.int32, logits.shape, 0)
    col = lax.broadcasted_iota(jnp.int32, logits.shape, 1)
    target = jnp.zeros_like(logits)
    for item in range(batch):
        target = jnp.where((row == item) & (col == positives[item]), 1.0, target)
    power = jnp.exp(logits)
    row_sum = jnp.sum(power, axis=1, keepdims=True)
    col_sum = jnp.sum(power, axis=0, keepdims=True)
    value = (
        jnp.sum(jnp.log(row_sum), axis=(0, 1), keepdims=True)
        + jnp.sum(jnp.log(col_sum), axis=(0, 1), keepdims=True)
        - 2.0 * jnp.sum(target * logits, axis=(0, 1), keepdims=True)
    ) / (2.0 * batch)
    loss[...] = jnp.broadcast_to(value, loss.shape)
    slope = (power / row_sum + power / col_sum - 2.0 * target) * (LOSS_SCALE / (2.0 * batch * TAU))
    emb_grads = [
        lax.dot_general(slope, embs[1], (((1,), (0,)), ((), ())), precision=exact, preferred_element_type=F32),
        lax.dot_general(slope.T, embs[0], (((1,), (0,)), ((), ())), precision=exact, preferred_element_type=F32),
    ]
    own = []
    for side in range(2):
        inner = jnp.sum(emb_grads[side] * embs[side], axis=1, keepdims=True)
        own.append(scale[side] * (emb_grads[side] - embs[side] * inner))
    latent_grad = jnp.where(branch == 0, own[0], own[1])
    rows = projection.shape[0]
    weights = projection[...].astype(F32)
    lane = lax.broadcasted_iota(jnp.int32, (rows, LANES), 1)
    spread = jnp.zeros((rows, LANES), F32)
    for item in range(batch):
        column = jnp.sum(weights * latent_grad[item : item + 1, :], axis=1, keepdims=True) * (1.0 / full_len)
        spread = jnp.where(lane == item, column, spread)
    factors[...] = spread
    for turn in range(groups):
        lines = [arrived[(branch * share + item) * groups + turn, 1:2, :] for item in range(batch)]
        lines = lines + [jnp.zeros((8 - batch % 8, LANES), F32)] if batch % 8 else lines
        sums = jnp.concatenate(lines, axis=0).T * (1.0 / full_len)
        value = sums[:, 0:1] * latent_grad[0:1, :]
        for item in range(1, batch):
            value = value + sums[:, item : item + 1] * latent_grad[item : item + 1, :]
        grad[turn * rows : (turn + 1) * rows, :] = value[:rows]


def combine_kernel(share, scalars, factors, *refs):
    pieces, out = refs[:share], refs[share]
    grp_pos = scalars[2]
    values = factors[...]
    lane = lax.broadcasted_iota(jnp.int32, values.shape, 1)
    result = None
    for turn in range(share):
        column = jnp.sum(jnp.where(lane == (grp_pos ^ turn), values, 0.0), axis=1, keepdims=True)
        term = column * pieces[turn][...]
        result = term if result is None else result + term
    out[...] = result


def by_steps(slots, groups, seq_pos, branch):
    order = jnp.arange(groups, dtype=jnp.int32) ^ seq_pos
    result = []
    for flip in range(2):
        held = jnp.stack(slots[flip * groups : (flip + 1) * groups])
        rows, chunk = held.shape[1:]
        split = held[order].reshape(groups, groups, 2, rows // (2 * groups), chunk)
        moved = jnp.transpose(split, (1, 2, 0, 3, 4)).reshape(groups, rows, chunk)
        picked = jnp.where(branch == 0, held, moved[order])
        result += [picked[turn] for turn in range(groups)]
    return result


def body(series, time_blocks, freq_blocks, positives, conv_weight, proj_weight):
    groups = lax.axis_size("seq")
    share = lax.axis_size("grp")
    sides = lax.axis_size("pair")
    seq_pos = lax.axis_index("seq")
    branch = lax.axis_index("pair")
    grp_pos = lax.axis_index("grp")
    samples, length, own_chan = series.shape
    assert samples == 1 and sides == 2
    full_len = length * groups
    hidden, width = conv_weight.shape[1:]
    emb_dim = proj_weight.shape[2]
    rest = full_len // (2 * LANES)
    tops = 2 * LANES // groups
    lows = rest // (LANES // tops)
    chans = own_chan // groups
    scalars = jnp.stack([seq_pos, branch, grp_pos]).astype(jnp.int32)

    piece = jax.ShapeDtypeStruct((chans * lows, LANES), F32)
    with jax.named_scope("arrange"):
        pieces = call(
            functools.partial(arrange_kernel, groups, rest),
            [piece] * groups,
            [SMEM, VMEM],
            [pltpu.VMEM((own_chan * lows, LANES), F32)],
            flops=10**8,
            moved=2 * 10**6,
        )(scalars, series[0])
    pieces = [pieces[0]] + [
        lax.ppermute(pieces[turn], "seq", [(i, i ^ turn) for i in range(groups)]) for turn in range(1, groups)
    ]
    wire = jax.ShapeDtypeStruct((2 * own_chan, length // 2), BF16)
    with jax.named_scope("time_view"):
        time_view = call(time_kernel, wire, [VMEM], flops=10**8, moved=2 * 10**6)(series[0])
    tables = [jnp.asarray(table) for table in fourier_tables(full_len)]
    with jax.named_scope("fourier"):
        own, pay = call(
            functools.partial(fourier_kernel, groups, full_len),
            [wire, wire],
            [SMEM] + [VMEM] * (5 + groups),
            [
                pltpu.VMEM((groups, chans * lows, LANES), F32),
                pltpu.VMEM((2 * chans * rest, LANES), F32),
                pltpu.VMEM((2 * own_chan, length // 2), F32),
            ],
            flops=10**9,
            moved=4 * 10**6,
        )(scalars, time_view, *tables, *pieces)

    slots = [None] * (2 * groups)
    for flip in range(2):
        for turn in range(0, groups, 2):
            block = pay if flip else own
            if flip or turn:
                pairs = [
                    (p * groups + i, (p ^ flip) * groups + (i ^ turn)) for p in range(2) for i in range(groups)
                ]
                block = lax.ppermute(block, ("pair", "seq"), pairs)
            slots[flip * groups + turn] = block
    for flip in range(2):
        for turn in range(0, groups, 2):
            slots[flip * groups + turn + 1] = lax.ppermute(
                slots[flip * groups + turn], "seq", [(i, i ^ 1) for i in range(groups)]
            )

    if chans % 8:
        slots = by_steps(slots, groups, seq_pos, branch)

    rows = hidden // (share * groups)
    picked = lax.dynamic_index_in_dim(
        conv_weight[0].reshape(share, groups, rows, width), seq_pos, 1, keepdims=False
    ).reshape(share * rows, width)
    proj_groups = proj_weight[0].reshape(share, groups, rows, emb_dim)
    proj_picked = lax.dynamic_index_in_dim(proj_groups, seq_pos, 1, keepdims=False)
    proj_own = lax.dynamic_index_in_dim(proj_picked, grp_pos, 0, keepdims=False)
    proj_picked = proj_picked.reshape(share * rows, emb_dim)
    halves = full_len // 2
    near_len = length // 2
    devices = sides * share * groups
    tile = 512
    with jax.named_scope("slope"):
        *grads, payload, near = call(
            functools.partial(slope_kernel, groups, tile),
            [jax.ShapeDtypeStruct((rows, width), F32)] * share
            + [
                jax.ShapeDtypeStruct((devices, 8, LANES), F32),
                jax.ShapeDtypeStruct((near_len + 24, LANES), F32),
            ],
            [SMEM] * 3 + [VMEM] * (2 + 2 * groups),
            [
                pltpu.VMEM((LANES, halves + 2 * LANES), F32),
                pltpu.VMEM((halves + 24, LANES), F32),
                pltpu.VMEM((halves + 16, LANES), F32),
                pltpu.VMEM((share * rows, width), F32),
                pltpu.VMEM((share * rows, LANES), F32),
            ],
            flops=4 * halves * 2 * share * rows * width,
            moved=4 * 10**6,
        )(scalars, time_blocks, freq_blocks, picked, proj_picked, *slots)
    arrived = lax.all_to_all(payload, ("pair", "grp", "seq"), split_axis=0, concat_axis=0, tiled=True)
    grads = [grads[0]] + [
        lax.ppermute(grads[turn], "grp", [(i, i ^ turn) for i in range(share)]) for turn in range(1, share)
    ]
    enc_tile = 256
    with jax.named_scope("encode"):
        encoded = pl.pallas_call(
            encode_kernel,
            out_shape=jax.ShapeDtypeStruct((near_len, hidden), BF16),
            grid=(near_len // enc_tile,),
            in_specs=[VMEM, VMEM],
            out_specs=pl.BlockSpec((enc_tile, hidden), lambda i: (i, 0)),
            compiler_params=pltpu.CompilerParams(vmem_limit_bytes=56 * 1024 * 1024),
            cost_estimate=pl.CostEstimate(
                flops=2 * length * hidden * width, bytes_accessed=4 * 10**6, transcendentals=length * hidden
            ),
        )(near, conv_weight[0])
    with jax.named_scope("loss"):
        loss, factors, proj_share = call(
            functools.partial(loss_kernel, groups, share, full_len),
            [
                jax.ShapeDtypeStruct((8, LANES), F32),
                jax.ShapeDtypeStruct((rows, LANES), F32),
                jax.ShapeDtypeStruct((groups * rows, emb_dim), F32),
            ],
            [SMEM] * 2 + [VMEM] * 2,
            flops=10**7,
            moved=10**6,
        )(scalars, positives, arrived, proj_own)
    with jax.named_scope("combine"):
        conv_share = call(
            functools.partial(combine_kernel, share),
            jax.ShapeDtypeStruct((rows, width), F32),
            [SMEM] + [VMEM] * (1 + share),
            flops=10**6,
            moved=5 * 10**5,
        )(scalars, factors, *grads)
    return (encoded[None, None], loss[0, 0], conv_share[None], proj_share[None])


def solution(mesh):
    in_specs = (
        P("grp", "seq", "pair"),
        P("grp", None),
        P("grp", None),
        P(),
        P("pair", None, None),
        P("pair", None, None),
    )
    out_specs = (
        P("pair", "grp", "seq", None),
        P(),
        P("pair", ("grp", "seq"), None),
        P("pair", "grp", None),
    )
    return jax.shard_map(body, mesh=mesh, in_specs=in_specs, out_specs=out_specs, check_vma=False)
```

profile of v0, /device:TPU:0, one launch (start us, length us, event | category | flops | bytes accessed | tf_op | source)
XLA Modules:
  0.0 74.7 jit_solution(7584723287115092276)
XLA Ops:
  0.6 0.0 copy-start
  0.7 2.3 %copy.15 = f32[1,2048,32]{2,1,0:T(8,128)} copy(f32[1,2048,32]{1,2,0:T(8,128)} %param.10) | data formatting | bytes 524288 | tf_op args[0]
  3.0 0.7 pad_add_fusion.scalars
  3.6 2.6 %arrange.1 = (f32[128,128]{1,0:T(8,128)}, f32[128,128]{1,0:T(8,128)}, f32[128,128]{1,0:T(8,128)}, f32[128,128]{1,0:T(8,128)}) custom-call(s32[3]{0:T(128)} %pad_add_fusion.scalars, f32[2048,32]{1,0:T(8,128)} %bitcast.19), custom_call_target="tpu_custom_call" | custom-call | flops 100000000 | bytes 2000000 | tf_op jit(solution)/shard_map/arrange/pallas_call | solution.py:400
  6.3 0.5 collective-permute-start
  6.7 2.5 %collective-permute-start.1 = (f32[128,128]{1,0:T(8,128)}, f32[128,128]{1,0:T(8,128)S(1)}, u32[]{:S(2)}, u32[]{:S(2)}) collective-permute-start(f32[128,128]{1,0:T(8,128)} %get-tuple-element.21), channel_id=1, source_target_pairs={{0,2},{1,3},{2,0},{3,1},{4,6},{5,7},{6,4},{7,5},{8,10},{9,11},{10,... | collective-permute-start | bytes 196616 | tf_op jit(solution)/shard_map/ppermute | solution.py:409
  9.2 0.1 collective-permute-start.2
  9.3 2.1 %time_view.1 = bf16[64,1024]{1,0:T(8,128)(2,1)} custom-call(f32[2048,32]{1,0:T(8,128)} %bitcast.20), custom_call_target="tpu_custom_call" | custom-call | flops 100000000 | bytes 2000000 | tf_op jit(solution)/shard_map/time_view/pallas_call | solution.py:413
  11.4 0.0 collective-permute-done.refs_1_
  11.4 0.8 %collective-permute-done.1.refs_2_ = f32[128,128]{1,0:T(8,128)S(1)} collective-permute-done((f32[128,128]{1,0:T(8,128)}, f32[128,128]{1,0:T(8,128)S(1)}, u32[]{:S(2)}, u32[]{:S(2)}) %collective-permute-start.1) | collective-permute-done | bytes 65568 | tf_op jit(solution)/shard_map/ppermute | solution.py:409
  12.2 1.3 %collective-permute-done.2.refs_3_ = f32[128,128]{1,0:T(8,128)S(1)} collective-permute-done((f32[128,128]{1,0:T(8,128)}, f32[128,128]{1,0:T(8,128)S(1)}, u32[]{:S(2)}, u32[]{:S(2)}) %collective-permute-start.2) | collective-permute-done | bytes 65568 | tf_op jit(solution)/shard_map/ppermute | solution.py:409
  13.5 0.6 copy-done.14
  14.1 2.8 %fourier.1 = (bf16[64,1024]{1,0:T(8,128)(2,1)}, bf16[64,1024]{1,0:T(8,128)(2,1)}) custom-call(s32[3]{0:T(128)} %pad_add_fusion.scalars, bf16[64,1024]{1,0:T(8,128)(2,1)} %time_view.1, bf16[768,512]{1,0:T(8,128)(2,1)} %constant.56.clone.stage_one, f32[32,256]{1,0:T(8,128)} %constant.57.clone.turn_cos, f32[32,256]{1,0:T(8,128)} %constant.58.clone.turn_sin, ...), custom_call_target="tpu_custom_call" | custom-call | flops 1000000000 | bytes 4000000 | tf_op jit(solution)/shard_map/fourier/pallas_call | solution.py:416
  16.9 2.4 %collective-permute-start.8 = (bf16[64,1024]{1,0:T(8,128)(2,1)}, bf16[64,1024]{1,0:T(8,128)(2,1)S(1)}, u32[]{:S(2)}, u32[]{:S(2)}) collective-permute-start(bf16[64,1024]{1,0:T(8,128)(2,1)} %get-tuple-element.24), channel_id=1, source_target_pairs={{0,18},{1,19},{2,16},{3,17},{16,2},{17,3},{18,0},{19,1},{4,22},{5,... | collective-permute-start | bytes 393224 | tf_op jit(solution)/shard_map/ppermute | solution.py:437
  19.4 0.5 collective-permute-start.6
  19.9 0.6 collective-permute-start.4
  20.4 0.0 collective-permute-start.3
  20.4 3.4 %collective-permute-done.8.refs_6_ = bf16[64,1024]{1,0:T(8,128)(2,1)S(1)} collective-permute-done((bf16[64,1024]{1,0:T(8,128)(2,1)}, bf16[64,1024]{1,0:T(8,128)(2,1)S(1)}, u32[]{:S(2)}, u32[]{:S(2)}) %collective-permute-start.8) | collective-permute-done | bytes 131104 | tf_op jit(solution)/shard_map/ppermute | solution.py:437
  23.9 0.0 collective-permute-start.9
  23.9 2.5 %collective-permute-done.6.refs_4_ = bf16[64,1024]{1,0:T(8,128)(2,1)S(1)} collective-permute-done((bf16[64,1024]{1,0:T(8,128)(2,1)}, bf16[64,1024]{1,0:T(8,128)(2,1)S(1)}, u32[]{:S(2)}, u32[]{:S(2)}) %collective-permute-start.6) | collective-permute-done | bytes 131104 | tf_op jit(solution)/shard_map/ppermute | solution.py:437
  26.4 0.0 collective-permute-start.7
  26.4 0.1 collective-permute-done.4.refs_2_
  26.5 0.4 collective-permute-start.5
  26.9 0.6 constant_dynamic-slice_fusion
  27.6 1.7 %constant_dynamic-slice_fusion.1 = bf16[4,1,64,512]{3,2,1,0:T(8,128)(2,1)} fusion(bf16[4,4,64,512]{3,2,1,0:T(8,128)(2,1)} %bitcast.23, s32[]{:T(128)S(6)} %select_n.14), kind=kLoop, calls=%fused_computation.2 | loop fusion | bytes 524292 | tf_op jit(solution)/shard_map/jit(dynamic_index_in_dim)/dynamic_slice | solution.py:449
  29.2 0.0 collective-permute-done.3.refs_1_
  29.2 0.0 collective-permute-done.9.refs_7_
  29.3 0.0 collective-permute-done.7.refs_5_
  29.3 0.0 collective-permute-done.5.refs_3_
  29.3 0.6 copy-done.8
  29.9 0.0 copy-done.9
  29.9 0.1 copy-done.10
  30.0 0.0 copy-done.11
  30.0 21.0 %slope.1 = (f32[64,512]{1,0:T(8,128)}, f32[64,512]{1,0:T(8,128)}, f32[64,512]{1,0:T(8,128)}, f32[64,512]{1,0:T(8,128)}, f32[32,8,128]{2,1,0:T(8,128)}, /*index=5*/f32[1048,128]{1,0:T(8,128)}) custom-call(s32[3]{0:T(128)} %pad_add_fusion.scalars, s32[1,4]{1,0:T(1,128)} %time_blocks.1, s32[1,4]{1,0:T(1,128)} %freq_blocks.1, bf16[256,512]{1,0:T(8,128)(2,1)} %bitcast.21, ...), custom_call_target="tpu_custom_call" | custom-call | flops 4294967296 | bytes 4000000 | tf_op jit(solution)/shard_map/slope/pallas_call | solution.py:461
  51.0 5.2 %all-to-all-start = ((f32[32,8,128]{2,1,0:T(8,128)}), f32[32,8,128]{2,1,0:T(8,128)S(1)}, u32[]{:S(2)}, u32[]{:S(2)}) async-start(f32[32,8,128]{2,1,0:T(8,128)} %get-tuple-element.26), calls=%async_computation | async-start | bytes 262144 | tf_op jit(solution)/shard_map/all_to_all | solution.py:479
  56.2 0.6 dynamic-slice_bitcast_fusion.projection
  56.8 1.8 %collective-permute-start.10 = (f32[64,512]{1,0:T(8,128)}, f32[64,512]{1,0:T(8,128)S(1)}, u32[]{:S(2)}, u32[]{:S(2)}) collective-permute-start(f32[64,512]{1,0:T(8,128)} %get-tuple-element.30), channel_id=1, source_target_pairs={{0,4},{4,0},{8,12},{12,8},{1,5},{5,1},{9,13},{13,9},{2,6},{6,2},{1... | collective-permute-start | bytes 393224 | tf_op jit(solution)/shard_map/ppermute | solution.py:481
  58.6 2.4 %collective-permute-start.11 = (f32[64,512]{1,0:T(8,128)}, f32[64,512]{1,0:T(8,128)S(1)}, u32[]{:S(2)}, u32[]{:S(2)}) collective-permute-start(f32[64,512]{1,0:T(8,128)} %get-tuple-element.31), channel_id=1, source_target_pairs={{0,8},{4,12},{8,0},{12,4},{1,9},{5,13},{9,1},{13,5},{2,10},{6,14},... | collective-permute-start | bytes 393224 | tf_op jit(solution)/shard_map/ppermute | solution.py:481
  61.0 0.2 collective-permute-start.12
  61.2 6.6 %encode.1 = bf16[1024,1024]{1,0:T(8,128)(2,1)} custom-call(f32[1048,128]{1,0:T(8,128)} %get-tuple-element.25.near, bf16[1024,512]{1,0:T(8,128)(2,1)} %bitcast.24), custom_call_target="tpu_custom_call" | custom-call | flops 2147483648 | bytes 4000000 | tf_op jit(solution)/shard_map/encode/pallas_call | solution.py:485
  67.8 0.7 copy-done.1
  68.4 2.4 %loss.1 = (f32[8,128]{1,0:T(8,128)}, f32[64,128]{1,0:T(8,128)}, f32[256,128]{1,0:T(8,128)}) custom-call(s32[3]{0:T(128)} %pad_add_fusion.scalars, s32[4]{0:T(128)} %positives.1, f32[32,8,128]{2,1,0:T(8,128)} %copy-done.1, bf16[64,128]{1,0:T(8,128)(2,1)} %dynamic-slice_bitcast_fusion.projection), custom_call_target="tpu_custom_call" | custom-call | flops 10000000 | bytes 1000000 | tf_op jit(solution)/shard_map/loss/pallas_call | solution.py:497
  70.8 1.2 %slice.3 = f32[1,1]{1,0:T(1,128)} slice(f32[8,128]{1,0:T(8,128)} %get-tuple-element.27), slice={[0:1], [0:1]} | slice | bytes 8 | tf_op jit(solution)/shard_map/slice | solution.py:516
  72.0 0.0 collective-permute-done.12.refs_3_
  72.1 0.6 copy-done.2
  72.7 0.0 copy-done.3
  72.7 0.1 copy-done.4
  72.8 1.9 %combine.1 = f32[64,512]{1,0:T(8,128)} custom-call(s32[3]{0:T(128)} %pad_add_fusion.scalars, f32[64,128]{1,0:T(8,128)} %get-tuple-element.28.factors, f32[64,512]{1,0:T(8,128)} %get-tuple-element.29.refs_0_, f32[64,512]{1,0:T(8,128)} %copy-done.2, f32[64,512]{1,0:T(8,128)} %copy-done.3, f32[64,512]{1,0:T(8,128)} %copy-done.4), custom_call_target="tpu_custom_call" | custom-call | flops 1000000 | bytes 500000 | tf_op jit(solution)/shard_map/combine/pallas_call | solution.py:509
  (23 shorter events, 0.0 us)
Async XLA Ops:
  0.6 26.3 %copy-start = (bf16[1,1024,128]{2,1,0:T(8,128)(2,1)S(1)}, bf16[1,1024,128]{2,1,0:T(8,128)(2,1)}, u32[]{:S(2)}) copy-start(bf16[1,1024,128]{2,1,0:T(8,128)(2,1)} %param.15) | copy-start | bytes 786436
  6.3 5.2 %collective-permute-start = (f32[128,128]{1,0:T(8,128)}, f32[128,128]{1,0:T(8,128)S(1)}, u32[]{:S(2)}, u32[]{:S(2)}) collective-permute-start(f32[128,128]{1,0:T(8,128)} %get-tuple-element.20), channel_id=1, source_target_pairs={{0,1},{1,0},{2,3},{3,2},{4,5},{5,4},{6,7},{7,6},{8,9},{9,8},{10,11... | collective-permute-start | bytes 196616 | tf_op jit(solution)/shard_map/ppermute | solution.py:409
  6.7 5.5 %collective-permute-start.1 = (f32[128,128]{1,0:T(8,128)}, f32[128,128]{1,0:T(8,128)S(1)}, u32[]{:S(2)}, u32[]{:S(2)}) collective-permute-start(f32[128,128]{1,0:T(8,128)} %get-tuple-element.21), channel_id=1, source_target_pairs={{0,2},{1,3},{2,0},{3,1},{4,6},{5,7},{6,4},{7,5},{8,10},{9,11},{10,... | collective-permute-start | bytes 196616 | tf_op jit(solution)/shard_map/ppermute | solution.py:409
  9.2 4.3 %collective-permute-start.2 = (f32[128,128]{1,0:T(8,128)}, f32[128,128]{1,0:T(8,128)S(1)}, u32[]{:S(2)}, u32[]{:S(2)}) collective-permute-start(f32[128,128]{1,0:T(8,128)} %get-tuple-element.22), channel_id=1, source_target_pairs={{0,3},{1,2},{2,1},{3,0},{4,7},{5,6},{6,5},{7,4},{8,11},{9,10},{10,... | collective-permute-start | bytes 196616 | tf_op jit(solution)/shard_map/ppermute | solution.py:409
  11.4 2.1 %copy-start.12 = (f32[128,128]{1,0:T(8,128)}, f32[128,128]{1,0:T(8,128)S(1)}, u32[]{:S(2)}) copy-start(f32[128,128]{1,0:T(8,128)S(1)} %collective-permute-done.refs_1_) | copy-start | bytes 196612
  12.2 1.3 %copy-start.13 = (f32[128,128]{1,0:T(8,128)}, f32[128,128]{1,0:T(8,128)S(1)}, u32[]{:S(2)}) copy-start(f32[128,128]{1,0:T(8,128)S(1)} %collective-permute-done.1.refs_2_) | copy-start | bytes 196612
  13.5 0.6 copy-start.14
  16.9 6.9 %collective-permute-start.8 = (bf16[64,1024]{1,0:T(8,128)(2,1)}, bf16[64,1024]{1,0:T(8,128)(2,1)S(1)}, u32[]{:S(2)}, u32[]{:S(2)}) collective-permute-start(bf16[64,1024]{1,0:T(8,128)(2,1)} %get-tuple-element.24), channel_id=1, source_target_pairs={{0,18},{1,19},{2,16},{3,17},{16,2},{17,3},{18,0},{19,1},{4,22},{5,... | collective-permute-start | bytes 393224 | tf_op jit(solution)/shard_map/ppermute | solution.py:437
  19.4 7.1 %collective-permute-start.6 = (bf16[64,1024]{1,0:T(8,128)(2,1)}, bf16[64,1024]{1,0:T(8,128)(2,1)S(1)}, u32[]{:S(2)}, u32[]{:S(2)}) collective-permute-start(bf16[64,1024]{1,0:T(8,128)(2,1)} %get-tuple-element.24), channel_id=1, source_target_pairs={{0,16},{1,17},{2,18},{3,19},{16,0},{17,1},{18,2},{19,3},{4,20},{5,... | collective-permute-start | bytes 393224 | tf_op jit(solution)/shard_map/ppermute | solution.py:437
  19.9 6.7 %collective-permute-start.4 = (bf16[64,1024]{1,0:T(8,128)(2,1)}, bf16[64,1024]{1,0:T(8,128)(2,1)S(1)}, u32[]{:S(2)}, u32[]{:S(2)}) collective-permute-start(bf16[64,1024]{1,0:T(8,128)(2,1)} %get-tuple-element.23.refs_0_), channel_id=1, source_target_pairs={{0,2},{1,3},{2,0},{3,1},{16,18},{17,19},{18,16},{19,17},{4,6},{5,7... | collective-permute-start | bytes 393224 | tf_op jit(solution)/shard_map/ppermute | solution.py:437
  20.4 8.8 %collective-permute-start.3 = (bf16[64,1024]{1,0:T(8,128)(2,1)}, bf16[64,1024]{1,0:T(8,128)(2,1)S(1)}, u32[]{:S(2)}, u32[]{:S(2)}) collective-permute-start(bf16[64,1024]{1,0:T(8,128)(2,1)} %get-tuple-element.23.refs_0_), channel_id=1, source_target_pairs={{0,1},{1,0},{2,3},{3,2},{4,5},{5,4},{6,7},{7,6},{8,9},{9,8},{10,11... | collective-permute-start | bytes 393224 | tf_op jit(solution)/shard_map/ppermute | solution.py:441
  23.9 5.4 %copy-start.5 = (bf16[64,1024]{1,0:T(8,128)(2,1)}, bf16[64,1024]{1,0:T(8,128)(2,1)S(1)}, u32[]{:S(2)}) copy-start(bf16[64,1024]{1,0:T(8,128)(2,1)S(1)} %collective-permute-done.8.refs_6_) | copy-start | bytes 393220
  23.9 5.4 %collective-permute-start.9 = (bf16[64,1024]{1,0:T(8,128)(2,1)S(1)}, bf16[64,1024]{1,0:T(8,128)(2,1)S(1)}, u32[]{:S(2)}, u32[]{:S(2)}) collective-permute-start(bf16[64,1024]{1,0:T(8,128)(2,1)S(1)} %collective-permute-done.8.refs_6_), channel_id=1, source_target_pairs={{0,1},{1,0},{2,3},{3,2},{4,5},{5,4},{6,7},{7,6},{8,9},{9,8},{10,11... | collective-permute-start | bytes 393224 | tf_op jit(solution)/shard_map/ppermute | solution.py:441
  26.4 2.9 %copy-start.6 = (bf16[64,1024]{1,0:T(8,128)(2,1)}, bf16[64,1024]{1,0:T(8,128)(2,1)S(1)}, u32[]{:S(2)}) copy-start(bf16[64,1024]{1,0:T(8,128)(2,1)S(1)} %collective-permute-done.6.refs_4_) | copy-start | bytes 393220
  26.4 2.9 %collective-permute-start.7 = (bf16[64,1024]{1,0:T(8,128)(2,1)S(1)}, bf16[64,1024]{1,0:T(8,128)(2,1)S(1)}, u32[]{:S(2)}, u32[]{:S(2)}) collective-permute-start(bf16[64,1024]{1,0:T(8,128)(2,1)S(1)} %collective-permute-done.6.refs_4_), channel_id=1, source_target_pairs={{0,1},{1,0},{2,3},{3,2},{4,5},{5,4},{6,7},{7,6},{8,9},{9,8},{10,11... | collective-permute-start | bytes 393224 | tf_op jit(solution)/shard_map/ppermute | solution.py:441
  26.5 2.8 %copy-start.7 = (bf16[64,1024]{1,0:T(8,128)(2,1)}, bf16[64,1024]{1,0:T(8,128)(2,1)S(1)}, u32[]{:S(2)}) copy-start(bf16[64,1024]{1,0:T(8,128)(2,1)S(1)} %collective-permute-done.4.refs_2_) | copy-start | bytes 393220
  26.5 2.8 %collective-permute-start.5 = (bf16[64,1024]{1,0:T(8,128)(2,1)S(1)}, bf16[64,1024]{1,0:T(8,128)(2,1)S(1)}, u32[]{:S(2)}, u32[]{:S(2)}) collective-permute-start(bf16[64,1024]{1,0:T(8,128)(2,1)S(1)} %collective-permute-done.4.refs_2_), channel_id=1, source_target_pairs={{0,1},{1,0},{2,3},{3,2},{4,5},{5,4},{6,7},{7,6},{8,9},{9,8},{10,11... | collective-permute-start | bytes 393224 | tf_op jit(solution)/shard_map/ppermute | solution.py:441
  29.2 0.7 copy-start.8
  29.3 0.7 copy-start.9
  29.3 0.7 copy-start.10
  29.3 0.7 copy-start.11
  51.0 16.8 %all-to-all-start = ((f32[32,8,128]{2,1,0:T(8,128)}), f32[32,8,128]{2,1,0:T(8,128)S(1)}, u32[]{:S(2)}, u32[]{:S(2)}) async-start(f32[32,8,128]{2,1,0:T(8,128)} %get-tuple-element.26), calls=%async_computation | async-start | bytes 262144 | tf_op jit(solution)/shard_map/all_to_all | solution.py:479
  56.8 15.2 %collective-permute-start.10 = (f32[64,512]{1,0:T(8,128)}, f32[64,512]{1,0:T(8,128)S(1)}, u32[]{:S(2)}, u32[]{:S(2)}) collective-permute-start(f32[64,512]{1,0:T(8,128)} %get-tuple-element.30), channel_id=1, source_target_pairs={{0,4},{4,0},{8,12},{12,8},{1,5},{5,1},{9,13},{13,9},{2,6},{6,2},{1... | collective-permute-start | bytes 393224 | tf_op jit(solution)/shard_map/ppermute | solution.py:481
  58.6 13.4 %collective-permute-start.11 = (f32[64,512]{1,0:T(8,128)}, f32[64,512]{1,0:T(8,128)S(1)}, u32[]{:S(2)}, u32[]{:S(2)}) collective-permute-start(f32[64,512]{1,0:T(8,128)} %get-tuple-element.31), channel_id=1, source_target_pairs={{0,8},{4,12},{8,0},{12,4},{1,9},{5,13},{9,1},{13,5},{2,10},{6,14},... | collective-permute-start | bytes 393224 | tf_op jit(solution)/shard_map/ppermute | solution.py:481
  61.0 11.0 %collective-permute-start.12 = (f32[64,512]{1,0:T(8,128)}, f32[64,512]{1,0:T(8,128)S(1)}, u32[]{:S(2)}, u32[]{:S(2)}) collective-permute-start(f32[64,512]{1,0:T(8,128)} %get-tuple-element.32), channel_id=1, source_target_pairs={{0,12},{4,8},{8,4},{12,0},{1,13},{5,9},{9,5},{13,1},{2,14},{6,10},... | collective-permute-start | bytes 393224 | tf_op jit(solution)/shard_map/ppermute | solution.py:481
  67.8 0.7 copy-start.1
  72.0 0.7 copy-start.2
  72.0 0.7 copy-start.3
  72.1 0.7 copy-start.4
where the time goes:
time: 75.1 us; the launch traced here: 74.7 us
  Pallas kernels  39.4 us (52%)
  starting transfers between devices  16.6 us (22%)
  local copies, waits for them, and re-layouts  9.11 us (12%)
  waiting for transfers between devices  8.14 us (11%)
  between operations  0.78 us (1%)
    pallas_call x1, Pallas kernels, body(): call(functools.partial(slope_kernel, groups, tile), [jax.ShapeDtypeStruct...  21 us
    pallas_call x1, Pallas kernels, body(): pl.pallas_call(encode_kernel, out_shape=jax.ShapeDtypeStruct((near_len, h...  6.58 us
    ppermute x3, waiting for transfers between devices, body(): block = lax.ppermute(block, ('pair', 'seq'), pairs)  6.05 us
    all_to_all x1, starting transfers between devices, body(): lax.all_to_all(payload, ('pair', 'grp', 'seq'), split_axis=0, concat_axis...  5.17 us
    unnamed x31, local copies, waits for them, and re-layouts  5.01 us
    ppermute x3, starting transfers between devices, body(): lax.ppermute(grads[turn], 'grp', [(i, i ^ turn) for i in range(share)])  4.39 us
    ppermute x3, starting transfers between devices, body(): block = lax.ppermute(block, ('pair', 'seq'), pairs)  3.49 us
    ppermute x3, starting transfers between devices, body(): lax.ppermute(pieces[turn], 'seq', [(i, i ^ turn) for i in range(groups)])  3.09 us
  transfers between devices with their start and end apart: 14, of which 5 were waited for; matrix products, arithmetic and copies ran while one was open for 5% of the time, Pallas kernels for 15%

commit v1 on v0

v1 whole, which is shorter than its diff:
```python
import functools
import math

import jax
import jax.numpy as jnp
import ml_dtypes
import numpy as np
from jax import lax
from jax.experimental import pallas as pl
from jax.experimental.pallas import tpu as pltpu
from jax.sharding import PartitionSpec as P

TAU = 0.2
LOSS_SCALE = 256.0
LANES = 128
ROOT = math.sqrt(2.0 / math.pi)
CUBIC = 0.044715
F32 = jnp.float32
BF16 = jnp.bfloat16

VMEM = pl.BlockSpec(memory_space=pltpu.VMEM)
SMEM = pl.BlockSpec(memory_space=pltpu.SMEM)


def call(kernel, out_shape, in_specs, scratch=(), flops=0, moved=0, room=16, out_specs=None):
    single = not isinstance(out_shape, (list, tuple))
    return pl.pallas_call(
        kernel,
        out_shape=out_shape,
        in_specs=in_specs,
        out_specs=out_specs or (VMEM if single else [VMEM] * len(out_shape)),
        scratch_shapes=list(scratch),
        compiler_params=pltpu.CompilerParams(vmem_limit_bytes=room * 1024 * 1024),
        cost_estimate=pl.CostEstimate(flops=flops, bytes_accessed=moved, transcendentals=0),
    )


def split_high_low(table):
    high = table.astype(ml_dtypes.bfloat16)
    low = (table - high.astype(np.float64)).astype(ml_dtypes.bfloat16)
    return high, low


def lane_order(low_count):
    inner = min(low_count, LANES)
    parts = LANES // inner
    lane = np.arange(LANES)
    return parts * (lane % inner) + lane // inner


def fourier_tables(full_len):
    low_count = full_len // LANES
    first = np.arange(low_count)
    rest = np.arange(LANES)
    second = lane_order(low_count)
    angle = (first[:, None] * first[None, :] % low_count) * (2.0 * np.pi / low_count)
    high, small = split_high_low(np.concatenate([np.cos(angle), -np.sin(angle)], axis=0))
    stage_one = np.concatenate([high, small, high], axis=1)
    turn = (first[:, None] * rest[None, :] % full_len) * (2.0 * np.pi / full_len)
    angle = (rest[:, None] * second[None, :] % LANES) * (2.0 * np.pi / LANES)
    cos, sin = np.cos(angle), np.sin(angle)
    high, small = split_high_low(np.block([[cos, -sin], [sin, cos]]))
    stage_two = np.concatenate([high, small, high], axis=0)
    return stage_one, np.cos(turn).astype(np.float32), np.sin(turn).astype(np.float32), stage_two


def arrange_kernel(scalars, series, *pieces):
    me = scalars[0]
    for turn, piece in enumerate(pieces):
        piece[...] = series[me ^ turn]


def high_low(values):
    high = values.astype(BF16)
    return high, (values - high.astype(F32)).astype(BF16)


def keep_lanes(scalars, first, number, low_count, block_len):
    lane = lax.broadcasted_iota(jnp.int32, (8, LANES), 1)
    inner = min(low_count, LANES)
    parts = LANES // inner
    high = parts * (lane % inner) + lane // inner
    block = high * low_count // block_len
    keep = jnp.ones((8, LANES), F32)
    for entry in range(first, first + number):
        keep = jnp.where(block == scalars[entry], 0.0, keep)
    return keep[0:1]


def fourier_kernel(
    groups, full_len, block_len, listed, scalars, stage_one, turn_cos, turn_sin, stage_two, *refs
):
    pieces = refs[:groups]
    own, pay, gathered, steps, mags, views, wire = refs[groups:]
    me, branch = scalars[0], scalars[1]
    low_count = full_len // LANES
    chans, length = pieces[0].shape
    tops = length // LANES
    for turn in range(groups):
        gathered[turn] = pieces[turn][...]
    for source in range(groups):
        block = gathered[source ^ me]
        for top in range(tops):
            at = (source * tops + top) * chans
            steps[at : at + chans, :] = block[:, top * LANES : (top + 1) * LANES]
    columns = [steps[pl.ds(chan, low_count, stride=chans), :] for chan in range(chans)]
    high, low = high_low(jnp.concatenate(columns, axis=1))
    first = jnp.dot(stage_one[...], jnp.concatenate([high, high, low], axis=0), preferred_element_type=F32)
    cos, sin = turn_cos[...], turn_sin[...]
    turned = []
    for chan in range(chans):
        part = first[:, chan * LANES : (chan + 1) * LANES]
        part_re, part_im = part[:low_count], part[low_count:]
        turned.append(jnp.concatenate([part_re * cos + part_im * sin, part_im * cos - part_re * sin], axis=1))
    high, low = high_low(jnp.concatenate(turned, axis=0))
    second = jnp.dot(jnp.concatenate([high, high, low], axis=1), stage_two[...], preferred_element_type=F32)
    spec_re, spec_im = second[:, :LANES], second[:, LANES:]
    magnitude = jnp.sqrt(1.0 + (spec_re * spec_re + spec_im * spec_im) * (1.0 / full_len))
    mags[...] = magnitude.astype(BF16).astype(F32) * keep_lanes(scalars, 3 + listed, listed, low_count, block_len)
    time_keep = keep_lanes(scalars, 3, listed, low_count, block_len)
    for chan in range(chans):
        if low_count < LANES:
            turned_steps = columns[chan].T
            view = jnp.concatenate(
                [turned_steps[part * low_count : (part + 1) * low_count] for part in range(LANES // low_count)], axis=1
            )
        else:
            parts = low_count // LANES
            view = jnp.concatenate(
                [steps[pl.ds(chan + chans * part, LANES, stride=chans * parts), :].T for part in range(parts)], axis=0
            )
        views[chan * low_count : (chan + 1) * low_count, :] = view * time_keep

    def spread(held, out):
        for low in range(low_count):
            wire[chans * low : chans * (low + 1), :] = held[pl.ds(low, chans, stride=low_count), :]
        out[...] = wire[...].astype(BF16)

    @pl.when(branch == 0)
    def _():
        spread(views, own)
        spread(mags, pay)

    @pl.when(branch != 0)
    def _():
        spread(mags, own)
        spread(views, pay)


def gelu_parts(values):
    square = values * values
    curve = jnp.tanh(values * (ROOT + (ROOT * CUBIC) * square))
    half = 0.5 * values
    return square, curve, half


def stack_rows(window, count):
    return jnp.concatenate([window[6 + shift : 6 + shift + count] for shift in range(4)], axis=1).astype(BF16)


def shift_high(tile, low_count, step):
    inner = min(low_count, LANES)
    lane = lax.broadcasted_iota(jnp.int32, tile.shape, 1)
    if step < 0:
        moved = jnp.where(lane < inner, pltpu.roll(tile, (inner + 1) % LANES, 1), pltpu.roll(tile, inner % LANES, 1))
        return jnp.where(lane == 0, 0.0, moved)
    back = LANES - inner
    moved = jnp.where(lane < back, pltpu.roll(tile, back, 1), pltpu.roll(tile, (back - 1) % LANES, 1))
    return jnp.where(lane == LANES - 1, 0.0, moved)


def swap_units(values, outer, inner):
    unit = outer * inner * 8
    blocks = []
    for start in range(0, values.shape[0], unit):
        for second in range(inner):
            for first in range(outer):
                at = start + (first * inner + second) * 8
                blocks.append(values[at : at + 8])
    return jnp.concatenate(blocks, axis=0)


def prepare_kernel(groups, share, ready, scalars, weight, picked, stage_one, turn_cos, turn_sin, stage_two, *outs):
    full, part, *tables = outs
    me = scalars[0]
    full[...] = swap_units(weight[...].astype(F32).T, 2, 8).astype(BF16)
    if ready:
        rows = picked[...]
    else:
        size = weight.shape[0] // (share * groups)
        starts = [pl.multiple_of((group * groups + me) * size, 16) for group in range(share)]
        rows = jnp.concatenate([weight[pl.ds(start, size), :] for start in starts], axis=0)
    part[...] = swap_units(rows.astype(F32).T, 2, 8).astype(BF16)
    for table, out in zip((stage_one, turn_cos, turn_sin, stage_two), tables):
        out[...] = table[...]


def slope_kernel(groups, ready, merged, scalars, weights, projection, *refs):
    count = 1 if ready else 2 * groups
    slots = refs[:count]
    grads = refs[count:-6]
    payload, flat, odd, total, pool, split = refs[-6:]
    me, branch, grp_pos = scalars[0], scalars[1], scalars[2]
    lows = flat.shape[0] - 4
    low_count = 2 * lows
    share = len(grads)
    wide = 4 * LANES
    rows = grads[0].shape[0]
    if ready:
        flat[2 : 2 + lows] = slots[0][...].reshape(lows, LANES, LANES)
        heads = projection[...]
    else:
        for flip in range(2):
            for turn in range(groups):
                at = pl.multiple_of(((branch ^ flip) * groups + (me ^ turn)) * 16, 16)
                flat[2 : 2 + lows, pl.ds(at, 16), :] = slots[flip * groups + turn][...].reshape(lows, 16, LANES)
        starts = [pl.multiple_of((group * groups + me) * rows, 16) for group in range(share)]
        heads = jnp.concatenate([projection[pl.ds(start, rows), :] for start in starts], axis=0)
    for edge in range(2):
        flat[edge] = shift_high(flat[lows + edge].astype(F32), low_count, -1).astype(BF16)
        flat[lows + 2 + edge] = shift_high(flat[2 + edge].astype(F32), low_count, 1).astype(BF16)
    current = flat[0].astype(F32).reshape(8, 2, 8, LANES)
    for index in range(lows + 3):
        following = flat[index + 1].astype(F32).reshape(8, 2, 8, LANES)
        mixed = jnp.concatenate([current[:, 1:2], following[:, 0:1]], axis=1)
        odd[index] = mixed.reshape(LANES, LANES).astype(BF16)
        current = following
    total[...] = jnp.zeros_like(total)
    pool[...] = jnp.zeros_like(pool)

    def step(index, _):
        first = index * merged
        sums = pool[...]
        for source in (flat, odd):
            across = jnp.concatenate(
                [
                    jnp.concatenate([source[first + item + move] for move in range(4)], axis=0)
                    for item in range(merged)
                ],
                axis=1,
            )
            preact = lax.dot_general(across, weights[...], (((0,), (0,)), ((), ())), preferred_element_type=F32)
            square, curve, half = gelu_parts(preact)
            active = half + half * curve
            sums = sums + jnp.sum(active.reshape(merged * LANES // 8, 8, active.shape[1]), axis=0)
            slope = (0.5 + 0.5 * curve) + (half * (1.0 - curve * curve)) * (ROOT + (3.0 * ROOT * CUBIC) * square)
            total[...] += jnp.dot(across, slope.astype(BF16), preferred_element_type=F32)
        pool[...] = sums
        return 0

    lax.fori_loop(0, lows // merged, step, 0)
    line = jnp.sum(pool[...], axis=0, keepdims=True)
    column = jnp.broadcast_to(line, (LANES, line.shape[1])).T
    latent = jnp.sum(column * heads.astype(F32), axis=0, keepdims=True)
    payload[...] = jnp.zeros_like(payload)
    for device in range(payload.shape[0]):
        target = device // groups % share
        payload[device, 0:1, :] = latent
        payload[device, 1:2, 0:rows] = line[:, target * rows : (target + 1) * rows]
    split[...] = swap_units(total[...], 8, 2).T.reshape(share, rows, wide)
    for turn in range(share):
        grads[turn][...] = split[grp_pos ^ turn]


def odd_rows(even, following):
    lane = lax.broadcasted_iota(jnp.int32, even.shape, 1)
    return jnp.where(lane % 16 < 8, pltpu.roll(even, LANES - 8, 1), pltpu.roll(following, 8, 1))


def encode_kernel(groups, scalars, flat, weights, out, tall, near):
    tile = out.shape[0]
    lows = flat.shape[0] - 4

    @pl.when(pl.program_id(0) == 0)
    def _():
        me = scalars[0]
        for index in range(lows + 4):
            tall[index * LANES : (index + 1) * LANES, :] = flat[index].astype(F32).T
        inner = min(2 * lows, LANES)
        parts = LANES // inner
        highs = LANES // groups
        end = 8 + highs * lows
        near[0:8, :] = jnp.zeros((8, LANES), F32)
        near[end:, :] = jnp.zeros((16, LANES), F32)
        for item in range(highs):
            high = me * highs + item
            lane = (high % parts) * inner + high // parts
            if item == 0:
                near[6:8, :] = tall[pl.ds(lane, 2, stride=LANES), :]
            near[8 + item * lows : 8 + (item + 1) * lows, :] = tall[pl.ds(2 * LANES + lane, lows, stride=LANES), :]
            if item == highs - 1:
                near[end : end + 2, :] = tall[pl.ds((lows + 2) * LANES + lane, 2, stride=LANES), :]

    at = pl.multiple_of(pl.program_id(0) * tile, tile)
    window = near[pl.ds(at, tile + 24), :]
    even = window[: tile + 16]
    shifted = odd_rows(even, window[1 : tile + 17])
    sums = None
    for rows in (even, shifted):
        preact = jnp.dot(stack_rows(rows, tile), weights[...], preferred_element_type=F32)
        _, curve, half = gelu_parts(preact)
        active = half + half * curve
        sums = active if sums is None else sums + active
    out[...] = (sums * 0.5).astype(BF16)


def loss_kernel(groups, share, full_len, listed, ready, scalars, arrived, projection, loss, factors, grad):
    branch, grp_pos = scalars[1], scalars[2]
    batch = share
    exact = lax.Precision.HIGHEST
    latents = []
    for side in range(2):
        lines = []
        for item in range(batch):
            base = (side * share + item) * groups
            line = arrived[base, 0:1, :]
            for turn in range(1, groups):
                line = line + arrived[base + turn, 0:1, :]
            lines.append(line * (1.0 / full_len))
        latents.append(jnp.concatenate(lines, axis=0))
    scale = [lax.rsqrt(jnp.sum(latent * latent, axis=1, keepdims=True) + 1e-06) for latent in latents]
    embs = [latent * factor for latent, factor in zip(latents, scale)]
    logits = lax.dot_general(embs[0], embs[1], (((1,), (1,)), ((), ())), precision=exact, preferred_element_type=F32) / TAU
    row = lax.broadcasted_iota(jnp.int32, logits.shape, 0)
    col = lax.broadcasted_iota(jnp.int32, logits.shape, 1)
    target = jnp.zeros_like(logits)
    for item in range(batch):
        target = jnp.where((row == item) & (col == scalars[3 + 2 * listed + item]), 1.0, target)
    power = jnp.exp(logits)
    row_sum = jnp.sum(power, axis=1, keepdims=True)
    col_sum = jnp.sum(power, axis=0, keepdims=True)
    value = (
        jnp.sum(jnp.log(row_sum), axis=(0, 1), keepdims=True)
        + jnp.sum(jnp.log(col_sum), axis=(0, 1), keepdims=True)
        - 2.0 * jnp.sum(target * logits, axis=(0, 1), keepdims=True)
    ) / (2.0 * batch)
    loss[0, 0] = jnp.sum(value)
    slope = (power / row_sum + power / col_sum - 2.0 * target) * (LOSS_SCALE / (2.0 * batch * TAU))
    emb_grads = [
        lax.dot_general(slope, embs[1], (((1,), (0,)), ((), ())), precision=exact, preferred_element_type=F32),
        lax.dot_general(slope.T, embs[0], (((1,), (0,)), ((), ())), precision=exact, preferred_element_type=F32),
    ]
    own = []
    for side in range(2):
        inner = jnp.sum(emb_grads[side] * embs[side], axis=1, keepdims=True)
        own.append(scale[side] * (emb_grads[side] - embs[side] * inner))
    latent_grad = jnp.where(branch == 0, own[0], own[1])
    rows = factors.shape[0]
    if ready:
        weights = projection[...].astype(F32)
    else:
        start = pl.multiple_of((grp_pos * groups + scalars[0]) * rows, 16)
        weights = projection[pl.ds(start, rows), :].astype(F32)
    lane = lax.broadcasted_iota(jnp.int32, (rows, LANES), 1)
    spread = jnp.zeros((rows, LANES), F32)
    for item in range(batch):
        column = jnp.sum(weights * latent_grad[item : item + 1, :], axis=1, keepdims=True) * (1.0 / full_len)
        spread = jnp.where(lane == item, column, spread)
    factors[...] = spread
    for turn in range(groups):
        lines = [arrived[(branch * share + item) * groups + turn, 1:2, :] for item in range(batch)]
        lines = lines + [jnp.zeros((8 - batch % 8, LANES), F32)] if batch % 8 else lines
        sums = jnp.concatenate(lines, axis=0).T * (1.0 / full_len)
        value = sums[:, 0:1] * latent_grad[0:1, :]
        for item in range(1, batch):
            value = value + sums[:, item : item + 1] * latent_grad[item : item + 1, :]
        grad[turn * rows : (turn + 1) * rows, :] = value[:rows]


def combine_kernel(share, scalars, factors, *refs):
    pieces, out = refs[:share], refs[share]
    grp_pos = scalars[2]
    values = factors[...]
    lane = lax.broadcasted_iota(jnp.int32, values.shape, 1)
    result = None
    for turn in range(share):
        column = jnp.sum(jnp.where(lane == (grp_pos ^ turn), values, 0.0), axis=1, keepdims=True)
        term = column * pieces[turn][...]
        result = term if result is None else result + term
    out[...] = result


def assemble(slots, groups, low_count, seq_pos, branch):
    order = jnp.arange(groups, dtype=jnp.int32) ^ seq_pos
    held = jnp.stack(slots).reshape(2, groups, low_count // 2, 2, -1, LANES)[:, order]
    held = jnp.where(branch == 0, held, held[::-1])
    held = jnp.transpose(held, (2, 3, 0, 1, 4, 5)).reshape(low_count // 2, 2, 8, 8, LANES)
    return jnp.transpose(held, (0, 2, 1, 3, 4)).reshape(-1, LANES)


def body(series, time_blocks, freq_blocks, positives, conv_weight, proj_weight):
    groups = lax.axis_size("seq")
    share = lax.axis_size("grp")
    sides = lax.axis_size("pair")
    seq_pos = lax.axis_index("seq")
    branch = lax.axis_index("pair")
    grp_pos = lax.axis_index("grp")
    samples, length, own_chan = series.shape
    assert samples == 1 and sides == 2 and 4 * own_chan == LANES
    full_len = length * groups
    hidden, width = conv_weight.shape[1:]
    emb_dim = proj_weight.shape[2]
    chans = own_chan // groups
    low_count = full_len // LANES
    lows = low_count // 2
    rows = hidden // (share * groups)
    listed = time_blocks.shape[1]
    ready = chans != 8 or rows % 16 != 0
    places = jnp.stack([seq_pos, branch, grp_pos]).astype(jnp.int32)
    scalars = jnp.concatenate([places, time_blocks[0], freq_blocks[0], positives])
    weight, heads = conv_weight[0], proj_weight[0]
    picked, own_heads, mid_heads = weight, heads, heads
    if ready:
        picked = lax.dynamic_index_in_dim(weight.reshape(share, groups, rows, width), seq_pos, 1, keepdims=False)
        picked = picked.reshape(share * rows, width)
        mid_heads = lax.dynamic_index_in_dim(heads.reshape(share, groups, rows, emb_dim), seq_pos, 1, keepdims=False)
        mid_heads = mid_heads.reshape(share * rows, emb_dim)
        own_heads = lax.dynamic_slice_in_dim(heads, (grp_pos * groups + seq_pos) * rows, rows, 0)

    piece = jax.ShapeDtypeStruct((chans, length), F32)
    with jax.named_scope("arrange"):
        pieces = call(arrange_kernel, [piece] * groups, [SMEM, VMEM], moved=5 * 10**5)(
            scalars, series[0].T.reshape(groups, chans, length)
        )
    pieces = [pieces[0]] + [
        lax.ppermute(pieces[turn], "seq", [(i, i ^ turn) for i in range(groups)]) for turn in range(1, groups)
    ]
    tables = [jnp.asarray(table) for table in fourier_tables(full_len)]
    with jax.named_scope("prepare"):
        weights, part_weights, *tables = call(
            functools.partial(prepare_kernel, groups, share, ready),
            [jax.ShapeDtypeStruct((width, hidden), BF16), jax.ShapeDtypeStruct((width, share * rows), BF16)]
            + [jax.ShapeDtypeStruct(table.shape, table.dtype) for table in tables],
            [SMEM] + [VMEM] * 6,
            flops=10**8,
            moved=3 * 10**6,
            room=24,
        )(scalars, weight, picked, *tables)
    wire = jax.ShapeDtypeStruct((chans * low_count, LANES), BF16)
    with jax.named_scope("fourier"):
        own, pay = call(
            functools.partial(fourier_kernel, groups, full_len, length // 8, listed),
            [wire, wire],
            [SMEM] + [VMEM] * (4 + groups),
            [
                pltpu.VMEM((groups, chans, length), F32),
                pltpu.VMEM((chans * low_count, LANES), F32),
                pltpu.VMEM((chans * low_count, LANES), F32),
                pltpu.VMEM((chans * low_count, LANES), F32),
                pltpu.VMEM((chans * low_count, LANES), F32),
            ],
            flops=10**9,
            moved=2 * 10**6,
        )(scalars, *tables, *pieces)

    slots = [None] * (2 * groups)
    for flip in range(2):
        for turn in range(0, groups, 2):
            block = pay if flip else own
            if flip or turn:
                pairs = [
                    (p * groups + i, (p ^ flip) * groups + (i ^ turn)) for p in range(2) for i in range(groups)
                ]
                block = lax.ppermute(block, ("pair", "seq"), pairs)
            slots[flip * groups + turn] = block
    for flip in range(2):
        for turn in range(0, groups, 2):
            slots[flip * groups + turn + 1] = lax.ppermute(
                slots[flip * groups + turn], "seq", [(i, i ^ 1) for i in range(groups)]
            )
    if ready:
        slots = [assemble(slots, groups, low_count, seq_pos, branch)]

    devices = sides * share * groups
    tiles = jax.ShapeDtypeStruct((lows + 4, LANES, LANES), BF16)
    with jax.named_scope("slope"):
        *grads, payload, flat = call(
            functools.partial(slope_kernel, groups, ready, 8),
            [jax.ShapeDtypeStruct((rows, width), F32)] * share
            + [jax.ShapeDtypeStruct((devices, 8, LANES), F32), tiles],
            [SMEM] + [VMEM] * (2 + len(slots)),
            [
                pltpu.VMEM((lows + 4, LANES, LANES), BF16),
                pltpu.VMEM((width, share * rows), F32),
                pltpu.VMEM((8, share * rows), F32),
                pltpu.VMEM((share, rows, width), F32),
            ],
            flops=4 * full_len * share * rows * width,
            moved=4 * 10**6,
            room=20 + 8 * (low_count // LANES),
        )(scalars, part_weights, mid_heads, *slots)
    grads = [grads[0]] + [
        lax.ppermute(grads[turn], "grp", [(i, i ^ turn) for i in range(share)]) for turn in range(1, share)
    ]
    arrived = lax.all_to_all(payload, ("pair", "grp", "seq"), split_axis=0, concat_axis=0, tiled=True)
    enc_tile = 256
    near_len = length // 2
    with jax.named_scope("encode"):
        encoded = pl.pallas_call(
            functools.partial(encode_kernel, groups),
            out_shape=jax.ShapeDtypeStruct((near_len, hidden), BF16),
            grid=(near_len // enc_tile,),
            in_specs=[SMEM, VMEM, VMEM],
            out_specs=pl.BlockSpec((enc_tile, hidden), lambda i: (i, 0)),
            scratch_shapes=[
                pltpu.VMEM(((lows + 4) * LANES, LANES), F32),
                pltpu.VMEM((near_len + 24, LANES), F32),
            ],
            compiler_params=pltpu.CompilerParams(vmem_limit_bytes=(20 + 12 * (low_count // LANES)) * 1024 * 1024),
            cost_estimate=pl.CostEstimate(
                flops=2 * length * hidden * width, bytes_accessed=4 * 10**6, transcendentals=length * hidden
            ),
        )(scalars, flat, weights)
    with jax.named_scope("loss"):
        loss, factors, proj_share = call(
            functools.partial(loss_kernel, groups, share, full_len, listed, ready),
            [
                jax.ShapeDtypeStruct((1, 1), F32),
                jax.ShapeDtypeStruct((rows, LANES), F32),
                jax.ShapeDtypeStruct((groups * rows, emb_dim), F32),
            ],
            [SMEM] + [VMEM] * 2,
            flops=10**7,
            moved=10**6,
            out_specs=[SMEM, VMEM, VMEM],
        )(scalars, arrived, own_heads)
    with jax.named_scope("combine"):
        conv_share = call(
            functools.partial(combine_kernel, share),
            jax.ShapeDtypeStruct((rows, width), F32),
            [SMEM] + [VMEM] * (1 + share),
            flops=10**6,
            moved=5 * 10**5,
        )(scalars, factors, *grads)
    return (encoded[None, None], loss.reshape(()), conv_share[None], proj_share[None])


def solution(mesh):
    in_specs = (
        P("grp", "seq", "pair"),
        P("grp", None),
        P("grp", None),
        P(),
        P("pair", None, None),
        P("pair", None, None),
    )
    out_specs = (
        P("pair", "grp", "seq", None),
        P(),
        P("pair", ("grp", "seq"), None),
        P("pair", "grp", None),
    )
    return jax.shard_map(body, mesh=mesh, in_specs=in_specs, out_specs=out_specs, check_vma=False)
```

time: 75.1 us -> 57.6 us (0.77)
  Pallas kernels: 39.4 us -> 23.7 us
  local copies, waits for them, and re-layouts: 9.11 us -> 6.3 us
  waiting for transfers between devices: 8.14 us -> 9.85 us
    pallas_call x6, Pallas kernels: 37.5 us -> 22.3 us  [the longest x1 10.8 us: body(): call(functools.partial(slope_kernel, groups, ready, 8), [jax.ShapeDtypeSt...]
    dynamic_slice x2 -> x0, local copies, waits for them, and re-layouts: 2.31 us -> none  [the longest x1 1.67 us: body(): lax.dynamic_index_in_dim(conv_weight[0].reshape(share, groups, rows, widt...]
    ppermute x3, waiting for transfers between devices: 0.01 us -> 2.31 us  [body(): lax.ppermute(grads[turn], 'grp', [(i, i ^ turn) for i in range(share)])]
    ppermute x3, waiting for transfers between devices: 2.07 us -> 0.01 us  [body(): lax.ppermute(pieces[turn], 'seq', [(i, i ^ turn) for i in range(groups)])]
    slice x1 -> x0, local copies, waits for them, and re-layouts: 1.18 us -> none  [body(): return (encoded[None, None], loss[0, 0], conv_share[None], proj_share[None])]
    ppermute x4, waiting for transfers between devices: 0.01 us -> 1.02 us  [body(): lax.ppermute(slots[flip * groups + turn], 'seq', [(i, i ^ 1) for i in ran...]
    concatenate x0 -> x1, local copies, waits for them, and re-layouts: none -> 0.77 us  [body(): jnp.concatenate([places, time_blocks[0], freq_blocks[0], positives])]
    unnamed x31 -> x14, local copies, waits for them, and re-layouts: 5.01 us -> 5.53 us
  transfers between devices with their start and end apart: 14 -> 14, of which waited for: 5 -> 5; matrix products, arithmetic and copies ran while one was open for 5% -> 0% of each run, Pallas kernels for 15% -> 17%
where the time goes in v1:
time: 57.6 us; the launch traced here: 57.1 us
  Pallas kernels  23.7 us (41%)
  starting transfers between devices  16.6 us (29%)
  waiting for transfers between devices  9.85 us (17%)
  local copies, waits for them, and re-layouts  6.3 us (11%)
  between operations  0.74 us (1%)
    pallas_call x1, Pallas kernels, body(): call(functools.partial(slope_kernel, groups, ready, 8), [jax.ShapeDtypeSt...  10.8 us
    pallas_call x1, Pallas kernels, body(): pl.pallas_call(functools.partial(encode_kernel, groups), out_shape=jax.Sh...  6.55 us
    ppermute x3, waiting for transfers between devices, body(): block = lax.ppermute(block, ('pair', 'seq'), pairs)  6.51 us
    unnamed x14, local copies, waits for them, and re-layouts  5.53 us
    all_to_all x1, starting transfers between devices, body(): lax.all_to_all(payload, ('pair', 'grp', 'seq'), split_axis=0, concat_axis...  4.93 us
    ppermute x3, starting transfers between devices, body(): lax.ppermute(grads[turn], 'grp', [(i, i ^ turn) for i in range(share)])  4.45 us
    ppermute x3, starting transfers between devices, body(): block = lax.ppermute(block, ('pair', 'seq'), pairs)  3.55 us
    ppermute x3, starting transfers between devices, body(): lax.ppermute(pieces[turn], 'seq', [(i, i ^ turn) for i in range(groups)])  3.15 us
  transfers between devices with their start and end apart: 14, of which 5 were waited for; matrix products, arithmetic and copies ran while one was open for 0% of the time, Pallas kernels for 17%

profile of v1, /device:TPU:0, one launch (start us, length us, event | category | flops | bytes accessed | tf_op | source)
XLA Modules:
  0.0 57.1 jit_solution(18352946210049598116)
XLA Ops:
  0.6 0.8 %concatenate.3.scalars = s32[15]{0:T(128)S(1)} concatenate(s32[1]{0:T(128)} %bitcast, s32[1]{0:T(128)} %bitcast.1, s32[1]{0:T(128)} %bitcast.2, s32[4]{0:T(128)} %bitcast.22, s32[4]{0:T(128)} %bitcast.23, s32[4]{0:T(128)} %param.13), dimensions={0} | concatenate | bytes 120 | tf_op jit(solution)/shard_map/concatenate | solution.py:410
  1.4 0.0 copy-start.3
  1.4 0.9 %copy-done.3 = f32[1,2048,32]{1,2,0:T(8,128)S(1)} copy-done((f32[1,2048,32]{1,2,0:T(8,128)S(1)}, f32[1,2048,32]{1,2,0:T(8,128)}, u32[]{:S(2)}) %copy-start.3) | copy-done | bytes 262168
  2.4 0.6 arrange.1
  2.9 0.5 collective-permute-start
  3.4 2.6 %collective-permute-start.1 = (f32[8,2048]{1,0:T(8,128)S(1)}, f32[8,2048]{1,0:T(8,128)S(1)}, u32[]{:S(2)}, u32[]{:S(2)}) collective-permute-start(f32[8,2048]{1,0:T(8,128)S(1)} %get-tuple-element.32), channel_id=1, source_target_pairs={{0,2},{1,3},{2,0},{3,1},{4,6},{5,7},{6,4},{7,5},{8,10},{9,11},{10,... | collective-permute-start | bytes 196616 | tf_op jit(solution)/shard_map/ppermute | solution.py:426
  6.0 0.1 collective-permute-start.2
  6.1 0.0 copy-start
  6.1 1.2 %copy-done = bf16[1,1024,512]{2,1,0:T(8,128)(2,1)S(1)} copy-done((bf16[1,1024,512]{2,1,0:T(8,128)(2,1)S(1)}, bf16[1,1024,512]{2,1,0:T(8,128)(2,1)}, u32[]{:S(2)}) %copy-start) | copy-done | bytes 1048600
  7.3 0.0 copy-start.1
  7.3 1.0 %copy-done.1 = bf16[768,256]{1,0:T(8,128)(2,1)S(1)} copy-done((bf16[768,256]{1,0:T(8,128)(2,1)S(1)}, bf16[768,256]{1,0:T(8,128)(2,1)}, u32[]{:S(2)}) %copy-start.1) | copy-done | bytes 393240
  8.3 0.0 copy-start.4
  8.3 0.8 %copy-done.4 = bf16[128,192]{1,0:T(8,128)(2,1)S(1)} copy-done((bf16[128,192]{1,0:T(8,128)(2,1)S(1)}, bf16[128,192]{1,0:T(8,128)(2,1)}, u32[]{:S(2)}) %copy-start.4) | copy-done | bytes 49176
  9.1 0.8 %copy-done.5 = f32[64,128]{1,0:T(8,128)S(1)} copy-done((f32[64,128]{1,0:T(8,128)S(1)}, f32[64,128]{1,0:T(8,128)}, u32[]{:S(2)}) %copy-start.5) | copy-done | bytes 32792
  9.9 0.8 %copy-done.6 = f32[64,128]{1,0:T(8,128)S(1)} copy-done((f32[64,128]{1,0:T(8,128)S(1)}, f32[64,128]{1,0:T(8,128)}, u32[]{:S(2)}) %copy-start.6) | copy-done | bytes 32792
  10.7 1.0 %prepare.1 = (bf16[512,1024]{1,0:T(8,128)(2,1)S(1)}, bf16[512,256]{1,0:T(8,128)(2,1)S(1)}, bf16[128,192]{1,0:T(8,128)(2,1)S(1)}, f32[64,128]{1,0:T(8,128)S(1)}, ...) custom-call(s32[15]{0:T(128)S(1)} %concatenate.3.scalars, bf16[1024,512]{1,0:T(8,128)(2,1)S(1)} %bitcast.16, ...), custom_call_target="tpu_custom_call" | custom-call | flops 100000000 | bytes 3000000 | tf_op jit(solution)/shard_map/prepare/pallas_call | solution.py:430
  11.6 0.0 copy-start.2
  11.6 0.0 collective-permute-done.refs_1_
  11.7 0.0 collective-permute-done.1.refs_2_
  11.7 0.0 collective-permute-done.2.refs_3_
  11.7 1.4 %fourier.1 = (bf16[512,128]{1,0:T(8,128)(2,1)S(1)}, bf16[512,128]{1,0:T(8,128)(2,1)S(1)}) custom-call(s32[15]{0:T(128)S(1)} %concatenate.3.scalars, bf16[128,192]{1,0:T(8,128)(2,1)S(1)} %get-tuple-element.26.stage_one, f32[64,128]{1,0:T(8,128)S(1)} %get-tuple-element.27.turn_cos, f32[64,128]{1,0:T(8,128)S(1)} %get-tuple-element.28.turn_sin, ...), custom_call_target="tpu_custom_call" | custom-call | flops 1000000000 | bytes 2000000 | tf_op jit(solution)/shard_map/fourier/pallas_call | solution.py:441
  13.1 1.8 %collective-permute-start.4 = (bf16[512,128]{1,0:T(8,128)(2,1)S(1)}, bf16[512,128]{1,0:T(8,128)(2,1)S(1)}, u32[]{:S(2)}, u32[]{:S(2)}) collective-permute-start(bf16[512,128]{1,0:T(8,128)(2,1)S(1)} %get-tuple-element.34.refs_0_), channel_id=1, source_target_pairs={{0,2},{1,3},{2,0},{3,1},{16,18},{17,19},{18,16},{19,17},{4,6},{5,7... | collective-permute-start | bytes 393224 | tf_op jit(solution)/shard_map/ppermute | solution.py:464
  14.9 1.5 %collective-permute-start.6 = (bf16[512,128]{1,0:T(8,128)(2,1)S(1)}, bf16[512,128]{1,0:T(8,128)(2,1)S(1)}, u32[]{:S(2)}, u32[]{:S(2)}) collective-permute-start(bf16[512,128]{1,0:T(8,128)(2,1)S(1)} %get-tuple-element.35), channel_id=1, source_target_pairs={{0,16},{1,17},{2,18},{3,19},{16,0},{17,1},{18,2},{19,3},{4,20},{5,... | collective-permute-start | bytes 393224 | tf_op jit(solution)/shard_map/ppermute | solution.py:464
  16.4 0.2 collective-permute-start.8
  16.7 0.0 collective-permute-start.3
  16.7 2.3 %collective-permute-done.4.refs_2_ = bf16[512,128]{1,0:T(8,128)(2,1)S(1)} collective-permute-done((bf16[512,128]{1,0:T(8,128)(2,1)S(1)}, bf16[512,128]{1,0:T(8,128)(2,1)S(1)}, u32[]{:S(2)}, u32[]{:S(2)}) %collective-permute-start.4) | collective-permute-done | bytes 131104 | tf_op jit(solution)/shard_map/ppermute | solution.py:464
  19.0 0.0 collective-permute-start.5
  19.0 4.2 %collective-permute-done.6.refs_4_ = bf16[512,128]{1,0:T(8,128)(2,1)S(1)} collective-permute-done((bf16[512,128]{1,0:T(8,128)(2,1)S(1)}, bf16[512,128]{1,0:T(8,128)(2,1)S(1)}, u32[]{:S(2)}, u32[]{:S(2)}) %collective-permute-start.6) | collective-permute-done | bytes 131104 | tf_op jit(solution)/shard_map/ppermute | solution.py:464
  23.2 0.0 collective-permute-start.7
  23.2 0.0 collective-permute-done.8.refs_6_
  23.2 0.5 collective-permute-start.9
  23.7 0.0 collective-permute-done.3.refs_1_
  23.7 0.0 collective-permute-done.5.refs_3_
  23.7 0.8 %collective-permute-done.7.refs_5_ = bf16[512,128]{1,0:T(8,128)(2,1)S(1)} collective-permute-done((bf16[512,128]{1,0:T(8,128)(2,1)S(1)}, bf16[512,128]{1,0:T(8,128)(2,1)S(1)}, u32[]{:S(2)}, u32[]{:S(2)}) %collective-permute-start.7) | collective-permute-done | bytes 131104 | tf_op jit(solution)/shard_map/ppermute | solution.py:468
  24.5 0.2 collective-permute-done.9.refs_7_
  24.7 0.0 copy-done.2
  24.7 10.8 %slope.1 = (f32[64,512]{1,0:T(8,128)S(1)}, f32[64,512]{1,0:T(8,128)S(1)}, f32[64,512]{1,0:T(8,128)S(1)}, f32[64,512]{1,0:T(8,128)S(1)}, f32[32,8,128]{2,1,0:T(8,128)}, /*index=5*/bf16[36,128,128]{2,1,0:T(8,128)(2,1)S(1)}) custom-call(s32[15]{0:T(128)S(1)} %concatenate.3.scalars, bf16[512,256]{1,0:T(8,128)(2,1)S(1)} %get-tuple-element.25.weights, ...), custom_call_target="tpu_custom_call" | custom-call | flops 4294967296 | bytes 4000000 | tf_op jit(solution)/shard_map/slope/pallas_call | solution.py:477
  35.5 4.9 %all-to-all-start = ((f32[32,8,128]{2,1,0:T(8,128)}), f32[32,8,128]{2,1,0:T(8,128)S(1)}, u32[]{:S(2)}, u32[]{:S(2)}) async-start(f32[32,8,128]{2,1,0:T(8,128)} %get-tuple-element.38), calls=%async_computation | async-start | bytes 262144 | tf_op jit(solution)/shard_map/all_to_all | solution.py:495
  40.5 1.8 %collective-permute-start.10 = (f32[64,512]{1,0:T(8,128)S(1)}, f32[64,512]{1,0:T(8,128)S(1)}, u32[]{:S(2)}, u32[]{:S(2)}) collective-permute-start(f32[64,512]{1,0:T(8,128)S(1)} %get-tuple-element.42), channel_id=1, source_target_pairs={{0,4},{4,0},{8,12},{12,8},{1,5},{5,1},{9,13},{13,9},{2,6},{6,2},{1... | collective-permute-start | bytes 393224 | tf_op jit(solution)/shard_map/ppermute | solution.py:493
  42.3 2.4 %collective-permute-start.11 = (f32[64,512]{1,0:T(8,128)S(1)}, f32[64,512]{1,0:T(8,128)S(1)}, u32[]{:S(2)}, u32[]{:S(2)}) collective-permute-start(f32[64,512]{1,0:T(8,128)S(1)} %get-tuple-element.43), channel_id=1, source_target_pairs={{0,8},{4,12},{8,0},{12,4},{1,9},{5,13},{9,1},{13,5},{2,10},{6,14},... | collective-permute-start | bytes 393224 | tf_op jit(solution)/shard_map/ppermute | solution.py:493
  44.7 0.2 collective-permute-start.12
  44.9 6.5 %encode.1 = bf16[1024,1024]{1,0:T(8,128)(2,1)} custom-call(s32[15]{0:T(128)S(1)} %concatenate.3.scalars, bf16[36,128,128]{2,1,0:T(8,128)(2,1)S(1)} %get-tuple-element.36.flat, bf16[512,1024]{1,0:T(8,128)(2,1)S(1)} %get-tuple-element.37.weights), custom_call_target="tpu_custom_call" | custom-call | flops 2147483648 | bytes 4000000 | tf_op jit(solution)/shard_map/encode/pallas_call | solution.py:499
  51.5 0.0 all-to-all-done.arrived
  51.5 2.0 %loss.1 = (f32[1,1]{1,0:T(1,128)}, f32[64,128]{1,0:T(8,128)S(1)}, f32[256,128]{1,0:T(8,128)}) custom-call(s32[15]{0:T(128)S(1)} %concatenate.3.scalars, f32[32,8,128]{2,1,0:T(8,128)S(1)} %all-to-all-done.arrived, bf16[1024,128]{1,0:T(8,128)(2,1)S(1)} %bitcast.19), custom_call_target="tpu_custom_call" | custom-call | flops 10000000 | bytes 1000000 | tf_op jit(solution)/shard_map/loss/pallas_call | solution.py:515
  53.5 0.0 collective-permute-done.10.refs_1_
  53.5 0.0 collective-permute-done.11.refs_2_
  53.5 2.3 %collective-permute-done.12.refs_3_ = f32[64,512]{1,0:T(8,128)S(1)} collective-permute-done((f32[64,512]{1,0:T(8,128)S(1)}, f32[64,512]{1,0:T(8,128)S(1)}, u32[]{:S(2)}, u32[]{:S(2)}) %collective-permute-start.12) | collective-permute-done | bytes 131104 | tf_op jit(solution)/shard_map/ppermute | solution.py:493
  55.8 1.3 %combine.1 = f32[64,512]{1,0:T(8,128)} custom-call(s32[15]{0:T(128)S(1)} %concatenate.3.scalars, f32[64,128]{1,0:T(8,128)S(1)} %get-tuple-element.40.factors, f32[64,512]{1,0:T(8,128)S(1)} %get-tuple-element.41.refs_0_, f32[64,512]{1,0:T(8,128)S(1)} %collective-permute-done.10.refs_1_, f32[64,512]{1,0:T(8,128)S(1)} %collective-permute-done.11.refs_2_, ...), custom_call_target="tpu_custom_call" | custom-call | flops 1000000 | bytes 500000 | tf_op jit(solution)/shard_map/combine/pallas_call | solution.py:528
  (2 shorter events, 0.0 us)
Async XLA Ops:
  1.4 1.0 %copy-start.3 = (f32[1,2048,32]{1,2,0:T(8,128)S(1)}, f32[1,2048,32]{1,2,0:T(8,128)}, u32[]{:S(2)}) copy-start(f32[1,2048,32]{1,2,0:T(8,128)} %param.10) | copy-start | bytes 786436
  2.9 8.7 %collective-permute-start = (f32[8,2048]{1,0:T(8,128)S(1)}, f32[8,2048]{1,0:T(8,128)S(1)}, u32[]{:S(2)}, u32[]{:S(2)}) collective-permute-start(f32[8,2048]{1,0:T(8,128)S(1)} %get-tuple-element.31), channel_id=1, source_target_pairs={{0,1},{1,0},{2,3},{3,2},{4,5},{5,4},{6,7},{7,6},{8,9},{9,8},{10,11... | collective-permute-start | bytes 196616 | tf_op jit(solution)/shard_map/ppermute | solution.py:426
  3.4 8.2 %collective-permute-start.1 = (f32[8,2048]{1,0:T(8,128)S(1)}, f32[8,2048]{1,0:T(8,128)S(1)}, u32[]{:S(2)}, u32[]{:S(2)}) collective-permute-start(f32[8,2048]{1,0:T(8,128)S(1)} %get-tuple-element.32), channel_id=1, source_target_pairs={{0,2},{1,3},{2,0},{3,1},{4,6},{5,7},{6,4},{7,5},{8,10},{9,11},{10,... | collective-permute-start | bytes 196616 | tf_op jit(solution)/shard_map/ppermute | solution.py:426
  6.0 5.7 %collective-permute-start.2 = (f32[8,2048]{1,0:T(8,128)S(1)}, f32[8,2048]{1,0:T(8,128)S(1)}, u32[]{:S(2)}, u32[]{:S(2)}) collective-permute-start(f32[8,2048]{1,0:T(8,128)S(1)} %get-tuple-element.33), channel_id=1, source_target_pairs={{0,3},{1,2},{2,1},{3,0},{4,7},{5,6},{6,5},{7,4},{8,11},{9,10},{10,... | collective-permute-start | bytes 196616 | tf_op jit(solution)/shard_map/ppermute | solution.py:426
  6.1 1.2 %copy-start = (bf16[1,1024,512]{2,1,0:T(8,128)(2,1)S(1)}, bf16[1,1024,512]{2,1,0:T(8,128)(2,1)}, u32[]{:S(2)}) copy-start(bf16[1,1024,512]{2,1,0:T(8,128)(2,1)} %param.14) | copy-start | bytes 3145732
  7.3 1.0 %copy-start.1 = (bf16[768,256]{1,0:T(8,128)(2,1)S(1)}, bf16[768,256]{1,0:T(8,128)(2,1)}, u32[]{:S(2)}) copy-start(bf16[768,256]{1,0:T(8,128)(2,1)} %constant.24.clone.stage_two) | copy-start | bytes 1179652
  8.3 0.8 %copy-start.4 = (bf16[128,192]{1,0:T(8,128)(2,1)S(1)}, bf16[128,192]{1,0:T(8,128)(2,1)}, u32[]{:S(2)}) copy-start(bf16[128,192]{1,0:T(8,128)(2,1)} %constant.21.clone.stage_one) | copy-start | bytes 147460
  9.1 0.8 %copy-start.5 = (f32[64,128]{1,0:T(8,128)S(1)}, f32[64,128]{1,0:T(8,128)}, u32[]{:S(2)}) copy-start(f32[64,128]{1,0:T(8,128)} %constant.22.clone.turn_cos) | copy-start | bytes 98308
  9.9 0.8 %copy-start.6 = (f32[64,128]{1,0:T(8,128)S(1)}, f32[64,128]{1,0:T(8,128)}, u32[]{:S(2)}) copy-start(f32[64,128]{1,0:T(8,128)} %constant.23.clone.turn_sin) | copy-start | bytes 98308
  11.6 13.1 %copy-start.2 = (bf16[1,1024,128]{2,1,0:T(8,128)(2,1)S(1)}, bf16[1,1024,128]{2,1,0:T(8,128)(2,1)}, u32[]{:S(2)}) copy-start(bf16[1,1024,128]{2,1,0:T(8,128)(2,1)} %param.15) | copy-start | bytes 786436
  13.1 5.9 %collective-permute-start.4 = (bf16[512,128]{1,0:T(8,128)(2,1)S(1)}, bf16[512,128]{1,0:T(8,128)(2,1)S(1)}, u32[]{:S(2)}, u32[]{:S(2)}) collective-permute-start(bf16[512,128]{1,0:T(8,128)(2,1)S(1)} %get-tuple-element.34.refs_0_), channel_id=1, source_target_pairs={{0,2},{1,3},{2,0},{3,1},{16,18},{17,19},{18,16},{19,17},{4,6},{5,7... | collective-permute-start | bytes 393224 | tf_op jit(solution)/shard_map/ppermute | solution.py:464
  14.9 8.3 %collective-permute-start.6 = (bf16[512,128]{1,0:T(8,128)(2,1)S(1)}, bf16[512,128]{1,0:T(8,128)(2,1)S(1)}, u32[]{:S(2)}, u32[]{:S(2)}) collective-permute-start(bf16[512,128]{1,0:T(8,128)(2,1)S(1)} %get-tuple-element.35), channel_id=1, source_target_pairs={{0,16},{1,17},{2,18},{3,19},{16,0},{17,1},{18,2},{19,3},{4,20},{5,... | collective-permute-start | bytes 393224 | tf_op jit(solution)/shard_map/ppermute | solution.py:464
  16.4 6.8 %collective-permute-start.8 = (bf16[512,128]{1,0:T(8,128)(2,1)S(1)}, bf16[512,128]{1,0:T(8,128)(2,1)S(1)}, u32[]{:S(2)}, u32[]{:S(2)}) collective-permute-start(bf16[512,128]{1,0:T(8,128)(2,1)S(1)} %get-tuple-element.35), channel_id=1, source_target_pairs={{0,18},{1,19},{2,16},{3,17},{16,2},{17,3},{18,0},{19,1},{4,22},{5,... | collective-permute-start | bytes 393224 | tf_op jit(solution)/shard_map/ppermute | solution.py:464
  16.7 7.0 %collective-permute-start.3 = (bf16[512,128]{1,0:T(8,128)(2,1)S(1)}, bf16[512,128]{1,0:T(8,128)(2,1)S(1)}, u32[]{:S(2)}, u32[]{:S(2)}) collective-permute-start(bf16[512,128]{1,0:T(8,128)(2,1)S(1)} %get-tuple-element.34.refs_0_), channel_id=1, source_target_pairs={{0,1},{1,0},{2,3},{3,2},{4,5},{5,4},{6,7},{7,6},{8,9},{9,8},{10,11... | collective-permute-start | bytes 393224 | tf_op jit(solution)/shard_map/ppermute | solution.py:468
  19.0 4.7 %collective-permute-start.5 = (bf16[512,128]{1,0:T(8,128)(2,1)S(1)}, bf16[512,128]{1,0:T(8,128)(2,1)S(1)}, u32[]{:S(2)}, u32[]{:S(2)}) collective-permute-start(bf16[512,128]{1,0:T(8,128)(2,1)S(1)} %collective-permute-done.4.refs_2_), channel_id=1, source_target_pairs={{0,1},{1,0},{2,3},{3,2},{4,5},{5,4},{6,7},{7,6},{8,9},{9,8},{10,11... | collective-permute-start | bytes 393224 | tf_op jit(solution)/shard_map/ppermute | solution.py:468
  23.2 1.3 %collective-permute-start.7 = (bf16[512,128]{1,0:T(8,128)(2,1)S(1)}, bf16[512,128]{1,0:T(8,128)(2,1)S(1)}, u32[]{:S(2)}, u32[]{:S(2)}) collective-permute-start(bf16[512,128]{1,0:T(8,128)(2,1)S(1)} %collective-permute-done.6.refs_4_), channel_id=1, source_target_pairs={{0,1},{1,0},{2,3},{3,2},{4,5},{5,4},{6,7},{7,6},{8,9},{9,8},{10,11... | collective-permute-start | bytes 393224 | tf_op jit(solution)/shard_map/ppermute | solution.py:468
  23.2 1.5 %collective-permute-start.9 = (bf16[512,128]{1,0:T(8,128)(2,1)S(1)}, bf16[512,128]{1,0:T(8,128)(2,1)S(1)}, u32[]{:S(2)}, u32[]{:S(2)}) collective-permute-start(bf16[512,128]{1,0:T(8,128)(2,1)S(1)} %collective-permute-done.8.refs_6_), channel_id=1, source_target_pairs={{0,1},{1,0},{2,3},{3,2},{4,5},{5,4},{6,7},{7,6},{8,9},{9,8},{10,11... | collective-permute-start | bytes 393224 | tf_op jit(solution)/shard_map/ppermute | solution.py:468
  35.5 15.9 %all-to-all-start = ((f32[32,8,128]{2,1,0:T(8,128)}), f32[32,8,128]{2,1,0:T(8,128)S(1)}, u32[]{:S(2)}, u32[]{:S(2)}) async-start(f32[32,8,128]{2,1,0:T(8,128)} %get-tuple-element.38), calls=%async_computation | async-start | bytes 262144 | tf_op jit(solution)/shard_map/all_to_all | solution.py:495
  40.5 13.0 %collective-permute-start.10 = (f32[64,512]{1,0:T(8,128)S(1)}, f32[64,512]{1,0:T(8,128)S(1)}, u32[]{:S(2)}, u32[]{:S(2)}) collective-permute-start(f32[64,512]{1,0:T(8,128)S(1)} %get-tuple-element.42), channel_id=1, source_target_pairs={{0,4},{4,0},{8,12},{12,8},{1,5},{5,1},{9,13},{13,9},{2,6},{6,2},{1... | collective-permute-start | bytes 393224 | tf_op jit(solution)/shard_map/ppermute | solution.py:493
  42.3 11.2 %collective-permute-start.11 = (f32[64,512]{1,0:T(8,128)S(1)}, f32[64,512]{1,0:T(8,128)S(1)}, u32[]{:S(2)}, u32[]{:S(2)}) collective-permute-start(f32[64,512]{1,0:T(8,128)S(1)} %get-tuple-element.43), channel_id=1, source_target_pairs={{0,8},{4,12},{8,0},{12,4},{1,9},{5,13},{9,1},{13,5},{2,10},{6,14},... | collective-permute-start | bytes 393224 | tf_op jit(solution)/shard_map/ppermute | solution.py:493
  44.7 11.1 %collective-permute-start.12 = (f32[64,512]{1,0:T(8,128)S(1)}, f32[64,512]{1,0:T(8,128)S(1)}, u32[]{:S(2)}, u32[]{:S(2)}) collective-permute-start(f32[64,512]{1,0:T(8,128)S(1)} %get-tuple-element.44), channel_id=1, source_target_pairs={{0,12},{4,8},{8,4},{12,0},{1,13},{5,9},{9,5},{13,1},{2,14},{6,10},... | collective-permute-start | bytes 393224 | tf_op jit(solution)/shard_map/ppermute | solution.py:493

commit v2 on v1

--- a/solution.py
+++ b/solution.py
@@ -3,7 +3,6 @@
 
 import jax
 import jax.numpy as jnp
-import ml_dtypes
 import numpy as np
 from jax import lax
 from jax.experimental import pallas as pl
@@ -20,6 +19,7 @@
 
 VMEM = pl.BlockSpec(memory_space=pltpu.VMEM)
 SMEM = pl.BlockSpec(memory_space=pltpu.SMEM)
+HBM = pl.BlockSpec(memory_space=pltpu.HBM)
 
 
 def call(kernel, out_shape, in_specs, scratch=(), flops=0, moved=0, room=16, out_specs=None):
@@ -35,12 +35,6 @@
     )
 
 
-def split_high_low(table):
-    high = table.astype(ml_dtypes.bfloat16)
-    low = (table - high.astype(np.float64)).astype(ml_dtypes.bfloat16)
-    return high, low
-
-
 def lane_order(low_count):
     inner = min(low_count, LANES)
     parts = LANES // inner
@@ -54,20 +48,25 @@
     rest = np.arange(LANES)
     second = lane_order(low_count)
     angle = (first[:, None] * first[None, :] % low_count) * (2.0 * np.pi / low_count)
-    high, small = split_high_low(np.concatenate([np.cos(angle), -np.sin(angle)], axis=0))
-    stage_one = np.concatenate([high, small, high], axis=1)
+    stage_one = np.concatenate([np.cos(angle), -np.sin(angle)], axis=0)
     turn = (first[:, None] * rest[None, :] % full_len) * (2.0 * np.pi / full_len)
     angle = (rest[:, None] * second[None, :] % LANES) * (2.0 * np.pi / LANES)
     cos, sin = np.cos(angle), np.sin(angle)
-    high, small = split_high_low(np.block([[cos, -sin], [sin, cos]]))
-    stage_two = np.concatenate([high, small, high], axis=0)
-    return stage_one, np.cos(turn).astype(np.float32), np.sin(turn).astype(np.float32), stage_two
-
-
-def arrange_kernel(scalars, series, *pieces):
-    me = scalars[0]
-    for turn, piece in enumerate(pieces):
-        piece[...] = series[me ^ turn]
+    stage_two = np.block([[cos, -sin], [sin, cos]])
+    wide = np.zeros((2 * low_count, 2 * LANES))
+    wide[:, :low_count] = stage_one
+    turns = np.concatenate([np.cos(turn), np.sin(turn)], axis=1)
+    return np.concatenate([stage_two, turns, wide], axis=0).astype(np.float32)
+
+
+def arrange_kernel(series, *refs):
+    *pieces, done = refs
+    me = lax.axis_index("seq")
+    copies = [pltpu.make_async_copy(series.at[me ^ turn], piece, done.at[turn]) for turn, piece in enumerate(pieces)]
+    for copy in copies:
+        copy.start()
+    for copy in copies:
+        copy.wait()
 
 
 def high_low(values):
@@ -88,7 +87,7 @@
 
 
 def fourier_kernel(
-    groups, full_len, block_len, listed, scalars, stage_one, turn_cos, turn_sin, stage_two, *refs
+    groups, full_len, block_len, listed, scalars, stage_one, turns, stage_two, *refs
 ):
     pieces = refs[:groups]
     own, pay, gathered, steps, mags, views, wire = refs[groups:]
@@ -106,7 +105,7 @@
     columns = [steps[pl.ds(chan, low_count, stride=chans), :] for chan in range(chans)]
     high, low = high_low(jnp.concatenate(columns, axis=1))
     first = jnp.dot(stage_one[...], jnp.concatenate([high, high, low], axis=0), preferred_element_type=F32)
-    cos, sin = turn_cos[...], turn_sin[...]
+    cos, sin = turns[:, :LANES], turns[:, LANES:]
     turned = []
     for chan in range(chans):
         part = first[:, chan * LANES : (chan + 1) * LANES]
@@ -147,11 +146,9 @@
         spread(views, pay)
 
 
-def gelu_parts(values):
-    square = values * values
-    curve = jnp.tanh(values * (ROOT + (ROOT * CUBIC) * square))
-    half = 0.5 * values
-    return square, curve, half
+def gelu_parts(half):
+    square = half * half
+    return square, 1.0 + jnp.tanh(half * (2.0 * ROOT + (8.0 * ROOT * CUBIC) * square))
 
 
 def stack_rows(window, count):
@@ -180,22 +177,28 @@
     return jnp.concatenate(blocks, axis=0)
 
 
-def prepare_kernel(groups, share, ready, scalars, weight, picked, stage_one, turn_cos, turn_sin, stage_two, *outs):
-    full, part, *tables = outs
+def prepare_kernel(groups, share, low_count, scalars, weight, picked, table, full, part, stage_one, turns, stage_two):
     me = scalars[0]
-    full[...] = swap_units(weight[...].astype(F32).T, 2, 8).astype(BF16)
-    if ready:
+    full[...] = swap_units(0.5 * weight[...].astype(F32).T, 2, 8).astype(BF16)
+    if picked is not None:
         rows = picked[...]
     else:
         size = weight.shape[0] // (share * groups)
         starts = [pl.multiple_of((group * groups + me) * size, 16) for group in range(share)]
         rows = jnp.concatenate([weight[pl.ds(start, size), :] for start in starts], axis=0)
-    part[...] = swap_units(rows.astype(F32).T, 2, 8).astype(BF16)
-    for table, out in zip((stage_one, turn_cos, turn_sin, stage_two), tables):
-        out[...] = table[...]
-
-
-def slope_kernel(groups, ready, merged, scalars, weights, projection, *refs):
+    part[...] = swap_units(0.5 * rows.astype(F32).T, 2, 8).astype(BF16)
+    high, low = high_low(table[: 2 * LANES])
+    stage_two[...] = jnp.concatenate([high, low, high], axis=0)
+    turns[...] = table[2 * LANES : 2 * LANES + low_count]
+    high, low = high_low(table[2 * LANES + low_count :, :low_count])
+    stage_one[...] = jnp.concatenate([high, low, high], axis=1)
+
+
+def prepare_whole(kernel, scalars, weight, *refs):
+    kernel(scalars, weight, None, *refs)
+
+
+def slope_kernel(groups, ready, merged, small, scalars, weights, projection, *refs):
     count = 1 if ready else 2 * groups
     slots = refs[:count]
     grads = refs[count:-6]
@@ -232,19 +235,23 @@
         first = index * merged
         sums = pool[...]
         for source in (flat, odd):
-            across = jnp.concatenate(
-                [
-                    jnp.concatenate([source[first + item + move] for move in range(4)], axis=0)
-                    for item in range(merged)
-                ],
-                axis=1,
+            patches, slopes = [], []
+            for item in range(0, merged, small):
+                stacks = [
+                    jnp.concatenate([source[first + item + at + move] for move in range(4)], axis=0)
+                    for at in range(small)
+                ]
+                across = jnp.concatenate(stacks, axis=1)
+                half = lax.dot_general(across, weights[...], (((0,), (0,)), ((), ())), preferred_element_type=F32)
+                square, curve = gelu_parts(half)
+                active = half * curve
+                sums = sums + jnp.sum(active.reshape(small * LANES // 8, 8, active.shape[1]), axis=0)
+                inner = half * (2.0 - curve) * (ROOT + (12.0 * ROOT * CUBIC) * square)
+                slopes.append((curve * (0.5 + inner)).astype(BF16))
+                patches.append(across)
+            total[...] += jnp.dot(
+                jnp.concatenate(patches, axis=1), jnp.concatenate(slopes, axis=0), preferred_element_type=F32
             )
-            preact = lax.dot_general(across, weights[...], (((0,), (0,)), ((), ())), preferred_element_type=F32)
-            square, curve, half = gelu_parts(preact)
-            active = half + half * curve
-            sums = sums + jnp.sum(active.reshape(merged * LANES // 8, 8, active.shape[1]), axis=0)
-            slope = (0.5 + 0.5 * curve) + (half * (1.0 - curve * curve)) * (ROOT + (3.0 * ROOT * CUBIC) * square)
-            total[...] += jnp.dot(across, slope.astype(BF16), preferred_element_type=F32)
         pool[...] = sums
         return 0
 
@@ -267,8 +274,8 @@
     return jnp.where(lane % 16 < 8, pltpu.roll(even, LANES - 8, 1), pltpu.roll(following, 8, 1))
 
 
-def encode_kernel(groups, scalars, flat, weights, out, tall, near):
-    tile = out.shape[0]
+def encode_kernel(groups, chunk, scalars, flat, weights, out, tall, near, patches):
+    count = out.shape[0]
     lows = flat.shape[0] - 4
 
     @pl.when(pl.program_id(0) == 0)
@@ -290,91 +297,85 @@
             near[8 + item * lows : 8 + (item + 1) * lows, :] = tall[pl.ds(2 * LANES + lane, lows, stride=LANES), :]
             if item == highs - 1:
                 near[end : end + 2, :] = tall[pl.ds((lows + 2) * LANES + lane, 2, stride=LANES), :]
-
-    at = pl.multiple_of(pl.program_id(0) * tile, tile)
-    window = near[pl.ds(at, tile + 24), :]
-    even = window[: tile + 16]
-    shifted = odd_rows(even, window[1 : tile + 17])
-    sums = None
-    for rows in (even, shifted):
-        preact = jnp.dot(stack_rows(rows, tile), weights[...], preferred_element_type=F32)
-        _, curve, half = gelu_parts(preact)
-        active = half + half * curve
-        sums = active if sums is None else sums + active
-    out[...] = (sums * 0.5).astype(BF16)
-
-
-def loss_kernel(groups, share, full_len, listed, ready, scalars, arrived, projection, loss, factors, grad):
+        for start in range(0, count, LANES):
+            window = near[start : start + LANES + 24, :]
+            even = window[: LANES + 16]
+            patches[0, start : start + LANES, :] = stack_rows(even, LANES)
+            patches[1, start : start + LANES, :] = stack_rows(odd_rows(even, window[1 : LANES + 17]), LANES)
+
+    for start in range(0, count, chunk):
+        sums = None
+        for parity in range(2):
+            half = jnp.dot(patches[parity, start : start + chunk], weights[...], preferred_element_type=F32)
+            active = half * gelu_parts(half)[1]
+            sums = active if sums is None else sums + active
+        out[start : start + chunk, :] = (sums * 0.5).astype(BF16)
+
+
+def loss_kernel(groups, share, full_len, listed, ready, scalars, arrived, projection, *refs):
+    pieces, (loss, out, grad) = refs[:share], refs[share:]
     branch, grp_pos = scalars[1], scalars[2]
     batch = share
-    exact = lax.Precision.HIGHEST
     latents = []
     for side in range(2):
         lines = []
         for item in range(batch):
             base = (side * share + item) * groups
-            line = arrived[base, 0:1, :]
-            for turn in range(1, groups):
-                line = line + arrived[base + turn, 0:1, :]
-            lines.append(line * (1.0 / full_len))
+            lines.append(jnp.sum(arrived[base : base + groups, 0:1, :], axis=0) * (1.0 / full_len))
         latents.append(jnp.concatenate(lines, axis=0))
     scale = [lax.rsqrt(jnp.sum(latent * latent, axis=1, keepdims=True) + 1e-06) for latent in latents]
     embs = [latent * factor for latent, factor in zip(latents, scale)]
-    logits = lax.dot_general(embs[0], embs[1], (((1,), (1,)), ((), ())), precision=exact, preferred_element_type=F32) / TAU
-    row = lax.broadcasted_iota(jnp.int32, logits.shape, 0)
-    col = lax.broadcasted_iota(jnp.int32, logits.shape, 1)
-    target = jnp.zeros_like(logits)
+    row = lax.broadcasted_iota(jnp.int32, (batch, LANES), 0)
+    lane = lax.broadcasted_iota(jnp.int32, (batch, LANES), 1)
+    logits = jnp.zeros((batch, LANES), F32)
+    target = jnp.zeros((batch, LANES), F32)
     for item in range(batch):
-        target = jnp.where((row == item) & (col == scalars[3 + 2 * listed + item]), 1.0, target)
-    power = jnp.exp(logits)
+        column = jnp.sum(embs[0] * embs[1][item : item + 1], axis=1, keepdims=True) / TAU
+        logits = jnp.where(lane == item, column, logits)
+        target = jnp.where((row == item) & (lane == scalars[3 + 2 * listed + item]), 1.0, target)
+    inside = lane < batch
+    power = jnp.where(inside, jnp.exp(logits), 0.0)
     row_sum = jnp.sum(power, axis=1, keepdims=True)
-    col_sum = jnp.sum(power, axis=0, keepdims=True)
-    value = (
-        jnp.sum(jnp.log(row_sum), axis=(0, 1), keepdims=True)
-        + jnp.sum(jnp.log(col_sum), axis=(0, 1), keepdims=True)
-        - 2.0 * jnp.sum(target * logits, axis=(0, 1), keepdims=True)
-    ) / (2.0 * batch)
-    loss[0, 0] = jnp.sum(value)
+    col_sum = jnp.where(inside[0:1], jnp.sum(power, axis=0, keepdims=True), 1.0)
+    value = jnp.log(col_sum) + jnp.sum(
+        jnp.where(lane == 0, jnp.log(row_sum), 0.0) - 2.0 * target * logits, axis=0, keepdims=True
+    )
+    loss[0, 0] = jnp.sum(value) / (2.0 * batch)
     slope = (power / row_sum + power / col_sum - 2.0 * target) * (LOSS_SCALE / (2.0 * batch * TAU))
-    emb_grads = [
-        lax.dot_general(slope, embs[1], (((1,), (0,)), ((), ())), precision=exact, preferred_element_type=F32),
-        lax.dot_general(slope.T, embs[0], (((1,), (0,)), ((), ())), precision=exact, preferred_element_type=F32),
-    ]
+    emb_grads = [jnp.zeros((batch, LANES), F32), []]
+    for item in range(batch):
+        column = slope[:, item : item + 1]
+        emb_grads[0] = emb_grads[0] + column * embs[1][item : item + 1]
+        emb_grads[1].append(jnp.sum(column * embs[0], axis=0, keepdims=True))
+    emb_grads[1] = jnp.concatenate(emb_grads[1], axis=0)
     own = []
     for side in range(2):
         inner = jnp.sum(emb_grads[side] * embs[side], axis=1, keepdims=True)
         own.append(scale[side] * (emb_grads[side] - embs[side] * inner))
-    latent_grad = jnp.where(branch == 0, own[0], own[1])
-    rows = factors.shape[0]
+    latent_grad = jnp.where(branch == 0, own[0], own[1]) * (1.0 / full_len)
+    rows = out.shape[0]
     if ready:
         weights = projection[...].astype(F32)
     else:
         start = pl.multiple_of((grp_pos * groups + scalars[0]) * rows, 16)
         weights = projection[pl.ds(start, rows), :].astype(F32)
+    spread = jnp.zeros((rows, LANES), F32)
     lane = lax.broadcasted_iota(jnp.int32, (rows, LANES), 1)
-    spread = jnp.zeros((rows, LANES), F32)
     for item in range(batch):
-        column = jnp.sum(weights * latent_grad[item : item + 1, :], axis=1, keepdims=True) * (1.0 / full_len)
+        column = jnp.sum(weights * latent_grad[item : item + 1, :], axis=1, keepdims=True)
         spread = jnp.where(lane == item, column, spread)
-    factors[...] = spread
     for turn in range(groups):
         lines = [arrived[(branch * share + item) * groups + turn, 1:2, :] for item in range(batch)]
-        lines = lines + [jnp.zeros((8 - batch % 8, LANES), F32)] if batch % 8 else lines
-        sums = jnp.concatenate(lines, axis=0).T * (1.0 / full_len)
+        if batch % 8:
+            lines.append(jnp.zeros((8 - batch % 8, LANES), F32))
+        sums = jnp.concatenate(lines, axis=0).T
         value = sums[:, 0:1] * latent_grad[0:1, :]
         for item in range(1, batch):
             value = value + sums[:, item : item + 1] * latent_grad[item : item + 1, :]
         grad[turn * rows : (turn + 1) * rows, :] = value[:rows]
-
-
-def combine_kernel(share, scalars, factors, *refs):
-    pieces, out = refs[:share], refs[share]
-    grp_pos = scalars[2]
-    values = factors[...]
-    lane = lax.broadcasted_iota(jnp.int32, values.shape, 1)
     result = None
     for turn in range(share):
-        column = jnp.sum(jnp.where(lane == (grp_pos ^ turn), values, 0.0), axis=1, keepdims=True)
+        column = jnp.sum(jnp.where(lane == (grp_pos ^ turn), spread, 0.0), axis=1, keepdims=True)
         term = column * pieces[turn][...]
         result = term if result is None else result + term
     out[...] = result
@@ -419,29 +420,41 @@
 
     piece = jax.ShapeDtypeStruct((chans, length), F32)
     with jax.named_scope("arrange"):
-        pieces = call(arrange_kernel, [piece] * groups, [SMEM, VMEM], moved=5 * 10**5)(
-            scalars, series[0].T.reshape(groups, chans, length)
-        )
+        pieces = call(
+            arrange_kernel,
+            [piece] * groups,
+            [HBM],
+            [pltpu.SemaphoreType.DMA((groups,))],
+            moved=5 * 10**5,
+        )(series[0].T.reshape(groups, chans, length))
     pieces = [pieces[0]] + [
         lax.ppermute(pieces[turn], "seq", [(i, i ^ turn) for i in range(groups)]) for turn in range(1, groups)
     ]
-    tables = [jnp.asarray(table) for table in fourier_tables(full_len)]
+    table = jnp.asarray(fourier_tables(full_len))
     with jax.named_scope("prepare"):
-        weights, part_weights, *tables = call(
-            functools.partial(prepare_kernel, groups, share, ready),
-            [jax.ShapeDtypeStruct((width, hidden), BF16), jax.ShapeDtypeStruct((width, share * rows), BF16)]
-            + [jax.ShapeDtypeStruct(table.shape, table.dtype) for table in tables],
-            [SMEM] + [VMEM] * 6,
+        kernel = functools.partial(prepare_kernel, groups, share, low_count)
+        if not ready:
+            kernel = functools.partial(prepare_whole, kernel)
+        weights, part_weights, stage_one, turns, stage_two = call(
+            kernel,
+            [
+                jax.ShapeDtypeStruct((width, hidden), BF16),
+                jax.ShapeDtypeStruct((width, share * rows), BF16),
+                jax.ShapeDtypeStruct((2 * low_count, 3 * low_count), BF16),
+                jax.ShapeDtypeStruct((low_count, 2 * LANES), F32),
+                jax.ShapeDtypeStruct((6 * LANES, 2 * LANES), BF16),
+            ],
+            [SMEM] + [VMEM] * (3 if ready else 2),
             flops=10**8,
             moved=3 * 10**6,
             room=24,
-        )(scalars, weight, picked, *tables)
+        )(*([scalars, weight, picked, table] if ready else [scalars, weight, table]))
     wire = jax.ShapeDtypeStruct((chans * low_count, LANES), BF16)
     with jax.named_scope("fourier"):
         own, pay = call(
             functools.partial(fourier_kernel, groups, full_len, length // 8, listed),
             [wire, wire],
-            [SMEM] + [VMEM] * (4 + groups),
+            [SMEM] + [VMEM] * (3 + groups),
             [
                 pltpu.VMEM((groups, chans, length), F32),
                 pltpu.VMEM((chans * low_count, LANES), F32),
@@ -451,11 +464,11 @@
             ],
             flops=10**9,
             moved=2 * 10**6,
-        )(scalars, *tables, *pieces)
+        )(scalars, stage_one, turns, stage_two, *pieces)
 
     slots = [None] * (2 * groups)
-    for flip in range(2):
-        for turn in range(0, groups, 2):
+    for flip in (1, 0):
+        for turn in range(groups - 2, -1, -2):
             block = pay if flip else own
             if flip or turn:
                 pairs = [
@@ -475,9 +488,9 @@
     tiles = jax.ShapeDtypeStruct((lows + 4, LANES, LANES), BF16)
     with jax.named_scope("slope"):
         *grads, payload, flat = call(
-            functools.partial(slope_kernel, groups, ready, 8),
+            functools.partial(slope_kernel, groups, ready, 32, 4),
             [jax.ShapeDtypeStruct((rows, width), F32)] * share
-            + [jax.ShapeDtypeStruct((devices, 8, LANES), F32), tiles],
+            + [jax.ShapeDtypeStruct((devices, 2, LANES), F32), tiles],
             [SMEM] + [VMEM] * (2 + len(slots)),
             [
                 pltpu.VMEM((lows + 4, LANES, LANES), BF16),
@@ -493,18 +506,18 @@
         lax.ppermute(grads[turn], "grp", [(i, i ^ turn) for i in range(share)]) for turn in range(1, share)
     ]
     arrived = lax.all_to_all(payload, ("pair", "grp", "seq"), split_axis=0, concat_axis=0, tiled=True)
-    enc_tile = 256
-    near_len = length // 2
+    near_len, columns = length // 2, 512
     with jax.named_scope("encode"):
         encoded = pl.pallas_call(
-            functools.partial(encode_kernel, groups),
+            functools.partial(encode_kernel, groups, 256),
             out_shape=jax.ShapeDtypeStruct((near_len, hidden), BF16),
-            grid=(near_len // enc_tile,),
-            in_specs=[SMEM, VMEM, VMEM],
-            out_specs=pl.BlockSpec((enc_tile, hidden), lambda i: (i, 0)),
+            grid=(hidden // columns,),
+            in_specs=[SMEM, VMEM, pl.BlockSpec((width, columns), lambda i: (0, i))],
+            out_specs=pl.BlockSpec((near_len, columns), lambda i: (0, i)),
             scratch_shapes=[
                 pltpu.VMEM(((lows + 4) * LANES, LANES), F32),
                 pltpu.VMEM((near_len + 24, LANES), F32),
+                pltpu.VMEM((2, near_len, width), BF16),
             ],
             compiler_params=pltpu.CompilerParams(vmem_limit_bytes=(20 + 12 * (low_count // LANES)) * 1024 * 1024),
             cost_estimate=pl.CostEstimate(
@@ -512,26 +525,18 @@
             ),
         )(scalars, flat, weights)
     with jax.named_scope("loss"):
-        loss, factors, proj_share = call(
+        loss, conv_share, proj_share = call(
             functools.partial(loss_kernel, groups, share, full_len, listed, ready),
             [
                 jax.ShapeDtypeStruct((1, 1), F32),
-                jax.ShapeDtypeStruct((rows, LANES), F32),
+                jax.ShapeDtypeStruct((rows, width), F32),
                 jax.ShapeDtypeStruct((groups * rows, emb_dim), F32),
             ],
-            [SMEM] + [VMEM] * 2,
+            [SMEM] + [VMEM] * (2 + share),
             flops=10**7,
             moved=10**6,
             out_specs=[SMEM, VMEM, VMEM],
-        )(scalars, arrived, own_heads)
-    with jax.named_scope("combine"):
-        conv_share = call(
-            functools.partial(combine_kernel, share),
-            jax.ShapeDtypeStruct((rows, width), F32),
-            [SMEM] + [VMEM] * (1 + share),
-            flops=10**6,
-            moved=5 * 10**5,
-        )(scalars, factors, *grads)
+        )(scalars, arrived, own_heads, *grads)
     return (encoded[None, None], loss.reshape(()), conv_share[None], proj_share[None])
 
 

time: 57.6 us -> 49.6 us (0.86)
  Pallas kernels: 23.7 us -> 17.5 us
  local copies, waits for them, and re-layouts: 6.3 us -> 3.96 us
    pallas_call x5 -> x4, Pallas kernels: 20.2 us -> 14.1 us  [the longest x1 6.91 us: body(): call(functools.partial(slope_kernel, groups, ready, 32, 4), [jax.ShapeDty...]
    all_to_all x1, waiting for transfers between devices: 0.01 us -> 2.75 us  [body(): lax.all_to_all(payload, ('pair', 'grp', 'seq'), split_axis=0, concat_axis...]
    unnamed x14 -> x8, local copies, waits for them, and re-layouts: 5.53 us -> 3.19 us
    ppermute x3, waiting for transfers between devices: 2.31 us -> 0.01 us  [body(): lax.ppermute(grads[turn], 'grp', [(i, i ^ turn) for i in range(share)])]
  transfers between devices with their start and end apart: 14 -> 14, of which waited for: 5 -> 5; matrix products, arithmetic and copies ran while one was open for 0% -> 2% of each run, Pallas kernels for 17% -> 14%
where the time goes in v2:
time: 49.6 us; the launch traced here: 49.4 us
  Pallas kernels  17.5 us (35%)
  starting transfers between devices  16.7 us (34%)
  waiting for transfers between devices  10.3 us (21%)
  local copies, waits for them, and re-layouts  3.96 us (8%)
  between operations  0.88 us (2%)
    pallas_call x1, Pallas kernels, body(): call(functools.partial(slope_kernel, groups, ready, 32, 4), [jax.ShapeDty...  6.91 us
    ppermute x3, waiting for transfers between devices, body(): block = lax.ppermute(block, ('pair', 'seq'), pairs)  6.51 us
    pallas_call x1, Pallas kernels, body(): pl.pallas_call(functools.partial(encode_kernel, groups, 256), out_shape=j...  5.8 us
    all_to_all x1, starting transfers between devices, body(): lax.all_to_all(payload, ('pair', 'grp', 'seq'), split_axis=0, concat_axis...  5.11 us
    ppermute x3, starting transfers between devices, body(): lax.ppermute(grads[turn], 'grp', [(i, i ^ turn) for i in range(share)])  4.39 us
    ppermute x3, starting transfers between devices, body(): block = lax.ppermute(block, ('pair', 'seq'), pairs)  3.55 us
    unnamed x8, local copies, waits for them, and re-layouts  3.19 us
    ppermute x3, starting transfers between devices, body(): lax.ppermute(pieces[turn], 'seq', [(i, i ^ turn) for i in range(groups)])  3.15 us
  transfers between devices with their start and end apart: 14, of which 5 were waited for; matrix products, arithmetic and copies ran while one was open for 2% of the time, Pallas kernels for 14%

profile of v2, /device:TPU:0, one launch (start us, length us, event | category | flops | bytes accessed | tf_op | source)
XLA Modules:
  0.0 49.4 jit_solution(8406385723446155126)
XLA Ops:
  0.6 0.0 copy-start.2
  0.6 0.9 %copy-done.2 = f32[1,2048,32]{1,2,0:T(8,128)S(1)} copy-done((f32[1,2048,32]{1,2,0:T(8,128)S(1)}, f32[1,2048,32]{1,2,0:T(8,128)}, u32[]{:S(2)}) %copy-start.2) | copy-done | bytes 262168
  1.6 0.3 arrange.1
  1.9 0.5 %collective-permute-start = (f32[8,2048]{1,0:T(8,128)S(1)}, f32[8,2048]{1,0:T(8,128)S(1)}, u32[]{:S(2)}, u32[]{:S(2)}) collective-permute-start(f32[8,2048]{1,0:T(8,128)S(1)} %get-tuple-element.29), channel_id=1, source_target_pairs={{0,1},{1,0},{2,3},{3,2},{4,5},{5,4},{6,7},{7,6},{8,9},{9,8},{10,11... | collective-permute-start | bytes 196616 | tf_op jit(solution)/shard_map/ppermute | solution.py:431
  2.5 2.6 %collective-permute-start.1 = (f32[8,2048]{1,0:T(8,128)S(1)}, f32[8,2048]{1,0:T(8,128)S(1)}, u32[]{:S(2)}, u32[]{:S(2)}) collective-permute-start(f32[8,2048]{1,0:T(8,128)S(1)} %get-tuple-element.30), channel_id=1, source_target_pairs={{0,2},{1,3},{2,0},{3,1},{4,6},{5,7},{6,4},{7,5},{8,10},{9,11},{10,... | collective-permute-start | bytes 196616 | tf_op jit(solution)/shard_map/ppermute | solution.py:431
  5.0 0.1 collective-permute-start.2
  5.1 0.8 %concatenate.3.scalars = s32[15]{0:T(128)S(1)} concatenate(s32[1]{0:T(128)} %bitcast, s32[1]{0:T(128)} %bitcast.1, s32[1]{0:T(128)} %bitcast.2, s32[4]{0:T(128)} %bitcast.20, s32[4]{0:T(128)} %bitcast.21, s32[4]{0:T(128)} %param.10), dimensions={0} | concatenate | bytes 120 | tf_op jit(solution)/shard_map/concatenate | solution.py:411
  5.9 0.0 copy-start
  5.9 1.2 %copy-done = bf16[1,1024,512]{2,1,0:T(8,128)(2,1)S(1)} copy-done((bf16[1,1024,512]{2,1,0:T(8,128)(2,1)S(1)}, bf16[1,1024,512]{2,1,0:T(8,128)(2,1)}, u32[]{:S(2)}) %copy-start) | copy-done | bytes 1048600
  7.1 0.0 copy-start.1
  7.1 1.0 %copy-done.1 = f32[448,256]{1,0:T(8,128)S(1)} copy-done((f32[448,256]{1,0:T(8,128)S(1)}, f32[448,256]{1,0:T(8,128)}, u32[]{:S(2)}) %copy-start.1) | copy-done | bytes 458776
  8.1 1.0 %prepare.1 = (bf16[512,1024]{1,0:T(8,128)(2,1)S(1)}, bf16[512,256]{1,0:T(8,128)(2,1)S(1)}, bf16[128,192]{1,0:T(8,128)(2,1)S(1)}, f32[64,256]{1,0:T(8,128)S(1)}, bf16[768,256]{1,0:T(8,128)(2,1)S(1)}) custom-call(s32[15]{0:T(128)S(1)} %concatenate.3.scalars, bf16[1024,512]{1,0:T(8,128)(2,1)S(1)} %bitcast.16, f32[448,256]{1,0:T(8,128)S(1)} %copy-done.1), custom_call_target="tpu_custom_call" | custom-call | flops 100000000 | bytes 3000000 | tf_op jit(solution)/shard_map/prepare/pallas_call | solution.py:438
  9.1 0.0 copy-start.3
  9.2 0.0 collective-permute-done.refs_1_
  9.2 0.0 collective-permute-done.1.refs_2_
  9.2 0.0 collective-permute-done.2.refs_3_
  9.2 1.4 %fourier.1 = (bf16[512,128]{1,0:T(8,128)(2,1)S(1)}, bf16[512,128]{1,0:T(8,128)(2,1)S(1)}) custom-call(s32[15]{0:T(128)S(1)} %concatenate.3.scalars, bf16[128,192]{1,0:T(8,128)(2,1)S(1)} %get-tuple-element.25.stage_one, f32[64,256]{1,0:T(8,128)S(1)} %get-tuple-element.26.turns, bf16[768,256]{1,0:T(8,128)(2,1)S(1)} %get-tuple-element.27.stage_two, ...), custom_call_target="tpu_custom_call" | custom-call | flops 1000000000 | bytes 2000000 | tf_op jit(solution)/shard_map/fourier/pallas_call | solution.py:454
  10.6 1.8 %collective-permute-start.4 = (bf16[512,128]{1,0:T(8,128)(2,1)S(1)}, bf16[512,128]{1,0:T(8,128)(2,1)S(1)}, u32[]{:S(2)}, u32[]{:S(2)}) collective-permute-start(bf16[512,128]{1,0:T(8,128)(2,1)S(1)} %get-tuple-element.32.refs_0_), channel_id=1, source_target_pairs={{0,2},{1,3},{2,0},{3,1},{16,18},{17,19},{18,16},{19,17},{4,6},{5,7... | collective-permute-start | bytes 393224 | tf_op jit(solution)/shard_map/ppermute | solution.py:477
  12.4 1.5 %collective-permute-start.6 = (bf16[512,128]{1,0:T(8,128)(2,1)S(1)}, bf16[512,128]{1,0:T(8,128)(2,1)S(1)}, u32[]{:S(2)}, u32[]{:S(2)}) collective-permute-start(bf16[512,128]{1,0:T(8,128)(2,1)S(1)} %get-tuple-element.33), channel_id=1, source_target_pairs={{0,16},{1,17},{2,18},{3,19},{16,0},{17,1},{18,2},{19,3},{4,20},{5,... | collective-permute-start | bytes 393224 | tf_op jit(solution)/shard_map/ppermute | solution.py:477
  14.0 0.2 collective-permute-start.8
  14.2 0.0 collective-permute-start.3
  14.2 2.3 %collective-permute-done.4.refs_2_ = bf16[512,128]{1,0:T(8,128)(2,1)S(1)} collective-permute-done((bf16[512,128]{1,0:T(8,128)(2,1)S(1)}, bf16[512,128]{1,0:T(8,128)(2,1)S(1)}, u32[]{:S(2)}, u32[]{:S(2)}) %collective-permute-start.4) | collective-permute-done | bytes 131104 | tf_op jit(solution)/shard_map/ppermute | solution.py:477
  16.5 0.0 collective-permute-start.5
  16.5 4.2 %collective-permute-done.6.refs_4_ = bf16[512,128]{1,0:T(8,128)(2,1)S(1)} collective-permute-done((bf16[512,128]{1,0:T(8,128)(2,1)S(1)}, bf16[512,128]{1,0:T(8,128)(2,1)S(1)}, u32[]{:S(2)}, u32[]{:S(2)}) %collective-permute-start.6) | collective-permute-done | bytes 131104 | tf_op jit(solution)/shard_map/ppermute | solution.py:477
  20.7 0.0 collective-permute-start.7
  20.7 0.0 collective-permute-done.8.refs_6_
  20.7 0.5 %collective-permute-start.9 = (bf16[512,128]{1,0:T(8,128)(2,1)S(1)}, bf16[512,128]{1,0:T(8,128)(2,1)S(1)}, u32[]{:S(2)}, u32[]{:S(2)}) collective-permute-start(bf16[512,128]{1,0:T(8,128)(2,1)S(1)} %collective-permute-done.8.refs_6_), channel_id=1, source_target_pairs={{0,1},{1,0},{2,3},{3,2},{4,5},{5,4},{6,7},{7,6},{8,9},{9,8},{10,11... | collective-permute-start | bytes 393224 | tf_op jit(solution)/shard_map/ppermute | solution.py:481
  21.2 0.0 collective-permute-done.3.refs_1_
  21.2 0.0 collective-permute-done.5.refs_3_
  21.2 0.8 %collective-permute-done.7.refs_5_ = bf16[512,128]{1,0:T(8,128)(2,1)S(1)} collective-permute-done((bf16[512,128]{1,0:T(8,128)(2,1)S(1)}, bf16[512,128]{1,0:T(8,128)(2,1)S(1)}, u32[]{:S(2)}, u32[]{:S(2)}) %collective-permute-start.7) | collective-permute-done | bytes 131104 | tf_op jit(solution)/shard_map/ppermute | solution.py:481
  22.1 0.2 collective-permute-done.9.refs_7_
  22.2 0.0 copy-done.3
  22.2 6.9 %slope.1 = (f32[64,512]{1,0:T(8,128)S(1)}, f32[64,512]{1,0:T(8,128)S(1)}, f32[64,512]{1,0:T(8,128)S(1)}, f32[64,512]{1,0:T(8,128)S(1)}, f32[32,2,128]{2,1,0:T(2,128)}, /*index=5*/bf16[36,128,128]{2,1,0:T(8,128)(2,1)S(1)}) custom-call(s32[15]{0:T(128)S(1)} %concatenate.3.scalars, bf16[512,256]{1,0:T(8,128)(2,1)S(1)} %get-tuple-element.24.weights, ...), custom_call_target="tpu_custom_call" | custom-call | flops 4294967296 | bytes 4000000 | tf_op jit(solution)/shard_map/slope/pallas_call | solution.py:490
  29.2 1.6 %collective-permute-start.10 = (f32[64,512]{1,0:T(8,128)S(1)}, f32[64,512]{1,0:T(8,128)S(1)}, u32[]{:S(2)}, u32[]{:S(2)}) collective-permute-start(f32[64,512]{1,0:T(8,128)S(1)} %get-tuple-element.38), channel_id=1, source_target_pairs={{0,4},{4,0},{8,12},{12,8},{1,5},{5,1},{9,13},{13,9},{2,6},{6,2},{1... | collective-permute-start | bytes 393224 | tf_op jit(solution)/shard_map/ppermute | solution.py:506
  30.7 2.6 %collective-permute-start.11 = (f32[64,512]{1,0:T(8,128)S(1)}, f32[64,512]{1,0:T(8,128)S(1)}, u32[]{:S(2)}, u32[]{:S(2)}) collective-permute-start(f32[64,512]{1,0:T(8,128)S(1)} %get-tuple-element.39), channel_id=1, source_target_pairs={{0,8},{4,12},{8,0},{12,4},{1,9},{5,13},{9,1},{13,5},{2,10},{6,14},... | collective-permute-start | bytes 393224 | tf_op jit(solution)/shard_map/ppermute | solution.py:506
  33.3 0.2 collective-permute-start.12
  33.5 5.1 %all-to-all-start = ((f32[32,2,128]{2,1,0:T(2,128)}), f32[32,2,128]{2,1,0:T(2,128)S(1)}, u32[]{:S(2)}, u32[]{:S(2)}) async-start(f32[32,2,128]{2,1,0:T(2,128)} %get-tuple-element.36), calls=%async_computation | async-start | bytes 65536 | tf_op jit(solution)/shard_map/all_to_all | solution.py:508
  38.7 5.8 %encode.1 = bf16[1024,1024]{1,0:T(8,128)(2,1)} custom-call(s32[15]{0:T(128)S(1)} %concatenate.3.scalars, bf16[36,128,128]{2,1,0:T(8,128)(2,1)S(1)} %get-tuple-element.34.flat, bf16[512,1024]{1,0:T(8,128)(2,1)S(1)} %get-tuple-element.35.weights), custom_call_target="tpu_custom_call" | custom-call | flops 2147483648 | bytes 4000000 | tf_op jit(solution)/shard_map/encode/pallas_call | solution.py:511
  44.5 2.8 %all-to-all-done.arrived = f32[32,2,128]{2,1,0:T(2,128)S(1)} async-done(((f32[32,2,128]{2,1,0:T(2,128)}), f32[32,2,128]{2,1,0:T(2,128)S(1)}, u32[]{:S(2)}, u32[]{:S(2)}) %all-to-all-start) | async-done | bytes 32800 | tf_op jit(solution)/shard_map/all_to_all | solution.py:508
  47.2 0.0 collective-permute-done.10.refs_1_
  47.2 0.0 collective-permute-done.11.refs_2_
  47.2 0.0 collective-permute-done.12.refs_3_
  47.2 2.0 %loss.1 = (f32[1,1]{1,0:T(1,128)}, f32[64,512]{1,0:T(8,128)}, f32[256,128]{1,0:T(8,128)}) custom-call(s32[15]{0:T(128)S(1)} %concatenate.3.scalars, f32[32,2,128]{2,1,0:T(2,128)S(1)} %all-to-all-done.arrived, bf16[1024,128]{1,0:T(8,128)(2,1)S(1)} %bitcast.19, f32[64,512]{1,0:T(8,128)S(1)} %get-tuple-element.37.refs_0_, ...), custom_call_target="tpu_custom_call" | custom-call | flops 10000000 | bytes 1000000 | tf_op jit(solution)/shard_map/loss/pallas_call | solution.py:528
Async XLA Ops:
  0.6 1.0 %copy-start.2 = (f32[1,2048,32]{1,2,0:T(8,128)S(1)}, f32[1,2048,32]{1,2,0:T(8,128)}, u32[]{:S(2)}) copy-start(f32[1,2048,32]{1,2,0:T(8,128)} %param.7) | copy-start | bytes 786436
  1.9 7.2 %collective-permute-start = (f32[8,2048]{1,0:T(8,128)S(1)}, f32[8,2048]{1,0:T(8,128)S(1)}, u32[]{:S(2)}, u32[]{:S(2)}) collective-permute-start(f32[8,2048]{1,0:T(8,128)S(1)} %get-tuple-element.29), channel_id=1, source_target_pairs={{0,1},{1,0},{2,3},{3,2},{4,5},{5,4},{6,7},{7,6},{8,9},{9,8},{10,11... | collective-permute-start | bytes 196616 | tf_op jit(solution)/shard_map/ppermute | solution.py:431
  2.5 6.7 %collective-permute-start.1 = (f32[8,2048]{1,0:T(8,128)S(1)}, f32[8,2048]{1,0:T(8,128)S(1)}, u32[]{:S(2)}, u32[]{:S(2)}) collective-permute-start(f32[8,2048]{1,0:T(8,128)S(1)} %get-tuple-element.30), channel_id=1, source_target_pairs={{0,2},{1,3},{2,0},{3,1},{4,6},{5,7},{6,4},{7,5},{8,10},{9,11},{10,... | collective-permute-start | bytes 196616 | tf_op jit(solution)/shard_map/ppermute | solution.py:431
  5.0 4.2 %collective-permute-start.2 = (f32[8,2048]{1,0:T(8,128)S(1)}, f32[8,2048]{1,0:T(8,128)S(1)}, u32[]{:S(2)}, u32[]{:S(2)}) collective-permute-start(f32[8,2048]{1,0:T(8,128)S(1)} %get-tuple-element.31), channel_id=1, source_target_pairs={{0,3},{1,2},{2,1},{3,0},{4,7},{5,6},{6,5},{7,4},{8,11},{9,10},{10,... | collective-permute-start | bytes 196616 | tf_op jit(solution)/shard_map/ppermute | solution.py:431
  5.9 1.2 %copy-start = (bf16[1,1024,512]{2,1,0:T(8,128)(2,1)S(1)}, bf16[1,1024,512]{2,1,0:T(8,128)(2,1)}, u32[]{:S(2)}) copy-start(bf16[1,1024,512]{2,1,0:T(8,128)(2,1)} %param.11) | copy-start | bytes 3145732
  7.1 1.0 %copy-start.1 = (f32[448,256]{1,0:T(8,128)S(1)}, f32[448,256]{1,0:T(8,128)}, u32[]{:S(2)}) copy-start(f32[448,256]{1,0:T(8,128)} %constant.15.clone.refs_0_) | copy-start | bytes 1376260
  9.1 13.1 %copy-start.3 = (bf16[1,1024,128]{2,1,0:T(8,128)(2,1)S(1)}, bf16[1,1024,128]{2,1,0:T(8,128)(2,1)}, u32[]{:S(2)}) copy-start(bf16[1,1024,128]{2,1,0:T(8,128)(2,1)} %param.12) | copy-start | bytes 786436
  10.6 5.9 %collective-permute-start.4 = (bf16[512,128]{1,0:T(8,128)(2,1)S(1)}, bf16[512,128]{1,0:T(8,128)(2,1)S(1)}, u32[]{:S(2)}, u32[]{:S(2)}) collective-permute-start(bf16[512,128]{1,0:T(8,128)(2,1)S(1)} %get-tuple-element.32.refs_0_), channel_id=1, source_target_pairs={{0,2},{1,3},{2,0},{3,1},{16,18},{17,19},{18,16},{19,17},{4,6},{5,7... | collective-permute-start | bytes 393224 | tf_op jit(solution)/shard_map/ppermute | solution.py:477
  12.4 8.3 %collective-permute-start.6 = (bf16[512,128]{1,0:T(8,128)(2,1)S(1)}, bf16[512,128]{1,0:T(8,128)(2,1)S(1)}, u32[]{:S(2)}, u32[]{:S(2)}) collective-permute-start(bf16[512,128]{1,0:T(8,128)(2,1)S(1)} %get-tuple-element.33), channel_id=1, source_target_pairs={{0,16},{1,17},{2,18},{3,19},{16,0},{17,1},{18,2},{19,3},{4,20},{5,... | collective-permute-start | bytes 393224 | tf_op jit(solution)/shard_map/ppermute | solution.py:477
  14.0 6.8 %collective-permute-start.8 = (bf16[512,128]{1,0:T(8,128)(2,1)S(1)}, bf16[512,128]{1,0:T(8,128)(2,1)S(1)}, u32[]{:S(2)}, u32[]{:S(2)}) collective-permute-start(bf16[512,128]{1,0:T(8,128)(2,1)S(1)} %get-tuple-element.33), channel_id=1, source_target_pairs={{0,18},{1,19},{2,16},{3,17},{16,2},{17,3},{18,0},{19,1},{4,22},{5,... | collective-permute-start | bytes 393224 | tf_op jit(solution)/shard_map/ppermute | solution.py:477
  14.2 7.0 %collective-permute-start.3 = (bf16[512,128]{1,0:T(8,128)(2,1)S(1)}, bf16[512,128]{1,0:T(8,128)(2,1)S(1)}, u32[]{:S(2)}, u32[]{:S(2)}) collective-permute-start(bf16[512,128]{1,0:T(8,128)(2,1)S(1)} %get-tuple-element.32.refs_0_), channel_id=1, source_target_pairs={{0,1},{1,0},{2,3},{3,2},{4,5},{5,4},{6,7},{7,6},{8,9},{9,8},{10,11... | collective-permute-start | bytes 393224 | tf_op jit(solution)/shard_map/ppermute | solution.py:481
  16.5 4.7 %collective-permute-start.5 = (bf16[512,128]{1,0:T(8,128)(2,1)S(1)}, bf16[512,128]{1,0:T(8,128)(2,1)S(1)}, u32[]{:S(2)}, u32[]{:S(2)}) collective-permute-start(bf16[512,128]{1,0:T(8,128)(2,1)S(1)} %collective-permute-done.4.refs_2_), channel_id=1, source_target_pairs={{0,1},{1,0},{2,3},{3,2},{4,5},{5,4},{6,7},{7,6},{8,9},{9,8},{10,11... | collective-permute-start | bytes 393224 | tf_op jit(solution)/shard_map/ppermute | solution.py:481
  20.7 1.3 %collective-permute-start.7 = (bf16[512,128]{1,0:T(8,128)(2,1)S(1)}, bf16[512,128]{1,0:T(8,128)(2,1)S(1)}, u32[]{:S(2)}, u32[]{:S(2)}) collective-permute-start(bf16[512,128]{1,0:T(8,128)(2,1)S(1)} %collective-permute-done.6.refs_4_), channel_id=1, source_target_pairs={{0,1},{1,0},{2,3},{3,2},{4,5},{5,4},{6,7},{7,6},{8,9},{9,8},{10,11... | collective-permute-start | bytes 393224 | tf_op jit(solution)/shard_map/ppermute | solution.py:481
  20.7 1.5 %collective-permute-start.9 = (bf16[512,128]{1,0:T(8,128)(2,1)S(1)}, bf16[512,128]{1,0:T(8,128)(2,1)S(1)}, u32[]{:S(2)}, u32[]{:S(2)}) collective-permute-start(bf16[512,128]{1,0:T(8,128)(2,1)S(1)} %collective-permute-done.8.refs_6_), channel_id=1, source_target_pairs={{0,1},{1,0},{2,3},{3,2},{4,5},{5,4},{6,7},{7,6},{8,9},{9,8},{10,11... | collective-permute-start | bytes 393224 | tf_op jit(solution)/shard_map/ppermute | solution.py:481
  29.2 18.1 %collective-permute-start.10 = (f32[64,512]{1,0:T(8,128)S(1)}, f32[64,512]{1,0:T(8,128)S(1)}, u32[]{:S(2)}, u32[]{:S(2)}) collective-permute-start(f32[64,512]{1,0:T(8,128)S(1)} %get-tuple-element.38), channel_id=1, source_target_pairs={{0,4},{4,0},{8,12},{12,8},{1,5},{5,1},{9,13},{13,9},{2,6},{6,2},{1... | collective-permute-start | bytes 393224 | tf_op jit(solution)/shard_map/ppermute | solution.py:506
  30.7 16.5 %collective-permute-start.11 = (f32[64,512]{1,0:T(8,128)S(1)}, f32[64,512]{1,0:T(8,128)S(1)}, u32[]{:S(2)}, u32[]{:S(2)}) collective-permute-start(f32[64,512]{1,0:T(8,128)S(1)} %get-tuple-element.39), channel_id=1, source_target_pairs={{0,8},{4,12},{8,0},{12,4},{1,9},{5,13},{9,1},{13,5},{2,10},{6,14},... | collective-permute-start | bytes 393224 | tf_op jit(solution)/shard_map/ppermute | solution.py:506
  33.3 13.9 %collective-permute-start.12 = (f32[64,512]{1,0:T(8,128)S(1)}, f32[64,512]{1,0:T(8,128)S(1)}, u32[]{:S(2)}, u32[]{:S(2)}) collective-permute-start(f32[64,512]{1,0:T(8,128)S(1)} %get-tuple-element.40), channel_id=1, source_target_pairs={{0,12},{4,8},{8,4},{12,0},{1,13},{5,9},{9,5},{13,1},{2,14},{6,10},... | collective-permute-start | bytes 393224 | tf_op jit(solution)/shard_map/ppermute | solution.py:506
  33.5 13.7 %all-to-all-start = ((f32[32,2,128]{2,1,0:T(2,128)}), f32[32,2,128]{2,1,0:T(2,128)S(1)}, u32[]{:S(2)}, u32[]{:S(2)}) async-start(f32[32,2,128]{2,1,0:T(2,128)} %get-tuple-element.36), calls=%async_computation | async-start | bytes 65536 | tf_op jit(solution)/shard_map/all_to_all | solution.py:508

commit v3 on v2

--- a/solution.py
+++ b/solution.py
@@ -133,7 +133,9 @@
     def spread(held, out):
         for low in range(low_count):
             wire[chans * low : chans * (low + 1), :] = held[pl.ds(low, chans, stride=low_count), :]
-        out[...] = wire[...].astype(BF16)
+        out[: wire.shape[0], :] = wire[...].astype(BF16)
+        if out.shape[0] > wire.shape[0]:
+            out[wire.shape[0] :, :] = jnp.zeros((out.shape[0] - wire.shape[0], LANES), BF16)
 
     @pl.when(branch == 0)
     def _():
@@ -177,38 +179,41 @@
     return jnp.concatenate(blocks, axis=0)
 
 
-def prepare_kernel(groups, share, low_count, scalars, weight, picked, table, full, part, stage_one, turns, stage_two):
+def tables_kernel(low_count, table, stage_one, turns, stage_two):
+    high, low = high_low(table[: 2 * LANES])
+    stage_two[...] = jnp.concatenate([high, low, high], axis=0)
+    turns[...] = table[2 * LANES : 2 * LANES + low_count]
+    high, low = high_low(table[2 * LANES + low_count :, :low_count])
+    stage_one[...] = jnp.concatenate([high, low, high], axis=1)
+
+
+def weights_kernel(groups, share, ready, scalars, weight, picked, full, part):
     me = scalars[0]
     full[...] = swap_units(0.5 * weight[...].astype(F32).T, 2, 8).astype(BF16)
-    if picked is not None:
+    if ready:
         rows = picked[...]
     else:
         size = weight.shape[0] // (share * groups)
         starts = [pl.multiple_of((group * groups + me) * size, 16) for group in range(share)]
         rows = jnp.concatenate([weight[pl.ds(start, size), :] for start in starts], axis=0)
     part[...] = swap_units(0.5 * rows.astype(F32).T, 2, 8).astype(BF16)
-    high, low = high_low(table[: 2 * LANES])
-    stage_two[...] = jnp.concatenate([high, low, high], axis=0)
-    turns[...] = table[2 * LANES : 2 * LANES + low_count]
-    high, low = high_low(table[2 * LANES + low_count :, :low_count])
-    stage_one[...] = jnp.concatenate([high, low, high], axis=1)
-
-
-def prepare_whole(kernel, scalars, weight, *refs):
-    kernel(scalars, weight, None, *refs)
+
+
+def weights_whole(kernel, scalars, weight, full, part):
+    kernel(scalars, weight, None, full, part)
 
 
 def slope_kernel(groups, ready, merged, small, scalars, weights, projection, *refs):
     count = 1 if ready else 2 * groups
     slots = refs[:count]
-    grads = refs[count:-6]
-    payload, flat, odd, total, pool, split = refs[-6:]
+    grads = refs[count:-7]
+    payload, flat, odd, total, pool, sample, split = refs[-7:]
     me, branch, grp_pos = scalars[0], scalars[1], scalars[2]
     lows = flat.shape[0] - 4
     low_count = 2 * lows
     share = len(grads)
     wide = 4 * LANES
-    rows = grads[0].shape[0]
+    rows = total.shape[1] // share
     if ready:
         flat[2 : 2 + lows] = slots[0][...].reshape(lows, LANES, LANES)
         heads = projection[...]
@@ -216,7 +221,7 @@
         for flip in range(2):
             for turn in range(groups):
                 at = pl.multiple_of(((branch ^ flip) * groups + (me ^ turn)) * 16, 16)
-                flat[2 : 2 + lows, pl.ds(at, 16), :] = slots[flip * groups + turn][...].reshape(lows, 16, LANES)
+                flat[2 : 2 + lows, pl.ds(at, 16), :] = slots[flip * groups + turn][: lows * 16, :].reshape(lows, 16, LANES)
         starts = [pl.multiple_of((group * groups + me) * rows, 16) for group in range(share)]
         heads = jnp.concatenate([projection[pl.ds(start, rows), :] for start in starts], axis=0)
     for edge in range(2):
@@ -230,6 +235,7 @@
         current = following
     total[...] = jnp.zeros_like(total)
     pool[...] = jnp.zeros_like(pool)
+    sample[...] = jnp.zeros_like(sample)
 
     def step(index, _):
         first = index * merged
@@ -252,6 +258,7 @@
             total[...] += jnp.dot(
                 jnp.concatenate(patches, axis=1), jnp.concatenate(slopes, axis=0), preferred_element_type=F32
             )
+            sample[...] += jnp.sum(slopes[0].astype(F32).reshape(small * LANES // 8, 8, -1), axis=0)
         pool[...] = sums
         return 0
 
@@ -259,14 +266,34 @@
     line = jnp.sum(pool[...], axis=0, keepdims=True)
     column = jnp.broadcast_to(line, (LANES, line.shape[1])).T
     latent = jnp.sum(column * heads.astype(F32), axis=0, keepdims=True)
-    payload[...] = jnp.zeros_like(payload)
-    for device in range(payload.shape[0]):
-        target = device // groups % share
-        payload[device, 0:1, :] = latent
-        payload[device, 1:2, 0:rows] = line[:, target * rows : (target + 1) * rows]
-    split[...] = swap_units(total[...], 8, 2).T.reshape(share, rows, wide)
-    for turn in range(share):
-        grads[turn][...] = split[grp_pos ^ turn]
+    features = jnp.sum(flat[2 : 2 + lows].astype(F32), axis=0)
+    features = jnp.sum(features, axis=1, keepdims=True).reshape(8, 2, 8, 1)
+    features = (features[:, 0] + features[:, 1]).astype(BF16).astype(F32)
+    column = jnp.broadcast_to(features[:, None], (8, 2, 8, 1)).reshape(LANES, 1)
+    column = jnp.concatenate([column] * 4, axis=0)
+    means = jnp.sum(sample[...], axis=0, keepdims=True) * (merged / (2.0 * small * LANES * lows))
+    means = means.astype(BF16).astype(F32)
+    split[...] = swap_units(total[...] - column * means, 8, 2).T.reshape(share, rows, wide)
+    sums = jnp.broadcast_to(features.reshape(LANES // 2, 1), (LANES // 2, LANES)).T[0:1]
+    fill = jnp.zeros((1, LANES - rows), F32)
+    for target in range(share):
+        part = slice(target * rows, (target + 1) * rows)
+        lines = [
+            latent,
+            jnp.concatenate([line[:, part], fill], axis=1),
+            jnp.concatenate([means[:, part], fill], axis=1),
+            jnp.concatenate([sums, sums], axis=1),
+        ]
+        block = jnp.concatenate(lines, axis=0)
+        for device in range(payload.shape[0]):
+            if device // groups % share == target:
+                payload[device] = block
+    for turn, grad in enumerate(grads):
+        part = split[grp_pos ^ turn]
+        lines = [part[:, at : at + LANES] for at in range(0, wide, LANES)]
+        if grad.shape[0] > 4 * rows:
+            lines.append(jnp.zeros((grad.shape[0] - 4 * rows, LANES), F32))
+        grad[...] = jnp.concatenate(lines, axis=0).astype(BF16)
 
 
 def odd_rows(even, following):
@@ -376,7 +403,12 @@
     result = None
     for turn in range(share):
         column = jnp.sum(jnp.where(lane == (grp_pos ^ turn), spread, 0.0), axis=1, keepdims=True)
-        term = column * pieces[turn][...]
+        piece = pieces[turn][: 4 * rows, :].astype(F32)
+        piece = jnp.concatenate([piece[at : at + rows] for at in range(0, 4 * rows, rows)], axis=1)
+        extra = arrived[(branch * share + (grp_pos ^ turn)) * groups + scalars[0]]
+        means = jnp.concatenate([extra, extra], axis=0).T[:rows, 2:3]
+        sums = jnp.concatenate([extra[3:4]] * (out.shape[1] // LANES), axis=1)
+        term = column * (piece + means * sums)
         result = term if result is None else result + term
     out[...] = result
 
@@ -431,29 +463,36 @@
         lax.ppermute(pieces[turn], "seq", [(i, i ^ turn) for i in range(groups)]) for turn in range(1, groups)
     ]
     table = jnp.asarray(fourier_tables(full_len))
-    with jax.named_scope("prepare"):
-        kernel = functools.partial(prepare_kernel, groups, share, low_count)
-        if not ready:
-            kernel = functools.partial(prepare_whole, kernel)
-        weights, part_weights, stage_one, turns, stage_two = call(
-            kernel,
+    with jax.named_scope("tables"):
+        stage_one, turns, stage_two = call(
+            functools.partial(tables_kernel, low_count),
             [
-                jax.ShapeDtypeStruct((width, hidden), BF16),
-                jax.ShapeDtypeStruct((width, share * rows), BF16),
                 jax.ShapeDtypeStruct((2 * low_count, 3 * low_count), BF16),
                 jax.ShapeDtypeStruct((low_count, 2 * LANES), F32),
                 jax.ShapeDtypeStruct((6 * LANES, 2 * LANES), BF16),
             ],
-            [SMEM] + [VMEM] * (3 if ready else 2),
+            [VMEM],
+            flops=10**6,
+            moved=10**6,
+        )(table)
+    with jax.named_scope("weights"):
+        kernel = functools.partial(weights_kernel, groups, share, ready)
+        if not ready:
+            kernel = functools.partial(weights_whole, kernel)
+        weights, part_weights = call(
+            kernel,
+            [jax.ShapeDtypeStruct((width, hidden), BF16), jax.ShapeDtypeStruct((width, share * rows), BF16)],
+            [SMEM] + [VMEM] * (2 if ready else 1),
             flops=10**8,
             moved=3 * 10**6,
             room=24,
-        )(*([scalars, weight, picked, table] if ready else [scalars, weight, table]))
+        )(*([scalars, weight, picked] if ready else [scalars, weight]))
     wire = jax.ShapeDtypeStruct((chans * low_count, LANES), BF16)
+    longer = jax.ShapeDtypeStruct((chans * low_count + 16, LANES), BF16)
     with jax.named_scope("fourier"):
         own, pay = call(
             functools.partial(fourier_kernel, groups, full_len, length // 8, listed),
-            [wire, wire],
+            [wire, longer],
             [SMEM] + [VMEM] * (3 + groups),
             [
                 pltpu.VMEM((groups, chans, length), F32),
@@ -482,6 +521,7 @@
                 slots[flip * groups + turn], "seq", [(i, i ^ 1) for i in range(groups)]
             )
     if ready:
+        slots = [slot[: chans * low_count] for slot in slots]
         slots = [assemble(slots, groups, low_count, seq_pos, branch)]
 
     devices = sides * share * groups
@@ -489,12 +529,16 @@
     with jax.named_scope("slope"):
         *grads, payload, flat = call(
             functools.partial(slope_kernel, groups, ready, 32, 4),
-            [jax.ShapeDtypeStruct((rows, width), F32)] * share
-            + [jax.ShapeDtypeStruct((devices, 2, LANES), F32), tiles],
+            [
+                jax.ShapeDtypeStruct((4 * rows + (16 if turn >= share // 2 else 0), LANES), BF16)
+                for turn in range(share)
+            ]
+            + [jax.ShapeDtypeStruct((devices, 4, LANES), F32), tiles],
             [SMEM] + [VMEM] * (2 + len(slots)),
             [
                 pltpu.VMEM((lows + 4, LANES, LANES), BF16),
                 pltpu.VMEM((width, share * rows), F32),
+                pltpu.VMEM((8, share * rows), F32),
                 pltpu.VMEM((8, share * rows), F32),
                 pltpu.VMEM((share, rows, width), F32),
             ],

time: 49.6 us -> 48.2 us (0.972)
  local copies, waits for them, and re-layouts: 3.96 us -> 2.82 us
  waiting for transfers between devices: 10.3 us -> 9.42 us
  Pallas kernels: 17.5 us -> 18.1 us
    ppermute x3, waiting for transfers between devices: 0.01 us -> 1.96 us  [body(): lax.ppermute(pieces[turn], 'seq', [(i, i ^ turn) for i in range(groups)])]
    all_to_all x1, waiting for transfers between devices: 2.75 us -> 1.42 us  [body(): lax.all_to_all(payload, ('pair', 'grp', 'seq'), split_axis=0, concat_axis...]
    unnamed x8, local copies, waits for them, and re-layouts: 3.19 us -> 1.97 us
    ppermute x3, waiting for transfers between devices: 6.51 us -> 5.69 us  [body(): block = lax.ppermute(block, ('pair', 'seq'), pairs)]
    ppermute x4, waiting for transfers between devices: 1.02 us -> 0.35 us  [body(): lax.ppermute(slots[flip * groups + turn], 'seq', [(i, i ^ 1) for i in ran...]
  transfers between devices with their start and end apart: 14 -> 14, of which waited for: 5 -> 7; matrix products, arithmetic and copies ran while one was open for 2% -> 2% of each run, Pallas kernels for 14% -> 14%
where the time goes in v3:
time: 48.2 us; the launch traced here: 48 us
  Pallas kernels  18.1 us (38%)
  starting transfers between devices  16.7 us (35%)
  waiting for transfers between devices  9.42 us (20%)
  local copies, waits for them, and re-layouts  2.82 us (6%)
  between operations  0.87 us (2%)
    pallas_call x1, Pallas kernels, body(): call(functools.partial(slope_kernel, groups, ready, 32, 4), [jax.ShapeDty...  7.27 us
    pallas_call x1, Pallas kernels, body(): pl.pallas_call(functools.partial(encode_kernel, groups, 256), out_shape=j...  5.8 us
    ppermute x3, waiting for transfers between devices, body(): block = lax.ppermute(block, ('pair', 'seq'), pairs)  5.69 us
    all_to_all x1, starting transfers between devices, body(): lax.all_to_all(payload, ('pair', 'grp', 'seq'), split_axis=0, concat_axis...  5.33 us
    ppermute x3, starting transfers between devices, body(): lax.ppermute(grads[turn], 'grp', [(i, i ^ turn) for i in range(share)])  4.17 us
    ppermute x3, starting transfers between devices, body(): block = lax.ppermute(block, ('pair', 'seq'), pairs)  3.55 us
    ppermute x3, starting transfers between devices, body(): lax.ppermute(pieces[turn], 'seq', [(i, i ^ turn) for i in range(groups)])  3.15 us
    pallas_call x1, Pallas kernels, body(): call(functools.partial(loss_kernel, groups, share, full_len, listed, read...  2.17 us
  transfers between devices with their start and end apart: 14, of which 7 were waited for; matrix products, arithmetic and copies ran while one was open for 2% of the time, Pallas kernels for 14%

profile of v3, /device:TPU:0, one launch (start us, length us, event | category | flops | bytes accessed | tf_op | source)
XLA Modules:
  0.0 48.0 jit_solution(6906661143103080692)
XLA Ops:
  0.6 0.0 copy-start.2
  0.6 0.9 %copy-done.2 = f32[1,2048,32]{1,2,0:T(8,128)S(1)} copy-done((f32[1,2048,32]{1,2,0:T(8,128)S(1)}, f32[1,2048,32]{1,2,0:T(8,128)}, u32[]{:S(2)}) %copy-start.2) | copy-done | bytes 262168
  1.6 0.3 arrange.1
  1.9 0.5 %collective-permute-start = (f32[8,2048]{1,0:T(8,128)S(1)}, f32[8,2048]{1,0:T(8,128)S(1)}, u32[]{:S(2)}, u32[]{:S(2)}) collective-permute-start(f32[8,2048]{1,0:T(8,128)S(1)} %get-tuple-element.29), channel_id=1, source_target_pairs={{0,1},{1,0},{2,3},{3,2},{4,5},{5,4},{6,7},{7,6},{8,9},{9,8},{10,11... | collective-permute-start | bytes 196616 | tf_op jit(solution)/shard_map/ppermute | solution.py:463
  2.5 2.6 %collective-permute-start.1 = (f32[8,2048]{1,0:T(8,128)S(1)}, f32[8,2048]{1,0:T(8,128)S(1)}, u32[]{:S(2)}, u32[]{:S(2)}) collective-permute-start(f32[8,2048]{1,0:T(8,128)S(1)} %get-tuple-element.30), channel_id=1, source_target_pairs={{0,2},{1,3},{2,0},{3,1},{4,6},{5,7},{6,4},{7,5},{8,10},{9,11},{10,... | collective-permute-start | bytes 196616 | tf_op jit(solution)/shard_map/ppermute | solution.py:463
  5.0 0.1 collective-permute-start.2
  5.1 0.0 copy-start
  5.1 0.9 %concatenate.3.scalars = s32[15]{0:T(128)S(1)} concatenate(s32[1]{0:T(128)} %bitcast, s32[1]{0:T(128)} %bitcast.1, s32[1]{0:T(128)} %bitcast.2, s32[4]{0:T(128)} %bitcast.20, s32[4]{0:T(128)} %bitcast.21, s32[4]{0:T(128)} %param.10), dimensions={0} | concatenate | bytes 120 | tf_op jit(solution)/shard_map/concatenate | solution.py:443
  5.9 0.0 copy-start.1
  5.9 1.0 %copy-done.1 = f32[448,256]{1,0:T(8,128)S(1)} copy-done((f32[448,256]{1,0:T(8,128)S(1)}, f32[448,256]{1,0:T(8,128)}, u32[]{:S(2)}) %copy-start.1) | copy-done | bytes 458776
  7.0 0.1 tables.1
  7.1 0.0 collective-permute-done.refs_1_
  7.1 0.6 %collective-permute-done.1.refs_2_ = f32[8,2048]{1,0:T(8,128)S(1)} collective-permute-done((f32[8,2048]{1,0:T(8,128)S(1)}, f32[8,2048]{1,0:T(8,128)S(1)}, u32[]{:S(2)}, u32[]{:S(2)}) %collective-permute-start.1) | collective-permute-done | bytes 65568 | tf_op jit(solution)/shard_map/ppermute | solution.py:463
  7.7 1.4 %collective-permute-done.2.refs_3_ = f32[8,2048]{1,0:T(8,128)S(1)} collective-permute-done((f32[8,2048]{1,0:T(8,128)S(1)}, f32[8,2048]{1,0:T(8,128)S(1)}, u32[]{:S(2)}, u32[]{:S(2)}) %collective-permute-start.2) | collective-permute-done | bytes 65568 | tf_op jit(solution)/shard_map/ppermute | solution.py:463
  9.1 0.0 copy-start.3
  9.1 1.4 %fourier.1 = (bf16[512,128]{1,0:T(8,128)(2,1)S(1)}, bf16[528,128]{1,0:T(8,128)(2,1)S(1)}) custom-call(s32[15]{0:T(128)S(1)} %concatenate.3.scalars, bf16[128,192]{1,0:T(8,128)(2,1)S(1)} %get-tuple-element.25.stage_one, f32[64,256]{1,0:T(8,128)S(1)} %get-tuple-element.26.turns, bf16[768,256]{1,0:T(8,128)(2,1)S(1)} %get-tuple-element.27.stage_two, ...), custom_call_target="tpu_custom_call" | custom-call | flops 1000000000 | bytes 2000000 | tf_op jit(solution)/shard_map/fourier/pallas_call | solution.py:493
  10.5 1.6 %collective-permute-start.6 = (bf16[528,128]{1,0:T(8,128)(2,1)S(1)}, bf16[528,128]{1,0:T(8,128)(2,1)S(1)}, u32[]{:S(2)}, u32[]{:S(2)}) collective-permute-start(bf16[528,128]{1,0:T(8,128)(2,1)S(1)} %get-tuple-element.33), channel_id=1, source_target_pairs={{0,16},{1,17},{2,18},{3,19},{16,0},{17,1},{18,2},{19,3},{4,20},{5,... | collective-permute-start | bytes 405512 | tf_op jit(solution)/shard_map/ppermute | solution.py:516
  12.1 1.3 %collective-permute-start.8 = (bf16[528,128]{1,0:T(8,128)(2,1)S(1)}, bf16[528,128]{1,0:T(8,128)(2,1)S(1)}, u32[]{:S(2)}, u32[]{:S(2)}) collective-permute-start(bf16[528,128]{1,0:T(8,128)(2,1)S(1)} %get-tuple-element.33), channel_id=1, source_target_pairs={{0,18},{1,19},{2,16},{3,17},{16,2},{17,3},{18,0},{19,1},{4,22},{5,... | collective-permute-start | bytes 405512 | tf_op jit(solution)/shard_map/ppermute | solution.py:516
  13.4 0.7 %collective-permute-start.4 = (bf16[512,128]{1,0:T(8,128)(2,1)S(1)}, bf16[512,128]{1,0:T(8,128)(2,1)S(1)}, u32[]{:S(2)}, u32[]{:S(2)}) collective-permute-start(bf16[512,128]{1,0:T(8,128)(2,1)S(1)} %get-tuple-element.32.refs_0_), channel_id=1, source_target_pairs={{0,2},{1,3},{2,0},{3,1},{16,18},{17,19},{18,16},{19,17},{4,6},{5,7... | collective-permute-start | bytes 393224 | tf_op jit(solution)/shard_map/ppermute | solution.py:516
  14.1 4.7 %collective-permute-done.6.refs_4_ = bf16[528,128]{1,0:T(8,128)(2,1)S(1)} collective-permute-done((bf16[528,128]{1,0:T(8,128)(2,1)S(1)}, bf16[528,128]{1,0:T(8,128)(2,1)S(1)}, u32[]{:S(2)}, u32[]{:S(2)}) %collective-permute-start.6) | collective-permute-done | bytes 135200 | tf_op jit(solution)/shard_map/ppermute | solution.py:516
  18.8 0.0 collective-permute-start.7
  18.8 0.7 %collective-permute-done.8.refs_6_ = bf16[528,128]{1,0:T(8,128)(2,1)S(1)} collective-permute-done((bf16[528,128]{1,0:T(8,128)(2,1)S(1)}, bf16[528,128]{1,0:T(8,128)(2,1)S(1)}, u32[]{:S(2)}, u32[]{:S(2)}) %collective-permute-start.8) | collective-permute-done | bytes 135200 | tf_op jit(solution)/shard_map/ppermute | solution.py:516
  19.5 0.0 collective-permute-start.9
  19.5 0.5 %collective-permute-start.3 = (bf16[512,128]{1,0:T(8,128)(2,1)S(1)}, bf16[512,128]{1,0:T(8,128)(2,1)S(1)}, u32[]{:S(2)}, u32[]{:S(2)}) collective-permute-start(bf16[512,128]{1,0:T(8,128)(2,1)S(1)} %get-tuple-element.32.refs_0_), channel_id=1, source_target_pairs={{0,1},{1,0},{2,3},{3,2},{4,5},{5,4},{6,7},{7,6},{8,9},{9,8},{10,11... | collective-permute-start | bytes 393224 | tf_op jit(solution)/shard_map/ppermute | solution.py:520
  20.0 0.3 collective-permute-done.4.refs_2_
  20.3 0.0 collective-permute-start.5
  20.3 0.0 copy-done
  20.3 1.0 %weights.1 = (bf16[512,1024]{1,0:T(8,128)(2,1)S(1)}, bf16[512,256]{1,0:T(8,128)(2,1)S(1)}) custom-call(s32[15]{0:T(128)S(1)} %concatenate.3.scalars, bf16[1024,512]{1,0:T(8,128)(2,1)S(1)} %bitcast.16), custom_call_target="tpu_custom_call" | custom-call | flops 100000000 | bytes 3000000 | tf_op jit(solution)/shard_map/weights/pallas_call | solution.py:482
  21.3 0.0 collective-permute-done.3.refs_1_
  21.3 0.3 collective-permute-done.5.refs_3_
  21.6 0.0 collective-permute-done.7.refs_5_
  21.6 0.0 collective-permute-done.9.refs_7_
  21.6 0.0 copy-done.3
  21.6 7.3 %slope.1 = (bf16[256,128]{1,0:T(8,128)(2,1)S(1)}, bf16[256,128]{1,0:T(8,128)(2,1)S(1)}, bf16[272,128]{1,0:T(8,128)(2,1)S(1)}, bf16[272,128]{1,0:T(8,128)(2,1)S(1...) custom-call(s32[15]{0:T(128)S(1)} %concatenate.3.scalars, bf16[512,256]{1,0:T(8,128)(2,1)S(1)} %get-tuple-element.24.weights, ...), custom_call_target="tpu_custom_call" | custom-call | flops 4294967296 | bytes 4000000 | tf_op jit(solution)/shard_map/slope/pallas_call | solution.py:530
  28.9 2.6 %collective-permute-start.11 = (bf16[272,128]{1,0:T(8,128)(2,1)S(1)}, bf16[272,128]{1,0:T(8,128)(2,1)S(1)}, u32[]{:S(2)}, u32[]{:S(2)}) collective-permute-start(bf16[272,128]{1,0:T(8,128)(2,1)S(1)} %get-tuple-element.39), channel_id=1, source_target_pairs={{0,8},{4,12},{8,0},{12,4},{1,9},{5,13},{9,1},{13,5},{2,10},{6,14},... | collective-permute-start | bytes 208904 | tf_op jit(solution)/shard_map/ppermute | solution.py:550
  31.5 1.3 %collective-permute-start.12 = (bf16[272,128]{1,0:T(8,128)(2,1)S(1)}, bf16[272,128]{1,0:T(8,128)(2,1)S(1)}, u32[]{:S(2)}, u32[]{:S(2)}) collective-permute-start(bf16[272,128]{1,0:T(8,128)(2,1)S(1)} %get-tuple-element.40), channel_id=1, source_target_pairs={{0,12},{4,8},{8,4},{12,0},{1,13},{5,9},{9,5},{13,1},{2,14},{6,10},... | collective-permute-start | bytes 208904 | tf_op jit(solution)/shard_map/ppermute | solution.py:550
  32.8 0.2 collective-permute-start.10
  33.1 5.3 %all-to-all-start = ((f32[32,4,128]{2,1,0:T(4,128)}), f32[32,4,128]{2,1,0:T(4,128)S(1)}, u32[]{:S(2)}, u32[]{:S(2)}) async-start(f32[32,4,128]{2,1,0:T(4,128)} %get-tuple-element.36), calls=%async_computation | async-start | bytes 131072 | tf_op jit(solution)/shard_map/all_to_all | solution.py:552
  38.4 5.8 %encode.1 = bf16[1024,1024]{1,0:T(8,128)(2,1)} custom-call(s32[15]{0:T(128)S(1)} %concatenate.3.scalars, bf16[36,128,128]{2,1,0:T(8,128)(2,1)S(1)} %get-tuple-element.34.flat, bf16[512,1024]{1,0:T(8,128)(2,1)S(1)} %get-tuple-element.35.weights), custom_call_target="tpu_custom_call" | custom-call | flops 2147483648 | bytes 4000000 | tf_op jit(solution)/shard_map/encode/pallas_call | solution.py:555
  44.2 0.0 collective-permute-done.10.refs_1_
  44.2 0.0 collective-permute-done.11.refs_2_
  44.2 0.0 collective-permute-done.12.refs_3_
  44.2 1.4 %all-to-all-done.arrived = f32[32,4,128]{2,1,0:T(4,128)S(1)} async-done(((f32[32,4,128]{2,1,0:T(4,128)}), f32[32,4,128]{2,1,0:T(4,128)S(1)}, u32[]{:S(2)}, u32[]{:S(2)}) %all-to-all-start) | async-done | bytes 65568 | tf_op jit(solution)/shard_map/all_to_all | solution.py:552
  45.6 2.2 %loss.1 = (f32[1,1]{1,0:T(1,128)}, f32[64,512]{1,0:T(8,128)}, f32[256,128]{1,0:T(8,128)}) custom-call(s32[15]{0:T(128)S(1)} %concatenate.3.scalars, f32[32,4,128]{2,1,0:T(4,128)S(1)} %all-to-all-done.arrived, bf16[1024,128]{1,0:T(8,128)(2,1)S(1)} %bitcast.19, bf16[256,128]{1,0:T(8,128)(2,1)S(1)} %get-tuple-element.37.refs_0_, ...), custom_call_target="tpu_custom_call" | custom-call | flops 10000000 | bytes 1000000 | tf_op jit(solution)/shard_map/loss/pallas_call | solution.py:572
Async XLA Ops:
  0.6 1.0 %copy-start.2 = (f32[1,2048,32]{1,2,0:T(8,128)S(1)}, f32[1,2048,32]{1,2,0:T(8,128)}, u32[]{:S(2)}) copy-start(f32[1,2048,32]{1,2,0:T(8,128)} %param.7) | copy-start | bytes 786436
  1.9 5.2 %collective-permute-start = (f32[8,2048]{1,0:T(8,128)S(1)}, f32[8,2048]{1,0:T(8,128)S(1)}, u32[]{:S(2)}, u32[]{:S(2)}) collective-permute-start(f32[8,2048]{1,0:T(8,128)S(1)} %get-tuple-element.29), channel_id=1, source_target_pairs={{0,1},{1,0},{2,3},{3,2},{4,5},{5,4},{6,7},{7,6},{8,9},{9,8},{10,11... | collective-permute-start | bytes 196616 | tf_op jit(solution)/shard_map/ppermute | solution.py:463
  2.5 5.3 %collective-permute-start.1 = (f32[8,2048]{1,0:T(8,128)S(1)}, f32[8,2048]{1,0:T(8,128)S(1)}, u32[]{:S(2)}, u32[]{:S(2)}) collective-permute-start(f32[8,2048]{1,0:T(8,128)S(1)} %get-tuple-element.30), channel_id=1, source_target_pairs={{0,2},{1,3},{2,0},{3,1},{4,6},{5,7},{6,4},{7,5},{8,10},{9,11},{10,... | collective-permute-start | bytes 196616 | tf_op jit(solution)/shard_map/ppermute | solution.py:463
  5.0 4.0 %collective-permute-start.2 = (f32[8,2048]{1,0:T(8,128)S(1)}, f32[8,2048]{1,0:T(8,128)S(1)}, u32[]{:S(2)}, u32[]{:S(2)}) collective-permute-start(f32[8,2048]{1,0:T(8,128)S(1)} %get-tuple-element.31), channel_id=1, source_target_pairs={{0,3},{1,2},{2,1},{3,0},{4,7},{5,6},{6,5},{7,4},{8,11},{9,10},{10,... | collective-permute-start | bytes 196616 | tf_op jit(solution)/shard_map/ppermute | solution.py:463
  5.1 15.2 %copy-start = (bf16[1,1024,512]{2,1,0:T(8,128)(2,1)S(1)}, bf16[1,1024,512]{2,1,0:T(8,128)(2,1)}, u32[]{:S(2)}) copy-start(bf16[1,1024,512]{2,1,0:T(8,128)(2,1)} %param.11) | copy-start | bytes 3145732
  5.9 1.0 %copy-start.1 = (f32[448,256]{1,0:T(8,128)S(1)}, f32[448,256]{1,0:T(8,128)}, u32[]{:S(2)}) copy-start(f32[448,256]{1,0:T(8,128)} %constant.15.clone.table) | copy-start | bytes 1376260
  9.1 12.6 %copy-start.3 = (bf16[1,1024,128]{2,1,0:T(8,128)(2,1)S(1)}, bf16[1,1024,128]{2,1,0:T(8,128)(2,1)}, u32[]{:S(2)}) copy-start(bf16[1,1024,128]{2,1,0:T(8,128)(2,1)} %param.12) | copy-start | bytes 786436
  10.5 8.3 %collective-permute-start.6 = (bf16[528,128]{1,0:T(8,128)(2,1)S(1)}, bf16[528,128]{1,0:T(8,128)(2,1)S(1)}, u32[]{:S(2)}, u32[]{:S(2)}) collective-permute-start(bf16[528,128]{1,0:T(8,128)(2,1)S(1)} %get-tuple-element.33), channel_id=1, source_target_pairs={{0,16},{1,17},{2,18},{3,19},{16,0},{17,1},{18,2},{19,3},{4,20},{5,... | collective-permute-start | bytes 405512 | tf_op jit(solution)/shard_map/ppermute | solution.py:516
  12.1 7.4 %collective-permute-start.8 = (bf16[528,128]{1,0:T(8,128)(2,1)S(1)}, bf16[528,128]{1,0:T(8,128)(2,1)S(1)}, u32[]{:S(2)}, u32[]{:S(2)}) collective-permute-start(bf16[528,128]{1,0:T(8,128)(2,1)S(1)} %get-tuple-element.33), channel_id=1, source_target_pairs={{0,18},{1,19},{2,16},{3,17},{16,2},{17,3},{18,0},{19,1},{4,22},{5,... | collective-permute-start | bytes 405512 | tf_op jit(solution)/shard_map/ppermute | solution.py:516
  13.4 6.9 %collective-permute-start.4 = (bf16[512,128]{1,0:T(8,128)(2,1)S(1)}, bf16[512,128]{1,0:T(8,128)(2,1)S(1)}, u32[]{:S(2)}, u32[]{:S(2)}) collective-permute-start(bf16[512,128]{1,0:T(8,128)(2,1)S(1)} %get-tuple-element.32.refs_0_), channel_id=1, source_target_pairs={{0,2},{1,3},{2,0},{3,1},{16,18},{17,19},{18,16},{19,17},{4,6},{5,7... | collective-permute-start | bytes 393224 | tf_op jit(solution)/shard_map/ppermute | solution.py:516
  18.8 2.8 %collective-permute-start.7 = (bf16[528,128]{1,0:T(8,128)(2,1)S(1)}, bf16[528,128]{1,0:T(8,128)(2,1)S(1)}, u32[]{:S(2)}, u32[]{:S(2)}) collective-permute-start(bf16[528,128]{1,0:T(8,128)(2,1)S(1)} %collective-permute-done.6.refs_4_), channel_id=1, source_target_pairs={{0,1},{1,0},{2,3},{3,2},{4,5},{5,4},{6,7},{7,6},{8,9},{9,8},{10,11... | collective-permute-start | bytes 405512 | tf_op jit(solution)/shard_map/ppermute | solution.py:520
  19.5 2.1 %collective-permute-start.9 = (bf16[528,128]{1,0:T(8,128)(2,1)S(1)}, bf16[528,128]{1,0:T(8,128)(2,1)S(1)}, u32[]{:S(2)}, u32[]{:S(2)}) collective-permute-start(bf16[528,128]{1,0:T(8,128)(2,1)S(1)} %collective-permute-done.8.refs_6_), channel_id=1, source_target_pairs={{0,1},{1,0},{2,3},{3,2},{4,5},{5,4},{6,7},{7,6},{8,9},{9,8},{10,11... | collective-permute-start | bytes 405512 | tf_op jit(solution)/shard_map/ppermute | solution.py:520
  19.5 1.8 %collective-permute-start.3 = (bf16[512,128]{1,0:T(8,128)(2,1)S(1)}, bf16[512,128]{1,0:T(8,128)(2,1)S(1)}, u32[]{:S(2)}, u32[]{:S(2)}) collective-permute-start(bf16[512,128]{1,0:T(8,128)(2,1)S(1)} %get-tuple-element.32.refs_0_), channel_id=1, source_target_pairs={{0,1},{1,0},{2,3},{3,2},{4,5},{5,4},{6,7},{7,6},{8,9},{9,8},{10,11... | collective-permute-start | bytes 393224 | tf_op jit(solution)/shard_map/ppermute | solution.py:520
  20.3 1.3 %collective-permute-start.5 = (bf16[512,128]{1,0:T(8,128)(2,1)S(1)}, bf16[512,128]{1,0:T(8,128)(2,1)S(1)}, u32[]{:S(2)}, u32[]{:S(2)}) collective-permute-start(bf16[512,128]{1,0:T(8,128)(2,1)S(1)} %collective-permute-done.4.refs_2_), channel_id=1, source_target_pairs={{0,1},{1,0},{2,3},{3,2},{4,5},{5,4},{6,7},{7,6},{8,9},{9,8},{10,11... | collective-permute-start | bytes 393224 | tf_op jit(solution)/shard_map/ppermute | solution.py:520
  28.9 15.3 %collective-permute-start.11 = (bf16[272,128]{1,0:T(8,128)(2,1)S(1)}, bf16[272,128]{1,0:T(8,128)(2,1)S(1)}, u32[]{:S(2)}, u32[]{:S(2)}) collective-permute-start(bf16[272,128]{1,0:T(8,128)(2,1)S(1)} %get-tuple-element.39), channel_id=1, source_target_pairs={{0,8},{4,12},{8,0},{12,4},{1,9},{5,13},{9,1},{13,5},{2,10},{6,14},... | collective-permute-start | bytes 208904 | tf_op jit(solution)/shard_map/ppermute | solution.py:550
  31.5 12.7 %collective-permute-start.12 = (bf16[272,128]{1,0:T(8,128)(2,1)S(1)}, bf16[272,128]{1,0:T(8,128)(2,1)S(1)}, u32[]{:S(2)}, u32[]{:S(2)}) collective-permute-start(bf16[272,128]{1,0:T(8,128)(2,1)S(1)} %get-tuple-element.40), channel_id=1, source_target_pairs={{0,12},{4,8},{8,4},{12,0},{1,13},{5,9},{9,5},{13,1},{2,14},{6,10},... | collective-permute-start | bytes 208904 | tf_op jit(solution)/shard_map/ppermute | solution.py:550
  32.8 11.4 %collective-permute-start.10 = (bf16[256,128]{1,0:T(8,128)(2,1)S(1)}, bf16[256,128]{1,0:T(8,128)(2,1)S(1)}, u32[]{:S(2)}, u32[]{:S(2)}) collective-permute-start(bf16[256,128]{1,0:T(8,128)(2,1)S(1)} %get-tuple-element.38), channel_id=1, source_target_pairs={{0,4},{4,0},{8,12},{12,8},{1,5},{5,1},{9,13},{13,9},{2,6},{6,2},{1... | collective-permute-start | bytes 196616 | tf_op jit(solution)/shard_map/ppermute | solution.py:550
  33.1 12.6 %all-to-all-start = ((f32[32,4,128]{2,1,0:T(4,128)}), f32[32,4,128]{2,1,0:T(4,128)S(1)}, u32[]{:S(2)}, u32[]{:S(2)}) async-start(f32[32,4,128]{2,1,0:T(4,128)} %get-tuple-element.36), calls=%async_computation | async-start | bytes 131072 | tf_op jit(solution)/shard_map/all_to_all | solution.py:552

commit v4 on v3

--- a/solution.py
+++ b/solution.py
@@ -187,27 +187,11 @@
     stage_one[...] = jnp.concatenate([high, low, high], axis=1)
 
 
-def weights_kernel(groups, share, ready, scalars, weight, picked, full, part):
-    me = scalars[0]
-    full[...] = swap_units(0.5 * weight[...].astype(F32).T, 2, 8).astype(BF16)
-    if ready:
-        rows = picked[...]
-    else:
-        size = weight.shape[0] // (share * groups)
-        starts = [pl.multiple_of((group * groups + me) * size, 16) for group in range(share)]
-        rows = jnp.concatenate([weight[pl.ds(start, size), :] for start in starts], axis=0)
-    part[...] = swap_units(0.5 * rows.astype(F32).T, 2, 8).astype(BF16)
-
-
-def weights_whole(kernel, scalars, weight, full, part):
-    kernel(scalars, weight, None, full, part)
-
-
-def slope_kernel(groups, ready, merged, small, scalars, weights, projection, *refs):
+def slope_kernel(groups, ready, merged, small, scalars, weight, projection, *refs):
     count = 1 if ready else 2 * groups
     slots = refs[:count]
-    grads = refs[count:-7]
-    payload, flat, odd, total, pool, sample, split = refs[-7:]
+    grads = refs[count:-8]
+    payload, flat, odd, weights, total, pool, sample, split = refs[-8:]
     me, branch, grp_pos = scalars[0], scalars[1], scalars[2]
     lows = flat.shape[0] - 4
     low_count = 2 * lows
@@ -217,6 +201,7 @@
     if ready:
         flat[2 : 2 + lows] = slots[0][...].reshape(lows, LANES, LANES)
         heads = projection[...]
+        picked = weight[...]
     else:
         for flip in range(2):
             for turn in range(groups):
@@ -224,6 +209,8 @@
                 flat[2 : 2 + lows, pl.ds(at, 16), :] = slots[flip * groups + turn][: lows * 16, :].reshape(lows, 16, LANES)
         starts = [pl.multiple_of((group * groups + me) * rows, 16) for group in range(share)]
         heads = jnp.concatenate([projection[pl.ds(start, rows), :] for start in starts], axis=0)
+        picked = jnp.concatenate([weight[pl.ds(start, rows), :] for start in starts], axis=0)
+    weights[...] = swap_units(0.5 * picked.astype(F32).T, 2, 8).astype(BF16)
     for edge in range(2):
         flat[edge] = shift_high(flat[lows + edge].astype(F32), low_count, -1).astype(BF16)
         flat[lows + 2 + edge] = shift_high(flat[2 + edge].astype(F32), low_count, 1).astype(BF16)
@@ -262,7 +249,10 @@
         pool[...] = sums
         return 0
 
-    lax.fori_loop(0, lows // merged, step, 0)
+    if lows == merged:
+        step(0, 0)
+    else:
+        lax.fori_loop(0, lows // merged, step, 0)
     line = jnp.sum(pool[...], axis=0, keepdims=True)
     column = jnp.broadcast_to(line, (LANES, line.shape[1])).T
     latent = jnp.sum(column * heads.astype(F32), axis=0, keepdims=True)
@@ -298,45 +288,59 @@
 
 def odd_rows(even, following):
     lane = lax.broadcasted_iota(jnp.int32, even.shape, 1)
-    return jnp.where(lane % 16 < 8, pltpu.roll(even, LANES - 8, 1), pltpu.roll(following, 8, 1))
-
-
-def encode_kernel(groups, chunk, scalars, flat, weights, out, tall, near, patches):
-    count = out.shape[0]
+    return jnp.where(lane < LANES // 2, pltpu.roll(even, LANES // 2, 1), pltpu.roll(following, LANES // 2, 1))
+
+
+def encode_kernel(groups, chunk, columns, scalars, flat, weight, out, tall, near, patches, held, done):
+    me = scalars[0]
+    count, hidden = held.shape
     lows = flat.shape[0] - 4
-
-    @pl.when(pl.program_id(0) == 0)
-    def _():
-        me = scalars[0]
-        for index in range(lows + 4):
-            tall[index * LANES : (index + 1) * LANES, :] = flat[index].astype(F32).T
-        inner = min(2 * lows, LANES)
-        parts = LANES // inner
-        highs = LANES // groups
-        end = 8 + highs * lows
-        near[0:8, :] = jnp.zeros((8, LANES), F32)
-        near[end:, :] = jnp.zeros((16, LANES), F32)
-        for item in range(highs):
-            high = me * highs + item
-            lane = (high % parts) * inner + high // parts
-            if item == 0:
-                near[6:8, :] = tall[pl.ds(lane, 2, stride=LANES), :]
-            near[8 + item * lows : 8 + (item + 1) * lows, :] = tall[pl.ds(2 * LANES + lane, lows, stride=LANES), :]
-            if item == highs - 1:
-                near[end : end + 2, :] = tall[pl.ds((lows + 2) * LANES + lane, 2, stride=LANES), :]
-        for start in range(0, count, LANES):
-            window = near[start : start + LANES + 24, :]
+    for index in range(lows + 4):
+        tall[index * LANES : (index + 1) * LANES, :] = 0.5 * swap_units(flat[index].astype(F32), 8, 2).T
+    inner = min(2 * lows, LANES)
+    parts = LANES // inner
+    highs = LANES // groups
+    end = 8 + highs * lows
+    near[0:8, :] = jnp.zeros((8, LANES), F32)
+    near[end:, :] = jnp.zeros((16, LANES), F32)
+
+    def fill(item):
+        high = me * highs + item
+        lane = (high % parts) * inner + high // parts
+        if item == 0:
+            near[6:8, :] = tall[pl.ds(lane, 2, stride=LANES), :]
+        near[8 + item * lows : 8 + (item + 1) * lows, :] = tall[pl.ds(2 * LANES + lane, lows, stride=LANES), :]
+        if item == highs - 1:
+            near[end : end + 2, :] = tall[pl.ds((lows + 2) * LANES + lane, 2, stride=LANES), :]
+
+    filled = 0
+    copies = []
+    for start in range(0, count, chunk):
+        while filled < highs and filled * lows < start + chunk + 16:
+            fill(filled)
+            filled += 1
+        for at in range(start, start + chunk, LANES):
+            window = near[at : at + LANES + 24, :]
             even = window[: LANES + 16]
-            patches[0, start : start + LANES, :] = stack_rows(even, LANES)
-            patches[1, start : start + LANES, :] = stack_rows(odd_rows(even, window[1 : LANES + 17]), LANES)
-
-    for start in range(0, count, chunk):
-        sums = None
-        for parity in range(2):
-            half = jnp.dot(patches[parity, start : start + chunk], weights[...], preferred_element_type=F32)
-            active = half * gelu_parts(half)[1]
-            sums = active if sums is None else sums + active
-        out[start : start + chunk, :] = (sums * 0.5).astype(BF16)
+            patches[0, at : at + LANES, :] = stack_rows(even, LANES)
+            patches[1, at : at + LANES, :] = stack_rows(odd_rows(even, window[1 : LANES + 17]), LANES)
+        for column in range(0, hidden, columns):
+            sums = None
+            for parity in range(2):
+                half = lax.dot_general(
+                    patches[parity, start : start + chunk],
+                    weight[column : column + columns],
+                    (((1,), (1,)), ((), ())),
+                    preferred_element_type=F32,
+                )
+                active = half * gelu_parts(half)[1]
+                sums = active if sums is None else sums + active
+            block = (pl.ds(start, chunk), pl.ds(column, columns))
+            held[start : start + chunk, column : column + columns] = (sums * 0.5).astype(BF16)
+            copies.append(pltpu.make_async_copy(held.at[block], out.at[block], done.at[len(copies)]))
+            copies[-1].start()
+    for copy in copies:
+        copy.wait()
 
 
 def loss_kernel(groups, share, full_len, listed, ready, scalars, arrived, projection, *refs):
@@ -475,18 +479,6 @@
             flops=10**6,
             moved=10**6,
         )(table)
-    with jax.named_scope("weights"):
-        kernel = functools.partial(weights_kernel, groups, share, ready)
-        if not ready:
-            kernel = functools.partial(weights_whole, kernel)
-        weights, part_weights = call(
-            kernel,
-            [jax.ShapeDtypeStruct((width, hidden), BF16), jax.ShapeDtypeStruct((width, share * rows), BF16)],
-            [SMEM] + [VMEM] * (2 if ready else 1),
-            flops=10**8,
-            moved=3 * 10**6,
-            room=24,
-        )(*([scalars, weight, picked] if ready else [scalars, weight]))
     wire = jax.ShapeDtypeStruct((chans * low_count, LANES), BF16)
     longer = jax.ShapeDtypeStruct((chans * low_count + 16, LANES), BF16)
     with jax.named_scope("fourier"):
@@ -530,13 +522,14 @@
         *grads, payload, flat = call(
             functools.partial(slope_kernel, groups, ready, 32, 4),
             [
-                jax.ShapeDtypeStruct((4 * rows + (16 if turn >= share // 2 else 0), LANES), BF16)
+                jax.ShapeDtypeStruct((4 * rows + (16 if turn < share // 2 else 0), LANES), BF16)
                 for turn in range(share)
             ]
             + [jax.ShapeDtypeStruct((devices, 4, LANES), F32), tiles],
             [SMEM] + [VMEM] * (2 + len(slots)),
             [
                 pltpu.VMEM((lows + 4, LANES, LANES), BF16),
+                pltpu.VMEM((width, share * rows), BF16),
                 pltpu.VMEM((width, share * rows), F32),
                 pltpu.VMEM((8, share * rows), F32),
                 pltpu.VMEM((8, share * rows), F32),
@@ -545,29 +538,30 @@
             flops=4 * full_len * share * rows * width,
             moved=4 * 10**6,
             room=20 + 8 * (low_count // LANES),
-        )(scalars, part_weights, mid_heads, *slots)
+        )(scalars, picked, mid_heads, *slots)
     grads = [grads[0]] + [
         lax.ppermute(grads[turn], "grp", [(i, i ^ turn) for i in range(share)]) for turn in range(1, share)
     ]
     arrived = lax.all_to_all(payload, ("pair", "grp", "seq"), split_axis=0, concat_axis=0, tiled=True)
-    near_len, columns = length // 2, 512
+    near_len, chunk, columns = length // 2, 512, 256
     with jax.named_scope("encode"):
         encoded = pl.pallas_call(
-            functools.partial(encode_kernel, groups, 256),
+            functools.partial(encode_kernel, groups, chunk, columns),
             out_shape=jax.ShapeDtypeStruct((near_len, hidden), BF16),
-            grid=(hidden // columns,),
-            in_specs=[SMEM, VMEM, pl.BlockSpec((width, columns), lambda i: (0, i))],
-            out_specs=pl.BlockSpec((near_len, columns), lambda i: (0, i)),
+            in_specs=[SMEM, VMEM, VMEM],
+            out_specs=HBM,
             scratch_shapes=[
                 pltpu.VMEM(((lows + 4) * LANES, LANES), F32),
                 pltpu.VMEM((near_len + 24, LANES), F32),
                 pltpu.VMEM((2, near_len, width), BF16),
+                pltpu.VMEM((near_len, hidden), BF16),
+                pltpu.SemaphoreType.DMA(((near_len // chunk) * (hidden // columns),)),
             ],
-            compiler_params=pltpu.CompilerParams(vmem_limit_bytes=(20 + 12 * (low_count // LANES)) * 1024 * 1024),
+            compiler_params=pltpu.CompilerParams(vmem_limit_bytes=(24 + 12 * (low_count // LANES)) * 1024 * 1024),
             cost_estimate=pl.CostEstimate(
                 flops=2 * length * hidden * width, bytes_accessed=4 * 10**6, transcendentals=length * hidden
             ),
-        )(scalars, flat, weights)
+        )(scalars, flat, weight)
     with jax.named_scope("loss"):
         loss, conv_share, proj_share = call(
             functools.partial(loss_kernel, groups, share, full_len, listed, ready),

time: 48.2 us -> 47 us (0.975)
  Pallas kernels: 18.1 us -> 16.5 us
  waiting for transfers between devices: 9.42 us -> 10 us
    pallas_call x2 -> x1, Pallas kernels: 6.78 us -> 5.18 us  [body(): pl.pallas_call(functools.partial(encode_kernel, groups, chunk, columns),...]
    all_to_all x1, waiting for transfers between devices: 1.42 us -> 0.01 us  [body(): lax.all_to_all(payload, ('pair', 'grp', 'seq'), split_axis=0, concat_axis...]
    ppermute x4, waiting for transfers between devices: 0.35 us -> 1.33 us  [body(): lax.ppermute(slots[flip * groups + turn], 'seq', [(i, i ^ 1) for i in ran...]
    ppermute x3, waiting for transfers between devices: 0.01 us -> 0.68 us  [body(): lax.ppermute(grads[turn], 'grp', [(i, i ^ turn) for i in range(share)])]
  transfers between devices with their start and end apart: 14 -> 14, of which waited for: 7 -> 8; matrix products, arithmetic and copies ran while one was open for 2% -> 2% of each run, Pallas kernels for 14% -> 11%
where the time goes in v4:
time: 47 us; the launch traced here: 46.7 us
  starting transfers between devices  16.7 us (36%)
  Pallas kernels  16.5 us (35%)
  waiting for transfers between devices  10 us (21%)
  local copies, waits for them, and re-layouts  2.73 us (6%)
  between operations  0.86 us (2%)
    pallas_call x1, Pallas kernels, body(): call(functools.partial(slope_kernel, groups, ready, 32, 4), [jax.ShapeDty...  7.2 us
    ppermute x3, waiting for transfers between devices, body(): block = lax.ppermute(block, ('pair', 'seq'), pairs)  5.96 us
    all_to_all x1, starting transfers between devices, body(): lax.all_to_all(payload, ('pair', 'grp', 'seq'), split_axis=0, concat_axis...  5.33 us
    pallas_call x1, Pallas kernels, body(): pl.pallas_call(functools.partial(encode_kernel, groups, chunk, columns),...  5.18 us
    ppermute x3, starting transfers between devices, body(): lax.ppermute(grads[turn], 'grp', [(i, i ^ turn) for i in range(share)])  4.08 us
    ppermute x3, starting transfers between devices, body(): block = lax.ppermute(block, ('pair', 'seq'), pairs)  3.55 us
    ppermute x3, starting transfers between devices, body(): lax.ppermute(pieces[turn], 'seq', [(i, i ^ turn) for i in range(groups)])  3.15 us
    pallas_call x1, Pallas kernels, body(): call(functools.partial(loss_kernel, groups, share, full_len, listed, read...  2.17 us
  transfers between devices with their start and end apart: 14, of which 8 were waited for; matrix products, arithmetic and copies ran while one was open for 2% of the time, Pallas kernels for 11%

profile of v4, /device:TPU:0, one launch (start us, length us, event | category | flops | bytes accessed | tf_op | source)
XLA Modules:
  0.0 46.7 jit_solution(8810900449135822142)
XLA Ops:
  0.6 0.0 copy-start.1
  0.6 0.9 %copy-done.1 = f32[1,2048,32]{1,2,0:T(8,128)S(1)} copy-done((f32[1,2048,32]{1,2,0:T(8,128)S(1)}, f32[1,2048,32]{1,2,0:T(8,128)}, u32[]{:S(2)}) %copy-start.1) | copy-done | bytes 262168
  1.6 0.3 arrange.1
  1.9 0.5 %collective-permute-start = (f32[8,2048]{1,0:T(8,128)S(1)}, f32[8,2048]{1,0:T(8,128)S(1)}, u32[]{:S(2)}, u32[]{:S(2)}) collective-permute-start(f32[8,2048]{1,0:T(8,128)S(1)} %get-tuple-element.26), channel_id=1, source_target_pairs={{0,1},{1,0},{2,3},{3,2},{4,5},{5,4},{6,7},{7,6},{8,9},{9,8},{10,11... | collective-permute-start | bytes 196616 | tf_op jit(solution)/shard_map/ppermute | solution.py:467
  2.5 2.6 %collective-permute-start.1 = (f32[8,2048]{1,0:T(8,128)S(1)}, f32[8,2048]{1,0:T(8,128)S(1)}, u32[]{:S(2)}, u32[]{:S(2)}) collective-permute-start(f32[8,2048]{1,0:T(8,128)S(1)} %get-tuple-element.27), channel_id=1, source_target_pairs={{0,2},{1,3},{2,0},{3,1},{4,6},{5,7},{6,4},{7,5},{8,10},{9,11},{10,... | collective-permute-start | bytes 196616 | tf_op jit(solution)/shard_map/ppermute | solution.py:467
  5.0 0.1 collective-permute-start.2
  5.1 0.8 %concatenate.3.scalars = s32[15]{0:T(128)S(1)} concatenate(s32[1]{0:T(128)} %bitcast, s32[1]{0:T(128)} %bitcast.1, s32[1]{0:T(128)} %bitcast.2, s32[4]{0:T(128)} %bitcast.21, s32[4]{0:T(128)} %bitcast.22, s32[4]{0:T(128)} %param.10), dimensions={0} | concatenate | bytes 120 | tf_op jit(solution)/shard_map/concatenate | solution.py:447
  5.9 0.0 copy-start
  5.9 1.0 %copy-done = f32[448,256]{1,0:T(8,128)S(1)} copy-done((f32[448,256]{1,0:T(8,128)S(1)}, f32[448,256]{1,0:T(8,128)}, u32[]{:S(2)}) %copy-start) | copy-done | bytes 458776
  6.9 0.0 copy-start.2
  6.9 0.0 copy-start.3
  6.9 0.1 tables.1
  7.0 0.0 collective-permute-done.refs_1_
  7.0 0.7 %collective-permute-done.1.refs_2_ = f32[8,2048]{1,0:T(8,128)S(1)} collective-permute-done((f32[8,2048]{1,0:T(8,128)S(1)}, f32[8,2048]{1,0:T(8,128)S(1)}, u32[]{:S(2)}, u32[]{:S(2)}) %collective-permute-start.1) | collective-permute-done | bytes 65568 | tf_op jit(solution)/shard_map/ppermute | solution.py:467
  7.7 1.4 %collective-permute-done.2.refs_3_ = f32[8,2048]{1,0:T(8,128)S(1)} collective-permute-done((f32[8,2048]{1,0:T(8,128)S(1)}, f32[8,2048]{1,0:T(8,128)S(1)}, u32[]{:S(2)}, u32[]{:S(2)}) %collective-permute-start.2) | collective-permute-done | bytes 65568 | tf_op jit(solution)/shard_map/ppermute | solution.py:467
  9.1 1.4 %fourier.1 = (bf16[512,128]{1,0:T(8,128)(2,1)S(1)}, bf16[528,128]{1,0:T(8,128)(2,1)S(1)}) custom-call(s32[15]{0:T(128)S(1)} %concatenate.3.scalars, bf16[128,192]{1,0:T(8,128)(2,1)S(1)} %get-tuple-element.22.stage_one, f32[64,256]{1,0:T(8,128)S(1)} %get-tuple-element.23.turns, bf16[768,256]{1,0:T(8,128)(2,1)S(1)} %get-tuple-element.24.stage_two, ...), custom_call_target="tpu_custom_call" | custom-call | flops 1000000000 | bytes 2000000 | tf_op jit(solution)/shard_map/fourier/pallas_call | solution.py:485
  10.5 2.4 %collective-permute-start.8 = (bf16[528,128]{1,0:T(8,128)(2,1)S(1)}, bf16[528,128]{1,0:T(8,128)(2,1)S(1)}, u32[]{:S(2)}, u32[]{:S(2)}) collective-permute-start(bf16[528,128]{1,0:T(8,128)(2,1)S(1)} %get-tuple-element.30), channel_id=1, source_target_pairs={{0,18},{1,19},{2,16},{3,17},{16,2},{17,3},{18,0},{19,1},{4,22},{5,... | collective-permute-start | bytes 405512 | tf_op jit(solution)/shard_map/ppermute | solution.py:508
  12.9 0.5 %collective-permute-start.6 = (bf16[528,128]{1,0:T(8,128)(2,1)S(1)}, bf16[528,128]{1,0:T(8,128)(2,1)S(1)}, u32[]{:S(2)}, u32[]{:S(2)}) collective-permute-start(bf16[528,128]{1,0:T(8,128)(2,1)S(1)} %get-tuple-element.30), channel_id=1, source_target_pairs={{0,16},{1,17},{2,18},{3,19},{16,0},{17,1},{18,2},{19,3},{4,20},{5,... | collective-permute-start | bytes 405512 | tf_op jit(solution)/shard_map/ppermute | solution.py:508
  13.4 0.7 %collective-permute-start.4 = (bf16[512,128]{1,0:T(8,128)(2,1)S(1)}, bf16[512,128]{1,0:T(8,128)(2,1)S(1)}, u32[]{:S(2)}, u32[]{:S(2)}) collective-permute-start(bf16[512,128]{1,0:T(8,128)(2,1)S(1)} %get-tuple-element.29.refs_0_), channel_id=1, source_target_pairs={{0,2},{1,3},{2,0},{3,1},{16,18},{17,19},{18,16},{19,17},{4,6},{5,7... | collective-permute-start | bytes 393224 | tf_op jit(solution)/shard_map/ppermute | solution.py:508
  14.1 3.5 %collective-permute-done.8.refs_6_ = bf16[528,128]{1,0:T(8,128)(2,1)S(1)} collective-permute-done((bf16[528,128]{1,0:T(8,128)(2,1)S(1)}, bf16[528,128]{1,0:T(8,128)(2,1)S(1)}, u32[]{:S(2)}, u32[]{:S(2)}) %collective-permute-start.8) | collective-permute-done | bytes 135200 | tf_op jit(solution)/shard_map/ppermute | solution.py:508
  17.5 0.0 collective-permute-start.9
  17.5 2.5 %collective-permute-done.6.refs_4_ = bf16[528,128]{1,0:T(8,128)(2,1)S(1)} collective-permute-done((bf16[528,128]{1,0:T(8,128)(2,1)S(1)}, bf16[528,128]{1,0:T(8,128)(2,1)S(1)}, u32[]{:S(2)}, u32[]{:S(2)}) %collective-permute-start.6) | collective-permute-done | bytes 135200 | tf_op jit(solution)/shard_map/ppermute | solution.py:508
  20.0 0.0 collective-permute-start.7
  20.0 0.5 %collective-permute-start.3 = (bf16[512,128]{1,0:T(8,128)(2,1)S(1)}, bf16[512,128]{1,0:T(8,128)(2,1)S(1)}, u32[]{:S(2)}, u32[]{:S(2)}) collective-permute-start(bf16[512,128]{1,0:T(8,128)(2,1)S(1)} %get-tuple-element.29.refs_0_), channel_id=1, source_target_pairs={{0,1},{1,0},{2,3},{3,2},{4,5},{5,4},{6,7},{7,6},{8,9},{9,8},{10,11... | collective-permute-start | bytes 393224 | tf_op jit(solution)/shard_map/ppermute | solution.py:512
  20.5 0.0 collective-permute-done.4.refs_2_
  20.5 0.0 collective-permute-start.5
  20.6 1.0 %collective-permute-done.3.refs_1_ = bf16[512,128]{1,0:T(8,128)(2,1)S(1)} collective-permute-done((bf16[512,128]{1,0:T(8,128)(2,1)S(1)}, bf16[512,128]{1,0:T(8,128)(2,1)S(1)}, u32[]{:S(2)}, u32[]{:S(2)}) %collective-permute-start.3) | collective-permute-done | bytes 131104 | tf_op jit(solution)/shard_map/ppermute | solution.py:512
  21.6 0.3 collective-permute-done.5.refs_3_
  21.9 0.0 collective-permute-done.9.refs_7_
  21.9 0.0 collective-permute-done.7.refs_5_
  21.9 0.0 copy-done.2
  21.9 0.0 copy-done.3
  21.9 7.2 %slope.1 = (bf16[272,128]{1,0:T(8,128)(2,1)S(1)}, bf16[272,128]{1,0:T(8,128)(2,1)S(1)}, bf16[256,128]{1,0:T(8,128)(2,1)S(1)}, bf16[256,128]{1,0:T(8,128)(2,1)S(1...) custom-call(s32[15]{0:T(128)S(1)} %concatenate.3.scalars, bf16[1024,512]{1,0:T(8,128)(2,1)S(1)} %bitcast.19, ...), custom_call_target="tpu_custom_call" | custom-call | flops 4294967296 | bytes 4000000 | tf_op jit(solution)/shard_map/slope/pallas_call | solution.py:522
  29.1 5.3 %all-to-all-start = ((f32[32,4,128]{2,1,0:T(4,128)}), f32[32,4,128]{2,1,0:T(4,128)S(1)}, u32[]{:S(2)}, u32[]{:S(2)}) async-start(f32[32,4,128]{2,1,0:T(4,128)} %get-tuple-element.32), calls=%async_computation | async-start | bytes 131072 | tf_op jit(solution)/shard_map/all_to_all | solution.py:545
  34.5 2.6 %collective-permute-start.11 = (bf16[256,128]{1,0:T(8,128)(2,1)S(1)}, bf16[256,128]{1,0:T(8,128)(2,1)S(1)}, u32[]{:S(2)}, u32[]{:S(2)}) collective-permute-start(bf16[256,128]{1,0:T(8,128)(2,1)S(1)} %get-tuple-element.35), channel_id=1, source_target_pairs={{0,8},{4,12},{8,0},{12,4},{1,9},{5,13},{9,1},{13,5},{2,10},{6,14},... | collective-permute-start | bytes 196616 | tf_op jit(solution)/shard_map/ppermute | solution.py:543
  37.0 1.5 %collective-permute-start.12 = (bf16[256,128]{1,0:T(8,128)(2,1)S(1)}, bf16[256,128]{1,0:T(8,128)(2,1)S(1)}, u32[]{:S(2)}, u32[]{:S(2)}) collective-permute-start(bf16[256,128]{1,0:T(8,128)(2,1)S(1)} %get-tuple-element.36), channel_id=1, source_target_pairs={{0,12},{4,8},{8,4},{12,0},{1,13},{5,9},{9,5},{13,1},{2,14},{6,10},... | collective-permute-start | bytes 196616 | tf_op jit(solution)/shard_map/ppermute | solution.py:543
  38.5 0.1 collective-permute-start.10
  38.5 5.2 %encode.1 = bf16[1024,1024]{1,0:T(8,128)(2,1)} custom-call(s32[15]{0:T(128)S(1)} %concatenate.3.scalars, bf16[36,128,128]{2,1,0:T(8,128)(2,1)S(1)} %get-tuple-element.31.flat, bf16[1024,512]{1,0:T(8,128)(2,1)S(1)} %bitcast.20), custom_call_target="tpu_custom_call" | custom-call | flops 2147483648 | bytes 4000000 | tf_op jit(solution)/shard_map/encode/pallas_call | solution.py:548
  43.7 0.4 collective-permute-done.11.refs_2_
  44.1 0.0 collective-permute-done.12.refs_3_
  44.1 0.3 collective-permute-done.10.refs_1_
  44.4 0.0 all-to-all-done.arrived
  44.4 2.2 %loss.1 = (f32[1,1]{1,0:T(1,128)}, f32[64,512]{1,0:T(8,128)}, f32[256,128]{1,0:T(8,128)}) custom-call(s32[15]{0:T(128)S(1)} %concatenate.3.scalars, f32[32,4,128]{2,1,0:T(4,128)S(1)} %all-to-all-done.arrived, bf16[1024,128]{1,0:T(8,128)(2,1)S(1)} %bitcast.18, bf16[272,128]{1,0:T(8,128)(2,1)S(1)} %get-tuple-element.33.refs_0_, ...), custom_call_target="tpu_custom_call" | custom-call | flops 10000000 | bytes 1000000 | tf_op jit(solution)/shard_map/loss/pallas_call | solution.py:566
Async XLA Ops:
  0.6 1.0 %copy-start.1 = (f32[1,2048,32]{1,2,0:T(8,128)S(1)}, f32[1,2048,32]{1,2,0:T(8,128)}, u32[]{:S(2)}) copy-start(f32[1,2048,32]{1,2,0:T(8,128)} %param.7) | copy-start | bytes 786436
  1.9 5.1 %collective-permute-start = (f32[8,2048]{1,0:T(8,128)S(1)}, f32[8,2048]{1,0:T(8,128)S(1)}, u32[]{:S(2)}, u32[]{:S(2)}) collective-permute-start(f32[8,2048]{1,0:T(8,128)S(1)} %get-tuple-element.26), channel_id=1, source_target_pairs={{0,1},{1,0},{2,3},{3,2},{4,5},{5,4},{6,7},{7,6},{8,9},{9,8},{10,11... | collective-permute-start | bytes 196616 | tf_op jit(solution)/shard_map/ppermute | solution.py:467
  2.5 5.3 %collective-permute-start.1 = (f32[8,2048]{1,0:T(8,128)S(1)}, f32[8,2048]{1,0:T(8,128)S(1)}, u32[]{:S(2)}, u32[]{:S(2)}) collective-permute-start(f32[8,2048]{1,0:T(8,128)S(1)} %get-tuple-element.27), channel_id=1, source_target_pairs={{0,2},{1,3},{2,0},{3,1},{4,6},{5,7},{6,4},{7,5},{8,10},{9,11},{10,... | collective-permute-start | bytes 196616 | tf_op jit(solution)/shard_map/ppermute | solution.py:467
  5.0 4.0 %collective-permute-start.2 = (f32[8,2048]{1,0:T(8,128)S(1)}, f32[8,2048]{1,0:T(8,128)S(1)}, u32[]{:S(2)}, u32[]{:S(2)}) collective-permute-start(f32[8,2048]{1,0:T(8,128)S(1)} %get-tuple-element.28), channel_id=1, source_target_pairs={{0,3},{1,2},{2,1},{3,0},{4,7},{5,6},{6,5},{7,4},{8,11},{9,10},{10,... | collective-permute-start | bytes 196616 | tf_op jit(solution)/shard_map/ppermute | solution.py:467
  5.9 1.0 %copy-start = (f32[448,256]{1,0:T(8,128)S(1)}, f32[448,256]{1,0:T(8,128)}, u32[]{:S(2)}) copy-start(f32[448,256]{1,0:T(8,128)} %constant.15.clone.table) | copy-start | bytes 1376260
  6.9 15.0 %copy-start.2 = (bf16[1,1024,128]{2,1,0:T(8,128)(2,1)S(1)}, bf16[1,1024,128]{2,1,0:T(8,128)(2,1)}, u32[]{:S(2)}) copy-start(bf16[1,1024,128]{2,1,0:T(8,128)(2,1)} %param.12) | copy-start | bytes 786436
  6.9 15.0 %copy-start.3 = (bf16[1,1024,512]{2,1,0:T(8,128)(2,1)S(1)}, bf16[1,1024,512]{2,1,0:T(8,128)(2,1)}, u32[]{:S(2)}) copy-start(bf16[1,1024,512]{2,1,0:T(8,128)(2,1)} %param.11) | copy-start | bytes 3145732
  10.5 7.0 %collective-permute-start.8 = (bf16[528,128]{1,0:T(8,128)(2,1)S(1)}, bf16[528,128]{1,0:T(8,128)(2,1)S(1)}, u32[]{:S(2)}, u32[]{:S(2)}) collective-permute-start(bf16[528,128]{1,0:T(8,128)(2,1)S(1)} %get-tuple-element.30), channel_id=1, source_target_pairs={{0,18},{1,19},{2,16},{3,17},{16,2},{17,3},{18,0},{19,1},{4,22},{5,... | collective-permute-start | bytes 405512 | tf_op jit(solution)/shard_map/ppermute | solution.py:508
  12.9 7.1 %collective-permute-start.6 = (bf16[528,128]{1,0:T(8,128)(2,1)S(1)}, bf16[528,128]{1,0:T(8,128)(2,1)S(1)}, u32[]{:S(2)}, u32[]{:S(2)}) collective-permute-start(bf16[528,128]{1,0:T(8,128)(2,1)S(1)} %get-tuple-element.30), channel_id=1, source_target_pairs={{0,16},{1,17},{2,18},{3,19},{16,0},{17,1},{18,2},{19,3},{4,20},{5,... | collective-permute-start | bytes 405512 | tf_op jit(solution)/shard_map/ppermute | solution.py:508
  13.4 7.2 %collective-permute-start.4 = (bf16[512,128]{1,0:T(8,128)(2,1)S(1)}, bf16[512,128]{1,0:T(8,128)(2,1)S(1)}, u32[]{:S(2)}, u32[]{:S(2)}) collective-permute-start(bf16[512,128]{1,0:T(8,128)(2,1)S(1)} %get-tuple-element.29.refs_0_), channel_id=1, source_target_pairs={{0,2},{1,3},{2,0},{3,1},{16,18},{17,19},{18,16},{19,17},{4,6},{5,7... | collective-permute-start | bytes 393224 | tf_op jit(solution)/shard_map/ppermute | solution.py:508
  17.5 4.4 %collective-permute-start.9 = (bf16[528,128]{1,0:T(8,128)(2,1)S(1)}, bf16[528,128]{1,0:T(8,128)(2,1)S(1)}, u32[]{:S(2)}, u32[]{:S(2)}) collective-permute-start(bf16[528,128]{1,0:T(8,128)(2,1)S(1)} %collective-permute-done.8.refs_6_), channel_id=1, source_target_pairs={{0,1},{1,0},{2,3},{3,2},{4,5},{5,4},{6,7},{7,6},{8,9},{9,8},{10,11... | collective-permute-start | bytes 405512 | tf_op jit(solution)/shard_map/ppermute | solution.py:512
  20.0 1.9 %collective-permute-start.7 = (bf16[528,128]{1,0:T(8,128)(2,1)S(1)}, bf16[528,128]{1,0:T(8,128)(2,1)S(1)}, u32[]{:S(2)}, u32[]{:S(2)}) collective-permute-start(bf16[528,128]{1,0:T(8,128)(2,1)S(1)} %collective-permute-done.6.refs_4_), channel_id=1, source_target_pairs={{0,1},{1,0},{2,3},{3,2},{4,5},{5,4},{6,7},{7,6},{8,9},{9,8},{10,11... | collective-permute-start | bytes 405512 | tf_op jit(solution)/shard_map/ppermute | solution.py:512
  20.0 1.5 %collective-permute-start.3 = (bf16[512,128]{1,0:T(8,128)(2,1)S(1)}, bf16[512,128]{1,0:T(8,128)(2,1)S(1)}, u32[]{:S(2)}, u32[]{:S(2)}) collective-permute-start(bf16[512,128]{1,0:T(8,128)(2,1)S(1)} %get-tuple-element.29.refs_0_), channel_id=1, source_target_pairs={{0,1},{1,0},{2,3},{3,2},{4,5},{5,4},{6,7},{7,6},{8,9},{9,8},{10,11... | collective-permute-start | bytes 393224 | tf_op jit(solution)/shard_map/ppermute | solution.py:512
  20.5 1.3 %collective-permute-start.5 = (bf16[512,128]{1,0:T(8,128)(2,1)S(1)}, bf16[512,128]{1,0:T(8,128)(2,1)S(1)}, u32[]{:S(2)}, u32[]{:S(2)}) collective-permute-start(bf16[512,128]{1,0:T(8,128)(2,1)S(1)} %collective-permute-done.4.refs_2_), channel_id=1, source_target_pairs={{0,1},{1,0},{2,3},{3,2},{4,5},{5,4},{6,7},{7,6},{8,9},{9,8},{10,11... | collective-permute-start | bytes 393224 | tf_op jit(solution)/shard_map/ppermute | solution.py:512
  29.1 15.3 %all-to-all-start = ((f32[32,4,128]{2,1,0:T(4,128)}), f32[32,4,128]{2,1,0:T(4,128)S(1)}, u32[]{:S(2)}, u32[]{:S(2)}) async-start(f32[32,4,128]{2,1,0:T(4,128)} %get-tuple-element.32), calls=%async_computation | async-start | bytes 131072 | tf_op jit(solution)/shard_map/all_to_all | solution.py:545
  34.5 9.7 %collective-permute-start.11 = (bf16[256,128]{1,0:T(8,128)(2,1)S(1)}, bf16[256,128]{1,0:T(8,128)(2,1)S(1)}, u32[]{:S(2)}, u32[]{:S(2)}) collective-permute-start(bf16[256,128]{1,0:T(8,128)(2,1)S(1)} %get-tuple-element.35), channel_id=1, source_target_pairs={{0,8},{4,12},{8,0},{12,4},{1,9},{5,13},{9,1},{13,5},{2,10},{6,14},... | collective-permute-start | bytes 196616 | tf_op jit(solution)/shard_map/ppermute | solution.py:543
  37.0 7.1 %collective-permute-start.12 = (bf16[256,128]{1,0:T(8,128)(2,1)S(1)}, bf16[256,128]{1,0:T(8,128)(2,1)S(1)}, u32[]{:S(2)}, u32[]{:S(2)}) collective-permute-start(bf16[256,128]{1,0:T(8,128)(2,1)S(1)} %get-tuple-element.36), channel_id=1, source_target_pairs={{0,12},{4,8},{8,4},{12,0},{1,13},{5,9},{9,5},{13,1},{2,14},{6,10},... | collective-permute-start | bytes 196616 | tf_op jit(solution)/shard_map/ppermute | solution.py:543
  38.5 5.9 %collective-permute-start.10 = (bf16[272,128]{1,0:T(8,128)(2,1)S(1)}, bf16[272,128]{1,0:T(8,128)(2,1)S(1)}, u32[]{:S(2)}, u32[]{:S(2)}) collective-permute-start(bf16[272,128]{1,0:T(8,128)(2,1)S(1)} %get-tuple-element.34), channel_id=1, source_target_pairs={{0,4},{4,0},{8,12},{12,8},{1,5},{5,1},{9,13},{13,9},{2,6},{6,2},{1... | collective-permute-start | bytes 208904 | tf_op jit(solution)/shard_map/ppermute | solution.py:543

commit v5 on v4

--- a/solution.py
+++ b/solution.py
@@ -390,11 +390,6 @@
     else:
         start = pl.multiple_of((grp_pos * groups + scalars[0]) * rows, 16)
         weights = projection[pl.ds(start, rows), :].astype(F32)
-    spread = jnp.zeros((rows, LANES), F32)
-    lane = lax.broadcasted_iota(jnp.int32, (rows, LANES), 1)
-    for item in range(batch):
-        column = jnp.sum(weights * latent_grad[item : item + 1, :], axis=1, keepdims=True)
-        spread = jnp.where(lane == item, column, spread)
     for turn in range(groups):
         lines = [arrived[(branch * share + item) * groups + turn, 1:2, :] for item in range(batch)]
         if batch % 8:
@@ -406,7 +401,8 @@
         grad[turn * rows : (turn + 1) * rows, :] = value[:rows]
     result = None
     for turn in range(share):
-        column = jnp.sum(jnp.where(lane == (grp_pos ^ turn), spread, 0.0), axis=1, keepdims=True)
+        line = jnp.sum(jnp.where(row == (grp_pos ^ turn), latent_grad, 0.0), axis=0, keepdims=True)
+        column = jnp.sum(weights * line, axis=1, keepdims=True)
         piece = pieces[turn][: 4 * rows, :].astype(F32)
         piece = jnp.concatenate([piece[at : at + rows] for at in range(0, 4 * rows, rows)], axis=1)
         extra = arrived[(branch * share + (grp_pos ^ turn)) * groups + scalars[0]]
@@ -480,7 +476,7 @@
             moved=10**6,
         )(table)
     wire = jax.ShapeDtypeStruct((chans * low_count, LANES), BF16)
-    longer = jax.ShapeDtypeStruct((chans * low_count + 16, LANES), BF16)
+    longer = wire
     with jax.named_scope("fourier"):
         own, pay = call(
             functools.partial(fourier_kernel, groups, full_len, length // 8, listed),

time: 47 us -> 46.3 us (0.985)
  transfers between devices with their start and end apart: 14 -> 14, of which waited for: 8 -> 9; matrix products, arithmetic and copies ran while one was open for 2% -> 2% of each run, Pallas kernels for 11% -> 12%
where the time goes in v5:
time: 46.3 us; the launch traced here: 46 us
  starting transfers between devices  16.5 us (36%)
  Pallas kernels  16.3 us (35%)
  waiting for transfers between devices  9.6 us (21%)
  local copies, waits for them, and re-layouts  2.73 us (6%)
  between operations  0.85 us (2%)
    pallas_call x1, Pallas kernels, body(): call(functools.partial(slope_kernel, groups, ready, 32, 4), [jax.ShapeDty...  7.19 us
    ppermute x3, waiting for transfers between devices, body(): block = lax.ppermute(block, ('pair', 'seq'), pairs)  5.86 us
    all_to_all x1, starting transfers between devices, body(): lax.all_to_all(payload, ('pair', 'grp', 'seq'), split_axis=0, concat_axis...  5.33 us
    pallas_call x1, Pallas kernels, body(): pl.pallas_call(functools.partial(encode_kernel, groups, chunk, columns),...  5.19 us
    ppermute x3, starting transfers between devices, body(): lax.ppermute(grads[turn], 'grp', [(i, i ^ turn) for i in range(share)])  4.08 us
    ppermute x3, starting transfers between devices, body(): block = lax.ppermute(block, ('pair', 'seq'), pairs)  3.55 us
    ppermute x3, starting transfers between devices, body(): lax.ppermute(pieces[turn], 'seq', [(i, i ^ turn) for i in range(groups)])  3.15 us
    ppermute x3, waiting for transfers between devices, body(): lax.ppermute(pieces[turn], 'seq', [(i, i ^ turn) for i in range(groups)])  2.04 us
  transfers between devices with their start and end apart: 14, of which 9 were waited for; matrix products, arithmetic and copies ran while one was open for 2% of the time, Pallas kernels for 12%

profile of v5, /device:TPU:0, one launch (start us, length us, event | category | flops | bytes accessed | tf_op | source)
XLA Modules:
  0.0 46.0 jit_solution(5847234187719483163)
XLA Ops:
  0.6 0.0 copy-start.1
  0.6 0.9 %copy-done.1 = f32[1,2048,32]{1,2,0:T(8,128)S(1)} copy-done((f32[1,2048,32]{1,2,0:T(8,128)S(1)}, f32[1,2048,32]{1,2,0:T(8,128)}, u32[]{:S(2)}) %copy-start.1) | copy-done | bytes 262168
  1.6 0.3 arrange.1
  1.9 0.5 %collective-permute-start = (f32[8,2048]{1,0:T(8,128)S(1)}, f32[8,2048]{1,0:T(8,128)S(1)}, u32[]{:S(2)}, u32[]{:S(2)}) collective-permute-start(f32[8,2048]{1,0:T(8,128)S(1)} %get-tuple-element.26), channel_id=1, source_target_pairs={{0,1},{1,0},{2,3},{3,2},{4,5},{5,4},{6,7},{7,6},{8,9},{9,8},{10,11... | collective-permute-start | bytes 196616 | tf_op jit(solution)/shard_map/ppermute | solution.py:463
  2.5 2.6 %collective-permute-start.1 = (f32[8,2048]{1,0:T(8,128)S(1)}, f32[8,2048]{1,0:T(8,128)S(1)}, u32[]{:S(2)}, u32[]{:S(2)}) collective-permute-start(f32[8,2048]{1,0:T(8,128)S(1)} %get-tuple-element.27), channel_id=1, source_target_pairs={{0,2},{1,3},{2,0},{3,1},{4,6},{5,7},{6,4},{7,5},{8,10},{9,11},{10,... | collective-permute-start | bytes 196616 | tf_op jit(solution)/shard_map/ppermute | solution.py:463
  5.0 0.1 collective-permute-start.2
  5.1 0.8 %concatenate.3.scalars = s32[15]{0:T(128)S(1)} concatenate(s32[1]{0:T(128)} %bitcast, s32[1]{0:T(128)} %bitcast.1, s32[1]{0:T(128)} %bitcast.2, s32[4]{0:T(128)} %bitcast.21, s32[4]{0:T(128)} %bitcast.22, s32[4]{0:T(128)} %param.10), dimensions={0} | concatenate | bytes 120 | tf_op jit(solution)/shard_map/concatenate | solution.py:443
  5.9 0.0 copy-start
  5.9 1.0 %copy-done = f32[448,256]{1,0:T(8,128)S(1)} copy-done((f32[448,256]{1,0:T(8,128)S(1)}, f32[448,256]{1,0:T(8,128)}, u32[]{:S(2)}) %copy-start) | copy-done | bytes 458776
  6.9 0.0 copy-start.2
  6.9 0.0 copy-start.3
  6.9 0.1 tables.1
  7.0 0.0 collective-permute-done.refs_1_
  7.0 0.7 %collective-permute-done.1.refs_2_ = f32[8,2048]{1,0:T(8,128)S(1)} collective-permute-done((f32[8,2048]{1,0:T(8,128)S(1)}, f32[8,2048]{1,0:T(8,128)S(1)}, u32[]{:S(2)}, u32[]{:S(2)}) %collective-permute-start.1) | collective-permute-done | bytes 65568 | tf_op jit(solution)/shard_map/ppermute | solution.py:463
  7.7 1.4 %collective-permute-done.2.refs_3_ = f32[8,2048]{1,0:T(8,128)S(1)} collective-permute-done((f32[8,2048]{1,0:T(8,128)S(1)}, f32[8,2048]{1,0:T(8,128)S(1)}, u32[]{:S(2)}, u32[]{:S(2)}) %collective-permute-start.2) | collective-permute-done | bytes 65568 | tf_op jit(solution)/shard_map/ppermute | solution.py:463
  9.1 1.4 %fourier.1 = (bf16[512,128]{1,0:T(8,128)(2,1)S(1)}, bf16[512,128]{1,0:T(8,128)(2,1)S(1)}) custom-call(s32[15]{0:T(128)S(1)} %concatenate.3.scalars, bf16[128,192]{1,0:T(8,128)(2,1)S(1)} %get-tuple-element.22.stage_one, f32[64,256]{1,0:T(8,128)S(1)} %get-tuple-element.23.turns, bf16[768,256]{1,0:T(8,128)(2,1)S(1)} %get-tuple-element.24.stage_two, ...), custom_call_target="tpu_custom_call" | custom-call | flops 1000000000 | bytes 2000000 | tf_op jit(solution)/shard_map/fourier/pallas_call | solution.py:481
  10.5 2.4 %collective-permute-start.8 = (bf16[512,128]{1,0:T(8,128)(2,1)S(1)}, bf16[512,128]{1,0:T(8,128)(2,1)S(1)}, u32[]{:S(2)}, u32[]{:S(2)}) collective-permute-start(bf16[512,128]{1,0:T(8,128)(2,1)S(1)} %get-tuple-element.30), channel_id=1, source_target_pairs={{0,18},{1,19},{2,16},{3,17},{16,2},{17,3},{18,0},{19,1},{4,22},{5,... | collective-permute-start | bytes 393224 | tf_op jit(solution)/shard_map/ppermute | solution.py:504
  12.9 0.5 %collective-permute-start.6 = (bf16[512,128]{1,0:T(8,128)(2,1)S(1)}, bf16[512,128]{1,0:T(8,128)(2,1)S(1)}, u32[]{:S(2)}, u32[]{:S(2)}) collective-permute-start(bf16[512,128]{1,0:T(8,128)(2,1)S(1)} %get-tuple-element.30), channel_id=1, source_target_pairs={{0,16},{1,17},{2,18},{3,19},{16,0},{17,1},{18,2},{19,3},{4,20},{5,... | collective-permute-start | bytes 393224 | tf_op jit(solution)/shard_map/ppermute | solution.py:504
  13.4 0.7 %collective-permute-start.4 = (bf16[512,128]{1,0:T(8,128)(2,1)S(1)}, bf16[512,128]{1,0:T(8,128)(2,1)S(1)}, u32[]{:S(2)}, u32[]{:S(2)}) collective-permute-start(bf16[512,128]{1,0:T(8,128)(2,1)S(1)} %get-tuple-element.29.refs_0_), channel_id=1, source_target_pairs={{0,2},{1,3},{2,0},{3,1},{16,18},{17,19},{18,16},{19,17},{4,6},{5,7... | collective-permute-start | bytes 393224 | tf_op jit(solution)/shard_map/ppermute | solution.py:504
  14.1 0.0 collective-permute-start.3
  14.1 3.3 %collective-permute-done.8.refs_6_ = bf16[512,128]{1,0:T(8,128)(2,1)S(1)} collective-permute-done((bf16[512,128]{1,0:T(8,128)(2,1)S(1)}, bf16[512,128]{1,0:T(8,128)(2,1)S(1)}, u32[]{:S(2)}, u32[]{:S(2)}) %collective-permute-start.8) | collective-permute-done | bytes 131104 | tf_op jit(solution)/shard_map/ppermute | solution.py:504
  17.4 0.0 collective-permute-start.9
  17.4 2.5 %collective-permute-done.6.refs_4_ = bf16[512,128]{1,0:T(8,128)(2,1)S(1)} collective-permute-done((bf16[512,128]{1,0:T(8,128)(2,1)S(1)}, bf16[512,128]{1,0:T(8,128)(2,1)S(1)}, u32[]{:S(2)}, u32[]{:S(2)}) %collective-permute-start.6) | collective-permute-done | bytes 131104 | tf_op jit(solution)/shard_map/ppermute | solution.py:504
  19.9 0.0 collective-permute-start.7
  19.9 0.1 collective-permute-done.4.refs_2_
  20.0 0.4 collective-permute-start.5
  20.4 0.0 collective-permute-done.3.refs_1_
  20.4 0.0 collective-permute-done.9.refs_7_
  20.4 0.8 %collective-permute-done.7.refs_5_ = bf16[512,128]{1,0:T(8,128)(2,1)S(1)} collective-permute-done((bf16[512,128]{1,0:T(8,128)(2,1)S(1)}, bf16[512,128]{1,0:T(8,128)(2,1)S(1)}, u32[]{:S(2)}, u32[]{:S(2)}) %collective-permute-start.7) | collective-permute-done | bytes 131104 | tf_op jit(solution)/shard_map/ppermute | solution.py:508
  21.2 0.2 collective-permute-done.5.refs_3_
  21.4 0.0 copy-done.2
  21.4 0.0 copy-done.3
  21.4 7.2 %slope.1 = (bf16[272,128]{1,0:T(8,128)(2,1)S(1)}, bf16[272,128]{1,0:T(8,128)(2,1)S(1)}, bf16[256,128]{1,0:T(8,128)(2,1)S(1)}, bf16[256,128]{1,0:T(8,128)(2,1)S(1...) custom-call(s32[15]{0:T(128)S(1)} %concatenate.3.scalars, bf16[1024,512]{1,0:T(8,128)(2,1)S(1)} %bitcast.19, ...), custom_call_target="tpu_custom_call" | custom-call | flops 4294967296 | bytes 4000000 | tf_op jit(solution)/shard_map/slope/pallas_call | solution.py:518
  28.6 5.3 %all-to-all-start = ((f32[32,4,128]{2,1,0:T(4,128)}), f32[32,4,128]{2,1,0:T(4,128)S(1)}, u32[]{:S(2)}, u32[]{:S(2)}) async-start(f32[32,4,128]{2,1,0:T(4,128)} %get-tuple-element.32), calls=%async_computation | async-start | bytes 131072 | tf_op jit(solution)/shard_map/all_to_all | solution.py:541
  33.9 2.6 %collective-permute-start.11 = (bf16[256,128]{1,0:T(8,128)(2,1)S(1)}, bf16[256,128]{1,0:T(8,128)(2,1)S(1)}, u32[]{:S(2)}, u32[]{:S(2)}) collective-permute-start(bf16[256,128]{1,0:T(8,128)(2,1)S(1)} %get-tuple-element.35), channel_id=1, source_target_pairs={{0,8},{4,12},{8,0},{12,4},{1,9},{5,13},{9,1},{13,5},{2,10},{6,14},... | collective-permute-start | bytes 196616 | tf_op jit(solution)/shard_map/ppermute | solution.py:539
  36.5 1.5 %collective-permute-start.12 = (bf16[256,128]{1,0:T(8,128)(2,1)S(1)}, bf16[256,128]{1,0:T(8,128)(2,1)S(1)}, u32[]{:S(2)}, u32[]{:S(2)}) collective-permute-start(bf16[256,128]{1,0:T(8,128)(2,1)S(1)} %get-tuple-element.36), channel_id=1, source_target_pairs={{0,12},{4,8},{8,4},{12,0},{1,13},{5,9},{9,5},{13,1},{2,14},{6,10},... | collective-permute-start | bytes 196616 | tf_op jit(solution)/shard_map/ppermute | solution.py:539
  38.0 0.1 collective-permute-start.10
  38.0 5.2 %encode.1 = bf16[1024,1024]{1,0:T(8,128)(2,1)} custom-call(s32[15]{0:T(128)S(1)} %concatenate.3.scalars, bf16[36,128,128]{2,1,0:T(8,128)(2,1)S(1)} %get-tuple-element.31.flat, bf16[1024,512]{1,0:T(8,128)(2,1)S(1)} %bitcast.20), custom_call_target="tpu_custom_call" | custom-call | flops 2147483648 | bytes 4000000 | tf_op jit(solution)/shard_map/encode/pallas_call | solution.py:544
  43.2 0.4 collective-permute-done.11.refs_2_
  43.6 0.0 collective-permute-done.12.refs_3_
  43.6 0.3 collective-permute-done.10.refs_1_
  43.9 0.0 all-to-all-done.arrived
  43.9 2.0 %loss.1 = (f32[1,1]{1,0:T(1,128)}, f32[64,512]{1,0:T(8,128)}, f32[256,128]{1,0:T(8,128)}) custom-call(s32[15]{0:T(128)S(1)} %concatenate.3.scalars, f32[32,4,128]{2,1,0:T(4,128)S(1)} %all-to-all-done.arrived, bf16[1024,128]{1,0:T(8,128)(2,1)S(1)} %bitcast.18, bf16[272,128]{1,0:T(8,128)(2,1)S(1)} %get-tuple-element.33.refs_0_, ...), custom_call_target="tpu_custom_call" | custom-call | flops 10000000 | bytes 1000000 | tf_op jit(solution)/shard_map/loss/pallas_call | solution.py:562
Async XLA Ops:
  0.6 1.0 %copy-start.1 = (f32[1,2048,32]{1,2,0:T(8,128)S(1)}, f32[1,2048,32]{1,2,0:T(8,128)}, u32[]{:S(2)}) copy-start(f32[1,2048,32]{1,2,0:T(8,128)} %param.7) | copy-start | bytes 786436
  1.9 5.1 %collective-permute-start = (f32[8,2048]{1,0:T(8,128)S(1)}, f32[8,2048]{1,0:T(8,128)S(1)}, u32[]{:S(2)}, u32[]{:S(2)}) collective-permute-start(f32[8,2048]{1,0:T(8,128)S(1)} %get-tuple-element.26), channel_id=1, source_target_pairs={{0,1},{1,0},{2,3},{3,2},{4,5},{5,4},{6,7},{7,6},{8,9},{9,8},{10,11... | collective-permute-start | bytes 196616 | tf_op jit(solution)/shard_map/ppermute | solution.py:463
  2.5 5.3 %collective-permute-start.1 = (f32[8,2048]{1,0:T(8,128)S(1)}, f32[8,2048]{1,0:T(8,128)S(1)}, u32[]{:S(2)}, u32[]{:S(2)}) collective-permute-start(f32[8,2048]{1,0:T(8,128)S(1)} %get-tuple-element.27), channel_id=1, source_target_pairs={{0,2},{1,3},{2,0},{3,1},{4,6},{5,7},{6,4},{7,5},{8,10},{9,11},{10,... | collective-permute-start | bytes 196616 | tf_op jit(solution)/shard_map/ppermute | solution.py:463
  5.0 4.0 %collective-permute-start.2 = (f32[8,2048]{1,0:T(8,128)S(1)}, f32[8,2048]{1,0:T(8,128)S(1)}, u32[]{:S(2)}, u32[]{:S(2)}) collective-permute-start(f32[8,2048]{1,0:T(8,128)S(1)} %get-tuple-element.28), channel_id=1, source_target_pairs={{0,3},{1,2},{2,1},{3,0},{4,7},{5,6},{6,5},{7,4},{8,11},{9,10},{10,... | collective-permute-start | bytes 196616 | tf_op jit(solution)/shard_map/ppermute | solution.py:463
  5.9 1.0 %copy-start = (f32[448,256]{1,0:T(8,128)S(1)}, f32[448,256]{1,0:T(8,128)}, u32[]{:S(2)}) copy-start(f32[448,256]{1,0:T(8,128)} %constant.15.clone.table) | copy-start | bytes 1376260
  6.9 14.5 %copy-start.2 = (bf16[1,1024,128]{2,1,0:T(8,128)(2,1)S(1)}, bf16[1,1024,128]{2,1,0:T(8,128)(2,1)}, u32[]{:S(2)}) copy-start(bf16[1,1024,128]{2,1,0:T(8,128)(2,1)} %param.12) | copy-start | bytes 786436
  6.9 14.5 %copy-start.3 = (bf16[1,1024,512]{2,1,0:T(8,128)(2,1)S(1)}, bf16[1,1024,512]{2,1,0:T(8,128)(2,1)}, u32[]{:S(2)}) copy-start(bf16[1,1024,512]{2,1,0:T(8,128)(2,1)} %param.11) | copy-start | bytes 3145732
  10.5 6.9 %collective-permute-start.8 = (bf16[512,128]{1,0:T(8,128)(2,1)S(1)}, bf16[512,128]{1,0:T(8,128)(2,1)S(1)}, u32[]{:S(2)}, u32[]{:S(2)}) collective-permute-start(bf16[512,128]{1,0:T(8,128)(2,1)S(1)} %get-tuple-element.30), channel_id=1, source_target_pairs={{0,18},{1,19},{2,16},{3,17},{16,2},{17,3},{18,0},{19,1},{4,22},{5,... | collective-permute-start | bytes 393224 | tf_op jit(solution)/shard_map/ppermute | solution.py:504
  12.9 7.0 %collective-permute-start.6 = (bf16[512,128]{1,0:T(8,128)(2,1)S(1)}, bf16[512,128]{1,0:T(8,128)(2,1)S(1)}, u32[]{:S(2)}, u32[]{:S(2)}) collective-permute-start(bf16[512,128]{1,0:T(8,128)(2,1)S(1)} %get-tuple-element.30), channel_id=1, source_target_pairs={{0,16},{1,17},{2,18},{3,19},{16,0},{17,1},{18,2},{19,3},{4,20},{5,... | collective-permute-start | bytes 393224 | tf_op jit(solution)/shard_map/ppermute | solution.py:504
  13.4 6.6 %collective-permute-start.4 = (bf16[512,128]{1,0:T(8,128)(2,1)S(1)}, bf16[512,128]{1,0:T(8,128)(2,1)S(1)}, u32[]{:S(2)}, u32[]{:S(2)}) collective-permute-start(bf16[512,128]{1,0:T(8,128)(2,1)S(1)} %get-tuple-element.29.refs_0_), channel_id=1, source_target_pairs={{0,2},{1,3},{2,0},{3,1},{16,18},{17,19},{18,16},{19,17},{4,6},{5,7... | collective-permute-start | bytes 393224 | tf_op jit(solution)/shard_map/ppermute | solution.py:504
  14.1 6.3 %collective-permute-start.3 = (bf16[512,128]{1,0:T(8,128)(2,1)S(1)}, bf16[512,128]{1,0:T(8,128)(2,1)S(1)}, u32[]{:S(2)}, u32[]{:S(2)}) collective-permute-start(bf16[512,128]{1,0:T(8,128)(2,1)S(1)} %get-tuple-element.29.refs_0_), channel_id=1, source_target_pairs={{0,1},{1,0},{2,3},{3,2},{4,5},{5,4},{6,7},{7,6},{8,9},{9,8},{10,11... | collective-permute-start | bytes 393224 | tf_op jit(solution)/shard_map/ppermute | solution.py:508
  17.4 3.0 %collective-permute-start.9 = (bf16[512,128]{1,0:T(8,128)(2,1)S(1)}, bf16[512,128]{1,0:T(8,128)(2,1)S(1)}, u32[]{:S(2)}, u32[]{:S(2)}) collective-permute-start(bf16[512,128]{1,0:T(8,128)(2,1)S(1)} %collective-permute-done.8.refs_6_), channel_id=1, source_target_pairs={{0,1},{1,0},{2,3},{3,2},{4,5},{5,4},{6,7},{7,6},{8,9},{9,8},{10,11... | collective-permute-start | bytes 393224 | tf_op jit(solution)/shard_map/ppermute | solution.py:508
  19.9 1.3 %collective-permute-start.7 = (bf16[512,128]{1,0:T(8,128)(2,1)S(1)}, bf16[512,128]{1,0:T(8,128)(2,1)S(1)}, u32[]{:S(2)}, u32[]{:S(2)}) collective-permute-start(bf16[512,128]{1,0:T(8,128)(2,1)S(1)} %collective-permute-done.6.refs_4_), channel_id=1, source_target_pairs={{0,1},{1,0},{2,3},{3,2},{4,5},{5,4},{6,7},{7,6},{8,9},{9,8},{10,11... | collective-permute-start | bytes 393224 | tf_op jit(solution)/shard_map/ppermute | solution.py:508
  20.0 1.4 %collective-permute-start.5 = (bf16[512,128]{1,0:T(8,128)(2,1)S(1)}, bf16[512,128]{1,0:T(8,128)(2,1)S(1)}, u32[]{:S(2)}, u32[]{:S(2)}) collective-permute-start(bf16[512,128]{1,0:T(8,128)(2,1)S(1)} %collective-permute-done.4.refs_2_), channel_id=1, source_target_pairs={{0,1},{1,0},{2,3},{3,2},{4,5},{5,4},{6,7},{7,6},{8,9},{9,8},{10,11... | collective-permute-start | bytes 393224 | tf_op jit(solution)/shard_map/ppermute | solution.py:508
  28.6 15.3 %all-to-all-start = ((f32[32,4,128]{2,1,0:T(4,128)}), f32[32,4,128]{2,1,0:T(4,128)S(1)}, u32[]{:S(2)}, u32[]{:S(2)}) async-start(f32[32,4,128]{2,1,0:T(4,128)} %get-tuple-element.32), calls=%async_computation | async-start | bytes 131072 | tf_op jit(solution)/shard_map/all_to_all | solution.py:541
  33.9 9.7 %collective-permute-start.11 = (bf16[256,128]{1,0:T(8,128)(2,1)S(1)}, bf16[256,128]{1,0:T(8,128)(2,1)S(1)}, u32[]{:S(2)}, u32[]{:S(2)}) collective-permute-start(bf16[256,128]{1,0:T(8,128)(2,1)S(1)} %get-tuple-element.35), channel_id=1, source_target_pairs={{0,8},{4,12},{8,0},{12,4},{1,9},{5,13},{9,1},{13,5},{2,10},{6,14},... | collective-permute-start | bytes 196616 | tf_op jit(solution)/shard_map/ppermute | solution.py:539
  36.5 7.1 %collective-permute-start.12 = (bf16[256,128]{1,0:T(8,128)(2,1)S(1)}, bf16[256,128]{1,0:T(8,128)(2,1)S(1)}, u32[]{:S(2)}, u32[]{:S(2)}) collective-permute-start(bf16[256,128]{1,0:T(8,128)(2,1)S(1)} %get-tuple-element.36), channel_id=1, source_target_pairs={{0,12},{4,8},{8,4},{12,0},{1,13},{5,9},{9,5},{13,1},{2,14},{6,10},... | collective-permute-start | bytes 196616 | tf_op jit(solution)/shard_map/ppermute | solution.py:539
  38.0 5.9 %collective-permute-start.10 = (bf16[272,128]{1,0:T(8,128)(2,1)S(1)}, bf16[272,128]{1,0:T(8,128)(2,1)S(1)}, u32[]{:S(2)}, u32[]{:S(2)}) collective-permute-start(bf16[272,128]{1,0:T(8,128)(2,1)S(1)} %get-tuple-element.34), channel_id=1, source_target_pairs={{0,4},{4,0},{8,12},{12,8},{1,5},{5,1},{9,13},{13,9},{2,6},{6,2},{1... | collective-permute-start | bytes 208904 | tf_op jit(solution)/shard_map/ppermute | solution.py:539
